TPU v7x, 128 devices: a whole 4x4x4 slice. The times are simulated.
128 devices in a mesh: row: 8 (over x, y_hi), col: 16 (over z, y_lo, core).
Axes of the slice: x: 4, y: 4 (y_hi: 2, y_lo: 2; y = y_hi * 2 + y_lo), z: 4, core: 2. Of those that a mesh axis runs over, the one named last changes fastest.
Arguments:
- click_counts: int32 [16384, 16384], P('row', 'col'), may hold values from 1 to 2047, as said below
- tile_pattern: int32 [64, 64], P('row', 'col'), may hold values from 0 to 1, as said below
- row_factors: bfloat16 [16384, 512], P(('row', 'col')), may hold values from 0.25 to 6, as said below
- column_factors: bfloat16 [16384, 512], P(('col', 'row')), may hold values from 0.25 to 6, as said below
Outputs:
- updated_rows: bfloat16 [16384, 512], P(('row', 'col'))
- updated_columns: bfloat16 [16384, 512], P(('col', 'row'))
Inputs may be any that keep to these rules, and one draw needn't show every extreme that they name: `click_counts`: whole numbers of clicks. `tile_pattern`: 1 marks a stored tile of 256 x 256 entries; the share of stored tiles differs strongly between blocks of 2048 x 1024 entries. `row_factors`: every entry is positive. `column_factors`: every entry is positive.
All inputs are finite; a program needn't handle non-finite values.
Results may differ from a plain program's by a relative error of at most 0.0026.
Values may be sent and summed in bfloat16 or wider, within the bound.
No kernel may reach another device: no remote copies, remote signals or barrier semaphores. Data moves between devices by JAX's collectives and lax.ppermute only.
A program may use at most 128 MiB of HBM per device.

v0:
```python
import jax
import jax.numpy as jnp
from jax import lax
from jax.sharding import PartitionSpec as P


def tile_plan(pattern):
    flat_pattern = pattern.reshape(-1)
    positions = jnp.arange(flat_pattern.shape[0], dtype=jnp.int32)
    keyed = jnp.where(flat_pattern > 0, positions, positions + flat_pattern.shape[0])
    tile_order = jnp.argsort(keyed, stable=True)
    live_count = jnp.sum(flat_pattern)
    return (tile_order, live_count)


def add_rows(totals, ratios, left_tile, right_tile, row_start, col_start):
    current = lax.dynamic_slice_in_dim(totals, row_start, ratios.shape[0], 0)
    term = jnp.dot(ratios, right_tile, preferred_element_type=jnp.float32)
    return lax.dynamic_update_slice_in_dim(totals, current + term, row_start, 0)


def add_columns(totals, ratios, left_tile, right_tile, row_start, col_start):
    current = lax.dynamic_slice_in_dim(totals, col_start, ratios.shape[1], 0)
    term = lax.dot_general(
        ratios, left_tile, (((0,), (0,)), ((), ())), preferred_element_type=jnp.float32
    )
    return lax.dynamic_update_slice_in_dim(totals, current + term, col_start, 0)


def sweep(
    counts,
    left_panel,
    right_panel,
    tile_order,
    use_count,
    tiles_across,
    tile_size,
    accumulate,
    initial,
):
    last_slot = tile_order.shape[0] - 1
    group_count = (use_count + 3) // 4

    def visit(group_index, totals):
        for member in range(4):
            slot = group_index * 4 + member
            chosen = tile_order[jnp.minimum(slot, last_slot)]
            is_live = (slot < use_count).astype(jnp.float32)
            row_start = chosen // tiles_across * tile_size
            col_start = chosen % tiles_across * tile_size
            left_tile = lax.dynamic_slice_in_dim(left_panel, row_start, tile_size, 0)
            right_tile = lax.dynamic_slice_in_dim(right_panel, col_start, tile_size, 0)
            count_tile = lax.dynamic_slice(
                counts, (row_start, col_start), (tile_size, tile_size)
            ).astype(jnp.float32)
            predicted = lax.dot_general(
                left_tile, right_tile, (((1,), (1,)), ((), ())), preferred_element_type=jnp.float32
            )
            ratios = (count_tile / predicted * is_live).astype(jnp.bfloat16)
            totals = accumulate(totals, ratios, left_tile, right_tile, row_start, col_start)
        return totals

    return lax.fori_loop(0, group_count, visit, initial)


def local(click_counts, tile_pattern, row_factors, column_factors):
    row_panel = lax.all_gather(row_factors, "col", axis=0, tiled=True)
    column_panel = lax.all_gather(column_factors, "row", axis=0, tiled=True)
    column_total = lax.psum(jnp.sum(column_factors.astype(jnp.float32), axis=0), ("row", "col"))
    width = row_factors.shape[1]
    tile_size = click_counts.shape[0] // tile_pattern.shape[0]
    tiles_across = tile_pattern.shape[1]
    tile_order, live_count = tile_plan(tile_pattern)
    row_sums = sweep(
        click_counts,
        row_panel,
        column_panel,
        tile_order,
        live_count,
        tiles_across,
        tile_size,
        add_rows,
        jnp.zeros((row_panel.shape[0], width), jnp.float32),
    )
    row_share = lax.psum_scatter(row_sums, "col", scatter_dimension=0, tiled=True)
    updated_rows = (row_factors.astype(jnp.float32) * row_share / column_total[None, :]).astype(
        jnp.bfloat16
    )
    new_panel = lax.all_gather(updated_rows, "col", axis=0, tiled=True)
    row_total = lax.psum(jnp.sum(updated_rows.astype(jnp.float32), axis=0), ("row", "col"))
    column_sums = sweep(
        click_counts,
        new_panel,
        column_panel,
        tile_order,
        live_count,
        tiles_across,
        tile_size,
        add_columns,
        jnp.zeros((column_panel.shape[0], width), jnp.float32),
    )
    column_share = lax.psum_scatter(column_sums, "row", scatter_dimension=0, tiled=True)
    updated_columns = (
        column_factors.astype(jnp.float32) * column_share / row_total[None, :]
    ).astype(jnp.bfloat16)
    return (updated_rows, updated_columns)


def solution(mesh):
    in_specs = (P("row", "col"), P("row", "col"), P(("row", "col"), None), P(("col", "row"), None))
    out_specs = (P(("row", "col"), None), P(("col", "row"), None))
    return jax.shard_map(local, mesh=mesh, in_specs=in_specs, out_specs=out_specs, check_vma=False)
```

profile of v0, /device:TPU:0, one launch (start us, length us, event | category | flops | bytes accessed | tf_op | source)
XLA Modules:
  0.0 636.7 jit_solution(17864636168695798854)
XLA Ops:
  7.2 0.0 all-gather.6.cloned.1.call-start
  7.2 0.7 all-gather.6.cloned.1.call-update
  7.9 0.0 all-gather.4.cloned.1.call-start
  7.9 0.7 all-gather.4.cloned.1.call-update
  8.6 0.0 reduce-scatter.3.cloned.1.call-start
  8.7 1.4 reduce_sum.27
  10.8 0.7 broadcast_compare_fusion
  11.5 0.1 copy.7
  11.6 0.1 gt.11
  11.7 1.6 sort.17
  13.3 46.9 %all-gather.6.cloned.1.call-done = bf16[1024,512]{1,0:T(8,128)(2,1)} async-done(((bf16[128,512]{1,0:T(8,128)(2,1)}), bf16[1024,512]{1,0:T(8,128)(2,1)}) %all-gather.6.cloned.1.call-update) | async-done | bytes 1048592 | tf_op jit(solution)/shard_map/all_gather | solution.py:68
  60.2 35.0 %all-gather.4.cloned.1.call-done = bf16[2048,512]{1,0:T(8,128)(2,1)} async-done(((bf16[128,512]{1,0:T(8,128)(2,1)}), bf16[2048,512]{1,0:T(8,128)(2,1)}) %all-gather.4.cloned.1.call-update) | async-done | bytes 2097168 | tf_op jit(solution)/shard_map/all_gather | solution.py:67
  95.2 2.5 broadcast_in_dim.8
  97.6 0.4 copy-done.4
  98.0 47.2 %while.26 = (s32[]{:T(128)}, f32[2048,512]{1,0:T(8,128)}, s32[]{:T(128)}, s32[32]{0:T(128)S(1)}, s32[2048,1024]{1,0:T(8,128)}, /*index=5*/bf16[2048,512]{1,0:T(8...) while((s32[]{:T(128)}, f32[2048,512]{1,0:T(8,128)}, ...), condition=%wide.region_3.4_spmd, body=%wide.region_2.3_spmd.sunk | while | flops 538443840 | bytes 8404569 | solution.py:63
  98.0 0.7 fusion.146
  102.2 2.4 fusion.147
  107.8 2.4 fusion.148
  113.4 2.5 fusion.149
  119.2 2.4 fusion.150
  121.6 0.7 fusion.146
  125.8 2.5 fusion.147
  131.4 2.4 fusion.148
  137.0 2.4 fusion.149
  142.7 2.5 fusion.150
  145.2 0.0 all-gather.8.cloned.1.call-start
  145.3 0.8 copy-done.1
  146.2 206.3 %psum.14 = f32[512]{0:T(512)S(1)} all-reduce(f32[512]{0:T(512)S(1)} %convert_reduce_fusion), channel_id=1, replica_groups=mesh['row'=8,'col'=16] {'row','col'}, use_global_device_ids=true, to_apply=%region_6.7 | all-reduce | flops 512 | bytes 4096 | tf_op jit(solution)/shard_map/psum | solution.py:69
  352.5 4.4 reduce-scatter.3.cloned.1.call-done
  356.9 1.7 convert_reduce_fusion.1
  358.6 0.0 reduce-scatter.5.cloned.1.call-start
  358.6 32.8 %all-gather.8.cloned.1.call-done = bf16[2048,512]{1,0:T(8,128)(2,1)} async-done(((bf16[128,512]{1,0:T(8,128)(2,1)}), bf16[2048,512]{1,0:T(8,128)(2,1)}) %all-gather.8.cloned.1.call-update) | async-done | bytes 2097168 | tf_op jit(solution)/shard_map/all_gather | solution.py:89
  391.4 0.2 broadcast_in_dim.9
  391.7 40.1 %while.27 = (s32[]{:T(128)}, f32[1024,512]{1,0:T(8,128)S(1)}, s32[]{:T(128)}, s32[32]{0:T(128)S(1)}, s32[2048,1024]{1,0:T(8,128)}, /*index=5*/bf16[2048,512]{1,0...) while((s32[]{:T(128)}, f32[1024,512]{1,0:T(8,128)S(1)}, ...), condition=%wide.region_8.9_spmd, body=%wide.region_7.8_spmd.sunk | while | flops 538443840 | bytes 8404569 | solution.py:63
  391.7 0.6 fusion.163
  395.3 1.7 fusion.164
  400.2 1.7 fusion.165
  405.1 1.7 fusion.166
  410.0 1.7 fusion.167
  411.8 0.6 fusion.163
  415.4 1.7 fusion.164
  420.3 1.7 fusion.165
  425.2 1.7 fusion.166
  430.1 1.7 fusion.167
  431.9 1.3 copy-done
  433.2 186.7 %psum.15 = f32[512]{0:T(512)S(1)} all-reduce(f32[512]{0:T(512)S(1)} %get-tuple-element.314), channel_id=1, replica_groups=mesh['row'=8,'col'=16] {'row','col'}, use_global_device_ids=true, to_apply=%region_11.12 | all-reduce | flops 512 | bytes 4096 | tf_op jit(solution)/shard_map/psum | solution.py:90
  619.9 8.6 %reduce-scatter.5.cloned.1.call-done = f32[128,512]{1,0:T(8,128)} async-done(((f32[1024,512]{1,0:T(8,128)}), f32[128,512]{1,0:T(8,128)}) %reduce-scatter.5.cloned.1.call-update) | async-done | bytes 262160 | tf_op jit(solution)/shard_map/reduce_scatter | solution.py:102
  628.6 1.6 fusion.97
  (13 shorter events, 0.1 us)
Async XLA Ops:
  7.2 53.0 %all-gather.6.cloned.1.call-start = ((), (), s32[]{:S(2)}) async-start(), calls=%async_computation.3 | async-start | bytes 1179648 | tf_op jit(solution)/shard_map/all_gather | solution.py:68
  7.9 87.3 %all-gather.4.cloned.1.call-start = ((), (), s32[]{:S(2)}) async-start(), calls=%async_computation.2 | async-start | bytes 2228224 | tf_op jit(solution)/shard_map/all_gather | solution.py:67
  8.6 348.3 %reduce-scatter.3.cloned.1.call-start = ((), (), s32[]{:S(2)}) async-start(), calls=%async_computation.4 | async-start | bytes 4456448 | tf_op jit(solution)/shard_map/reduce_scatter | solution.py:85
  95.2 2.5 copy-start.3
  95.2 2.8 copy-start.4
  145.2 0.9 copy-start.1
  145.2 211.7 %copy-start.2 = (bf16[128,512]{1,0:T(8,128)(2,1)S(1)}, bf16[128,512]{1,0:T(8,128)(2,1)}, u32[]{:S(2)}) copy-start(bf16[128,512]{1,0:T(8,128)(2,1)} %param.10) | copy-start | bytes 393220
  145.2 246.2 %all-gather.8.cloned.1.call-start = ((), (), s32[]{:S(2)}) async-start(), calls=%async_computation.5 | async-start | bytes 2228224 | tf_op jit(solution)/shard_map/all_gather | solution.py:89
  358.6 270.0 %reduce-scatter.5.cloned.1.call-start = ((), (), s32[]{:S(2)}) async-start(), calls=%async_computation.6 | async-start | bytes 2359296 | tf_op jit(solution)/shard_map/reduce_scatter | solution.py:102
  431.9 1.4 copy-start
Sparse Core Ops, SparseCore 0:
  10.3 49.7 all-gather.5
  61.9 33.2 all-gather.3
  145.4 211.4 reduce-scatter.2
  359.0 32.3 all-gather.7
  433.3 195.1 reduce-scatter.4
where the time goes:
time: 641 us; the launch traced here: 637 us
  blocking collectives  393 us (61%)
  waiting for transfers between devices  129 us (20%)
  loops' own time  51.3 us (8%)
  matrix products  33.4 us (5%)
  between operations  14.5 us (2%)
  local copies, waits for them, and re-layouts  8.03 us (1%)
  other arithmetic  7.04 us (1%)
    psum x1, blocking collectives, local(): lax.psum(jnp.sum(column_factors.astype(jnp.float32), axis=0), ('row', 'co...  206 us
    psum x1, blocking collectives, local(): lax.psum(jnp.sum(updated_rows.astype(jnp.float32), axis=0), ('row', 'col'))  187 us
    another operation x2, loops' own time, sweep(): return lax.fori_loop(0, group_count, visit, initial)  51.3 us
    all_gather x1, waiting for transfers between devices, local(): column_panel = lax.all_gather(column_factors, 'row', axis=0, tiled=True)  46.9 us
    all_gather x1, waiting for transfers between devices, local(): row_panel = lax.all_gather(row_factors, 'col', axis=0, tiled=True)  35 us
    all_gather x1, waiting for transfers between devices, local(): new_panel = lax.all_gather(updated_rows, 'col', axis=0, tiled=True)  32.8 us
    dot_general x8, matrix products, add_rows(): term = jnp.dot(ratios, right_tile, preferred_element_type=jnp.float32)  19.6 us
    dot_general x8, matrix products, add_columns(): lax.dot_general(ratios, left_tile, (((0,), (0,)), ((), ())), preferred_el...  13.8 us
  transfers between devices with their start and end apart: 5, of which 5 were waited for; matrix products, arithmetic and copies ran while one was open for 1% of the time, Pallas kernels for 0%

commit v1 on v0

v1 whole, which is shorter than its diff:
```python
import functools

import jax
import jax.numpy as jnp
from jax import lax
from jax.experimental import pallas as pl
from jax.experimental.pallas import tpu as pltpu
from jax.sharding import PartitionSpec as P

WIRE = jnp.float16
ROW_SCALE = 2.0**-6
COLUMN_SCALE = 2.0**-11
BLOCK = 128
TILE = 256
F32 = jnp.float32


def along_z(step):
    return [(j, (j // 4 + step) % 4 * 4 + j % 4) for j in range(16)]


def along_x(step):
    return [(i, (i // 2 + step) % 4 * 2 + i % 2) for i in range(8)]


SWAP_CORE = [(j, j ^ 1) for j in range(16)]
SWAP_PAIR = [(j, j ^ 2) for j in range(16)]
SWAP_FAR = [(i, i ^ 1) for i in range(8)]


def contract_last(a, b):
    return lax.dot_general(a, b, (((1,), (1,)), ((), ())), preferred_element_type=F32)


def tile_ratios(counts, predicted, live_ref, row_tile, tiles_across):
    parts = []
    for j in range(tiles_across):
        window = slice(j * TILE, (j + 1) * TILE)
        live = live_ref[row_tile * tiles_across + j] > 0
        value = counts[:, window].astype(F32) / predicted[:, window]
        parts.append(jnp.where(live, value, 0.0).astype(jnp.bfloat16))
    return parts


def place_panel(place_ref, panel_ref, placed):
    for k in range(placed.shape[0]):
        placed[place_ref[k]] = panel_ref[k]


def rows_kernel(tiles_across, rows_ref, live_ref, place_ref, c0, c1, a, b, panel, keep, send, placed):
    step = pl.program_id(0)

    @pl.when(step == 0)
    def _():
        place_panel(place_ref, panel, placed)

    columns = placed[...].reshape(-1, placed.shape[-1])
    left = jnp.concatenate([a[0], b[0]], axis=0)
    counts = jnp.concatenate([c0[...], c1[...]], axis=0)
    predicted = contract_last(left, columns)
    ratios = tile_ratios(counts, predicted, live_ref, rows_ref[2 * step] // 2, tiles_across)
    total = jnp.dot(jnp.concatenate(ratios, axis=1), columns, preferred_element_type=F32)
    keep[0] = total[:BLOCK]
    send[0] = total[BLOCK:]


def columns_kernel(
    tiles_across, rows_ref, live_ref, place_ref, c0, c1, a, b, panel, keep, send, placed, total
):
    step = pl.program_id(0)

    @pl.when(step == 0)
    def _():
        place_panel(place_ref, panel, placed)
        total[...] = jnp.zeros_like(total)

    columns = placed[...].reshape(-1, placed.shape[-1])
    left = jnp.concatenate([a[0], b[0]], axis=0)
    counts = jnp.concatenate([c0[...], c1[...]], axis=0)
    predicted = contract_last(left, columns)
    ratios = tile_ratios(counts, predicted, live_ref, rows_ref[2 * step] // 2, tiles_across)
    for j in range(tiles_across):
        term = lax.dot_general(
            ratios[j], left, (((0,), (0,)), ((), ())), preferred_element_type=F32
        )
        total[2 * j] += term[:BLOCK]
        total[2 * j + 1] += term[BLOCK:]

    @pl.when(step == pl.num_programs(0) - 1)
    def _():
        for k in range(2):
            keep[k] = total[place_ref[k]]
        for k in range(2, 8):
            send[k - 2] = total[place_ref[k]]


def sweep(kernel, rows_at, live, columns_at, counts, own, other, panel, out_shape, out_specs, scratch):
    width = own.shape[-1]
    across = counts.shape[1]

    def counts_spec(half):
        return pl.BlockSpec((BLOCK, across), lambda g, rows, live, place: (rows[2 * g + half], 0))

    block = pl.BlockSpec((1, BLOCK, width), lambda g, rows, live, place: (g, 0, 0))
    grid_spec = pltpu.PrefetchScalarGridSpec(
        num_scalar_prefetch=3,
        grid=(8,),
        in_specs=[
            counts_spec(0),
            counts_spec(1),
            block,
            block,
            pl.BlockSpec(panel.shape, lambda g, rows, live, place: (0, 0, 0)),
        ],
        out_specs=out_specs,
        scratch_shapes=[pltpu.VMEM(panel.shape, panel.dtype)] + scratch,
    )
    flops = 4 * counts.shape[0] * across * width
    return pl.pallas_call(
        functools.partial(kernel, across // TILE),
        grid_spec=grid_spec,
        out_shape=out_shape,
        cost_estimate=pl.CostEstimate(
            flops=flops, bytes_accessed=4 * counts.size + 8 * own.size, transcendentals=0
        ),
        compiler_params=pltpu.CompilerParams(vmem_limit_bytes=48 * 2**20),
    )(rows_at, live, columns_at, counts, counts, own, other, panel)


def gather_z(pair):
    up = lax.ppermute(pair, "col", along_z(-1))
    down = lax.ppermute(pair, "col", along_z(1))
    far_up = lax.ppermute(up[0], "col", along_z(-1))
    far_down = lax.ppermute(down[1], "col", along_z(1))
    return jnp.concatenate([pair, up, far_up[None], far_down[None], down], axis=0)


def gather_x(pair):
    up = lax.ppermute(pair, "row", along_x(-1))
    down = lax.ppermute(pair, "row", along_x(1))
    far_up = lax.ppermute(up[0], "row", along_x(-1))
    far_down = lax.ppermute(down[1], "row", along_x(1))
    return jnp.concatenate([pair, up, far_up[None], far_down[None], down], axis=0)


def total_over_col(partial):
    partial = partial + lax.ppermute(partial, "col", SWAP_CORE)
    partial = partial + lax.ppermute(partial, "col", SWAP_PAIR)
    partial = partial + lax.ppermute(partial, "col", along_z(2))
    return partial + lax.ppermute(partial, "col", along_z(1))


def total_over_row(partial):
    partial = partial + lax.ppermute(partial, "row", SWAP_FAR)
    partial = partial + lax.ppermute(partial, "row", along_x(2))
    return partial + lax.ppermute(partial, "row", along_x(1))


def local(click_counts, tile_pattern, row_factors, column_factors):
    width = row_factors.shape[1]
    at_row, at_col = lax.axis_index("row"), lax.axis_index("col")
    z, pair, core = at_col // 4, at_col // 2 % 2, at_col % 2
    x, far = at_row // 2, at_row % 2
    rows_at = jnp.stack(
        [
            (z + dz) % 4 * 4 + (pair + dl) % 2 * 2 + (core + dc) % 2
            for dz in range(4)
            for dl in range(2)
            for dc in range(2)
        ]
    ).astype(jnp.int32)
    columns_at = jnp.stack(
        [(x + dx) % 4 * 2 + (far + dh) % 2 for dx in range(4) for dh in range(2)]
    ).astype(jnp.int32)
    live = tile_pattern.reshape(-1)

    with jax.named_scope("gather_in"):
        row_pair = jnp.stack([row_factors, lax.ppermute(row_factors, "col", SWAP_PAIR)])
        column_pair = jnp.stack([column_factors, lax.ppermute(column_factors, "row", SWAP_FAR)])
        own = gather_z(row_pair)
        panel = gather_x(column_pair)
        other = lax.ppermute(own, "col", SWAP_CORE)
    with jax.named_scope("column_total"):
        column_total = total_over_col(jnp.sum(panel.astype(F32), axis=(0, 1)))

    block = pl.BlockSpec((1, BLOCK, width), lambda g, rows, live, place: (g, 0, 0))
    keep, send = sweep(
        rows_kernel,
        rows_at,
        live,
        columns_at,
        click_counts,
        own,
        other,
        panel,
        (
            jax.ShapeDtypeStruct((8, BLOCK, width), F32),
            jax.ShapeDtypeStruct((8, BLOCK, width), F32),
        ),
        (block, block),
        [],
    )
    with jax.named_scope("reduce_rows"):
        came = lax.ppermute(send, "col", SWAP_CORE)
        partial = (keep + came) * ROW_SCALE
        packed = partial.astype(WIRE)
        arrived = [
            lax.ppermute(packed[2 * dz : 2 * dz + 2], "col", along_z(dz)) for dz in (1, 2, 3)
        ]
        partial = partial[:2] + sum(a.astype(F32) for a in arrived)
        packed = partial.astype(WIRE)
        came = lax.ppermute(packed, "col", SWAP_PAIR)
        share = (packed.astype(F32) + came[::-1].astype(F32)) * (1 / ROW_SCALE)
    updated_pair = (row_pair.astype(F32) * share / column_total).astype(jnp.bfloat16)
    with jax.named_scope("gather_new"):
        own = gather_z(updated_pair)
        other = lax.ppermute(own, "col", SWAP_CORE)
    with jax.named_scope("row_total"):
        row_total = total_over_row(
            jnp.sum(own.astype(F32), axis=(0, 1)) + jnp.sum(other.astype(F32), axis=(0, 1))
        )
    keep, send = sweep(
        columns_kernel,
        rows_at,
        live,
        columns_at,
        click_counts,
        own,
        other,
        panel,
        (
            jax.ShapeDtypeStruct((2, BLOCK, width), F32),
            jax.ShapeDtypeStruct((6, BLOCK, width), F32),
        ),
        (
            pl.BlockSpec((2, BLOCK, width), lambda g, rows, live, place: (0, 0, 0)),
            pl.BlockSpec((6, BLOCK, width), lambda g, rows, live, place: (0, 0, 0)),
        ),
        [pltpu.VMEM((8, BLOCK, width), F32)],
    )
    with jax.named_scope("reduce_columns"):
        send = (send * COLUMN_SCALE).astype(WIRE)
        arrived = [
            lax.ppermute(send[2 * dx - 2 : 2 * dx], "row", along_x(dx)) for dx in (1, 2, 3)
        ]
        partial = keep * COLUMN_SCALE + sum(a.astype(F32) for a in arrived)
        came = lax.ppermute(partial[1].astype(WIRE), "row", SWAP_FAR)
        share = (partial[0] + came.astype(F32)) * (1 / COLUMN_SCALE)
    updated_columns = (column_factors.astype(F32) * share / row_total).astype(jnp.bfloat16)
    return (updated_pair[0], updated_columns)


def solution(mesh):
    in_specs = (P("row", "col"), P("row", "col"), P(("row", "col"), None), P(("col", "row"), None))
    out_specs = (P(("row", "col"), None), P(("col", "row"), None))
    return jax.shard_map(local, mesh=mesh, in_specs=in_specs, out_specs=out_specs, check_vma=False)
```

time: 641 us -> 143 us (0.22)
  blocking collectives: 393 us -> 0 us
  waiting for transfers between devices: 129 us -> 69 us
  loops' own time: 51.3 us -> 0 us
  starting transfers between devices: 0.2 us -> 41.8 us
  matrix products: 33.4 us -> 0 us
  Pallas kernels: 0 us -> 20.8 us
  between operations: 14.5 us -> 1.19 us
    psum x2 -> x0, blocking collectives: 393 us -> none  [the longest x1 206 us: local(): lax.psum(jnp.sum(column_factors.astype(jnp.float32), axis=0), ('row', 'co...]
    all_gather x3 -> x0, waiting for transfers between devices: 115 us -> none  [the longest x1 46.9 us: local(): column_panel = lax.all_gather(column_factors, 'row', axis=0, tiled=True)]
    ppermute x0 -> x32, waiting for transfers between devices: none -> 69 us  [the longest x3 12.6 us: local(): lax.ppermute(packed[2 * dz:2 * dz + 2], 'col', along_z(dz))]
    another operation x2 -> x0, loops' own time: 51.3 us -> none  [sweep(): return lax.fori_loop(0, group_count, visit, initial)]
    ppermute x0 -> x32, starting transfers between devices: none -> 41.8 us  [the longest x2 6.13 us: gather_z(): far_up = lax.ppermute(up[0], 'col', along_z(-1))]
    dot_general x16 -> x0, matrix products: 33.4 us -> none  [the longest x8 19.6 us: add_rows(): term = jnp.dot(ratios, right_tile, preferred_element_type=jnp.float32)]
    pallas_call x0 -> x2, Pallas kernels: none -> 20.8 us  [sweep(): pl.pallas_call(functools.partial(kernel, across // TILE), grid_spec=grid_...]
    reduce_scatter x2 -> x0, waiting for transfers between devices: 13.1 us -> none  [the longest x1 8.62 us: local(): lax.psum_scatter(column_sums, 'row', scatter_dimension=0, tiled=True)]
  transfers between devices with their start and end apart: 5 -> 32, of which waited for: 5 -> 21; matrix products, arithmetic and copies ran while one was open for 1% -> 5% of each run, Pallas kernels for 0% -> 0%
where the time goes in v1:
time: 143 us; the launch traced here: 141 us
  waiting for transfers between devices  69 us (48%)
  starting transfers between devices  41.8 us (29%)
  Pallas kernels  20.8 us (15%)
  other arithmetic  4.49 us (3%)
  local copies, waits for them, and re-layouts  4.1 us (3%)
    pallas_call x2, Pallas kernels, sweep(): pl.pallas_call(functools.partial(kernel, across // TILE), grid_spec=grid_...  20.8 us
    ppermute x3, waiting for transfers between devices, local(): lax.ppermute(packed[2 * dz:2 * dz + 2], 'col', along_z(dz))  12.6 us
    ppermute x2, waiting for transfers between devices, gather_z(): far_down = lax.ppermute(down[1], 'col', along_z(1))  7.42 us
    ppermute x2, waiting for transfers between devices, gather_z(): up = lax.ppermute(pair, 'col', along_z(-1))  6.95 us
    ppermute x2, starting transfers between devices, gather_z(): far_up = lax.ppermute(up[0], 'col', along_z(-1))  6.13 us
    ppermute x2, starting transfers between devices, gather_z(): up = lax.ppermute(pair, 'col', along_z(-1))  5.99 us
    ppermute x2, waiting for transfers between devices, gather_z(): far_up = lax.ppermute(up[0], 'col', along_z(-1))  4.83 us
    ppermute x1, waiting for transfers between devices, local(): came = lax.ppermute(send, 'col', SWAP_CORE)  4.37 us
  transfers between devices with their start and end apart: 32, of which 21 were waited for; matrix products, arithmetic and copies ran while one was open for 5% of the time, Pallas kernels for 0%

profile of v1, /device:TPU:0, one launch (start us, length us, event | category | flops | bytes accessed | tf_op | source)
XLA Modules:
  0.0 141.4 jit_solution(15014266023248835203)
XLA Ops:
  0.6 1.7 %collective-permute-start = (bf16[128,512]{1,0:T(8,128)(2,1)}, bf16[128,512]{1,0:T(8,128)(2,1)S(1)}, u32[]{:S(2)}, u32[]{:S(2)}) collective-permute-start(bf16[128,512]{1,0:T(8,128)(2,1)} %param.6), channel_id=1, source_target_pairs={{0,2},{1,3},{2,0},{3,1},{4,6},{5,7},{6,4},{7,5},{8,10},{9,11},{10,... | collective-permute-start | bytes 393224 | tf_op jit(solution)/shard_map/gather_in/ppermute | solution.py:178
  2.4 2.9 %collective-permute-start.6 = (bf16[128,512]{1,0:T(8,128)(2,1)}, bf16[128,512]{1,0:T(8,128)(2,1)S(1)}, u32[]{:S(2)}, u32[]{:S(2)}) collective-permute-start(bf16[128,512]{1,0:T(8,128)(2,1)} %param.7), channel_id=1, source_target_pairs={{0,16},{16,0},{32,48},{48,32},{64,80},{80,64},{96,112},{112,96},{1... | collective-permute-start | bytes 393224 | tf_op jit(solution)/shard_map/gather_in/ppermute | solution.py:179
  5.3 0.9 constant_dynamic-update-slice_fusion.3
  6.2 0.9 constant_dynamic-update-slice_fusion.7
  7.3 0.8 copy.7
  8.4 0.9 pad_maximum_fusion
  9.3 4.1 %collective-permute-start.1 = (bf16[2,128,512]{2,1,0:T(8,128)(2,1)S(1)}, bf16[2,128,512]{2,1,0:T(8,128)(2,1)S(1)}, u32[]{:S(2)}, u32[]{:S(2)}) collective-permute-start(bf16[2,128,512]{2,1,0:T(8,128)(2,1)S(1)} %pad_maximum_fusion), channel_id=1, source_target_pairs={{0,12},{1,13},{2,14},{3,15},{4,0},{5,1},{6,2},{7,3},{8,4},{9,5},{1... | collective-permute-start | bytes 786440 | tf_op jit(solution)/shard_map/gather_in/ppermute | solution.py:131
  13.4 0.9 pad_maximum_fusion.1
  14.4 2.8 %collective-permute-start.7 = (bf16[2,128,512]{2,1,0:T(8,128)(2,1)S(1)}, bf16[2,128,512]{2,1,0:T(8,128)(2,1)S(1)}, u32[]{:S(2)}, u32[]{:S(2)}) collective-permute-start(bf16[2,128,512]{2,1,0:T(8,128)(2,1)S(1)} %pad_maximum_fusion.1), channel_id=1, source_target_pairs={{0,96},{16,112},{32,0},{48,16},{64,32},{80,48},{96,64},{112,80},{1... | collective-permute-start | bytes 786440 | tf_op jit(solution)/shard_map/gather_in/ppermute | solution.py:139
  17.2 1.2 collective-permute-done.1
  18.4 3.8 %collective-permute-start.2 = (bf16[128,512]{1,0:T(8,128)(2,1)S(1)}, bf16[128,512]{1,0:T(8,128)(2,1)S(1)}, u32[]{:S(2)}, u32[]{:S(2)}) collective-permute-start(bf16[128,512]{1,0:T(8,128)(2,1)S(1)} %slice_bitcast_fusion.7), channel_id=1, source_target_pairs={{0,12},{1,13},{2,14},{3,15},{4,0},{5,1},{6,2},{7,3},{8,4},{9,5},{1... | collective-permute-start | bytes 393224 | tf_op jit(solution)/shard_map/gather_in/ppermute | solution.py:133
  22.3 2.4 %collective-permute-done.2 = bf16[128,512]{1,0:T(8,128)(2,1)S(1)} collective-permute-done((bf16[128,512]{1,0:T(8,128)(2,1)S(1)}, bf16[128,512]{1,0:T(8,128)(2,1)S(1)}, u32[]{:S(2)}, u32[]{:S(2)}) %collective-permute-start.2) | collective-permute-done | bytes 131104 | tf_op jit(solution)/shard_map/gather_in/ppermute | solution.py:133
  24.7 3.7 %collective-permute-done.4 = bf16[128,512]{1,0:T(8,128)(2,1)S(1)} collective-permute-done((bf16[128,512]{1,0:T(8,128)(2,1)S(1)}, bf16[128,512]{1,0:T(8,128)(2,1)S(1)}, u32[]{:S(2)}, u32[]{:S(2)}) %collective-permute-start.4) | collective-permute-done | bytes 131104 | tf_op jit(solution)/shard_map/gather_in/ppermute | solution.py:134
  28.6 2.8 %collective-permute-start.8 = (bf16[128,512]{1,0:T(8,128)(2,1)S(1)}, bf16[128,512]{1,0:T(8,128)(2,1)S(1)}, u32[]{:S(2)}, u32[]{:S(2)}) collective-permute-start(bf16[128,512]{1,0:T(8,128)(2,1)S(1)} %slice_bitcast_fusion.5), channel_id=1, source_target_pairs={{0,96},{16,112},{32,0},{48,16},{64,32},{80,48},{96,64},{112,80},{1... | collective-permute-start | bytes 393224 | tf_op jit(solution)/shard_map/gather_in/ppermute | solution.py:141
  31.6 3.3 %collective-permute-done.8 = bf16[128,512]{1,0:T(8,128)(2,1)S(1)} collective-permute-done((bf16[128,512]{1,0:T(8,128)(2,1)S(1)}, bf16[128,512]{1,0:T(8,128)(2,1)S(1)}, u32[]{:S(2)}, u32[]{:S(2)}) %collective-permute-start.8) | collective-permute-done | bytes 131104 | tf_op jit(solution)/shard_map/gather_in/ppermute | solution.py:141
  34.9 3.5 %collective-permute-done.10 = bf16[128,512]{1,0:T(8,128)(2,1)S(1)} collective-permute-done((bf16[128,512]{1,0:T(8,128)(2,1)S(1)}, bf16[128,512]{1,0:T(8,128)(2,1)S(1)}, u32[]{:S(2)}, u32[]{:S(2)}) %collective-permute-start.10) | collective-permute-done | bytes 131104 | tf_op jit(solution)/shard_map/gather_in/ppermute | solution.py:142
  38.4 10.5 %shard_map.59 = (f32[8,128,512]{2,1,0:T(8,128)S(1)}, f32[8,128,512]{2,1,0:T(8,128)}) custom-call(s32[16]{0:T(128)S(1)} %stack.115.rows_ref, s32[32]{0:T(128)S(1)} %reshape.10.live_ref, s32[8]{0:T(128)S(1)} %stack.124.place_ref, s32[2048,1024]{1,0:T(8,128)} %c1.3, s32[2048,1024]{1,0:T(8,128)} %c1.3, ...), custom_call_target="tpu_custom_call" | custom-call | flops 4294967296 | bytes 12582912 | tf_op jit(solution)/shard_map/pallas_call | solution.py:119
  48.9 4.4 %collective-permute-done.11 = f32[8,128,512]{2,1,0:T(8,128)S(1)} collective-permute-done((f32[8,128,512]{2,1,0:T(8,128)}, f32[8,128,512]{2,1,0:T(8,128)S(1)}, u32[]{:S(2)}, u32[]{:S(2)}) %collective-permute-start.11) | collective-permute-done | bytes 2097184 | tf_op jit(solution)/shard_map/reduce_rows/ppermute | solution.py:204
  54.1 1.4 collective-permute-start.13
  55.5 1.8 %collective-permute-start.14 = (f16[2,128,512]{2,1,0:T(8,128)(2,1)S(1)}, f16[2,128,512]{2,1,0:T(8,128)(2,1)S(1)}, u32[]{:S(2)}, u32[]{:S(2)}) collective-permute-start(f16[2,128,512]{2,1,0:T(8,128)(2,1)S(1)} %get-tuple-element.15), channel_id=1, source_target_pairs={{0,12},{1,13},{2,14},{3,15},{4,0},{5,1},{6,2},{7,3},{8,4},{9,5},{1... | collective-permute-start | bytes 786440 | tf_op jit(solution)/shard_map/reduce_rows/ppermute | solution.py:208
  57.3 11.9 %collective-permute-done.12 = f16[2,128,512]{2,1,0:T(8,128)(2,1)S(1)} collective-permute-done((f16[2,128,512]{2,1,0:T(8,128)(2,1)S(1)}, f16[2,128,512]{2,1,0:T(8,128)(2,1)S(1)}, u32[]{:S(2)}, u32[]{:S(2)}) %collective-permute-start.12) | collective-permute-done | bytes 262176 | tf_op jit(solution)/shard_map/reduce_rows/ppermute | solution.py:208
  69.3 0.6 collective-permute-done.14
  70.6 1.1 collective-permute-done.16
  71.7 1.9 %collective-permute-start.17 = (f32[512]{0:T(512)S(1)}, f32[512]{0:T(512)S(1)}, u32[]{:S(2)}, u32[]{:S(2)}) collective-permute-start(f32[512]{0:T(512)S(1)} %add.379), channel_id=1, source_target_pairs={{0,2},{1,3},{2,0},{3,1},{4,6},{5,7},{6,4},{7,5},{8,10},{9,11},{10,... | collective-permute-start | bytes 6152 | tf_op jit(solution)/shard_map/column_total/ppermute | solution.py:148
  73.6 3.8 %collective-permute-done.17 = f32[512]{0:T(512)S(1)} collective-permute-done((f32[512]{0:T(512)S(1)}, f32[512]{0:T(512)S(1)}, u32[]{:S(2)}, u32[]{:S(2)}) %collective-permute-start.17) | collective-permute-done | bytes 2080 | tf_op jit(solution)/shard_map/column_total/ppermute | solution.py:148
  77.4 1.2 collective-permute-start.18
  78.6 3.9 %collective-permute-done.18 = f32[512]{0:T(512)S(1)} collective-permute-done((f32[512]{0:T(512)S(1)}, f32[512]{0:T(512)S(1)}, u32[]{:S(2)}, u32[]{:S(2)}) %collective-permute-start.18) | collective-permute-done | bytes 2080 | tf_op jit(solution)/shard_map/column_total/ppermute | solution.py:149
  82.5 1.2 collective-permute-start.19
  83.7 3.6 %collective-permute-done.19 = f32[512]{0:T(512)S(1)} collective-permute-done((f32[512]{0:T(512)S(1)}, f32[512]{0:T(512)S(1)}, u32[]{:S(2)}, u32[]{:S(2)}) %collective-permute-start.19) | collective-permute-done | bytes 2080 | tf_op jit(solution)/shard_map/column_total/ppermute | solution.py:150
  87.5 1.9 %collective-permute-start.20 = (bf16[2,128,512]{2,1,0:T(8,128)(2,1)S(1)}, bf16[2,128,512]{2,1,0:T(8,128)(2,1)S(1)}, u32[]{:S(2)}, u32[]{:S(2)}) collective-permute-start(bf16[2,128,512]{2,1,0:T(8,128)(2,1)S(1)} %get-tuple-element.11), channel_id=1, source_target_pairs={{0,12},{1,13},{2,14},{3,15},{4,0},{5,1},{6,2},{7,3},{8,4},{9,5},{1... | collective-permute-start | bytes 786440 | tf_op jit(solution)/shard_map/gather_new/ppermute | solution.py:131
  89.6 5.8 %collective-permute-done.20 = bf16[2,128,512]{2,1,0:T(8,128)(2,1)S(1)} collective-permute-done((bf16[2,128,512]{2,1,0:T(8,128)(2,1)S(1)}, bf16[2,128,512]{2,1,0:T(8,128)(2,1)S(1)}, u32[]{:S(2)}, u32[]{:S(2)}) %collective-permute-start.20) | collective-permute-done | bytes 262176 | tf_op jit(solution)/shard_map/gather_new/ppermute | solution.py:131
  95.3 2.4 %collective-permute-start.21 = (bf16[128,512]{1,0:T(8,128)(2,1)S(1)}, bf16[128,512]{1,0:T(8,128)(2,1)S(1)}, u32[]{:S(2)}, u32[]{:S(2)}) collective-permute-start(bf16[128,512]{1,0:T(8,128)(2,1)S(1)} %slice_bitcast_fusion.2), channel_id=1, source_target_pairs={{0,12},{1,13},{2,14},{3,15},{4,0},{5,1},{6,2},{7,3},{8,4},{9,5},{1... | collective-permute-start | bytes 393224 | tf_op jit(solution)/shard_map/gather_new/ppermute | solution.py:133
  97.9 2.4 %collective-permute-done.21 = bf16[128,512]{1,0:T(8,128)(2,1)S(1)} collective-permute-done((bf16[128,512]{1,0:T(8,128)(2,1)S(1)}, bf16[128,512]{1,0:T(8,128)(2,1)S(1)}, u32[]{:S(2)}, u32[]{:S(2)}) %collective-permute-start.21) | collective-permute-done | bytes 131104 | tf_op jit(solution)/shard_map/gather_new/ppermute | solution.py:133
  100.4 3.7 %collective-permute-done.23 = bf16[128,512]{1,0:T(8,128)(2,1)S(1)} collective-permute-done((bf16[128,512]{1,0:T(8,128)(2,1)S(1)}, bf16[128,512]{1,0:T(8,128)(2,1)S(1)}, u32[]{:S(2)}, u32[]{:S(2)}) %collective-permute-start.23) | collective-permute-done | bytes 131104 | tf_op jit(solution)/shard_map/gather_new/ppermute | solution.py:134
  104.4 2.6 %collective-permute-done.24.b = bf16[8,128,512]{2,1,0:T(8,128)(2,1)S(1)} collective-permute-done((bf16[8,128,512]{2,1,0:T(8,128)(2,1)S(1)}, bf16[8,128,512]{2,1,0:T(8,128)(2,1)S(1)}, u32[]{:S(2)}, u32[]{:S(2)}) %collective-permute-start.24) | collective-permute-done | bytes 1048608 | tf_op jit(solution)/shard_map/gather_new/ppermute | solution.py:217
  107.0 10.3 %shard_map.60 = (f32[2,128,512]{2,1,0:T(8,128)S(1)}, f32[6,128,512]{2,1,0:T(8,128)S(1)}) custom-call(s32[16]{0:T(128)S(1)} %stack.115.rows_ref, s32[32]{0:T(128)S(1)} %reshape.10.live_ref, s32[8]{0:T(128)S(1)} %stack.124.place_ref, s32[2048,1024]{1,0:T(8,128)} %c1.3, s32[2048,1024]{1,0:T(8,128)} %c1.3, ...), custom_call_target="tpu_custom_call" | custom-call | flops 4294967296 | bytes 12582912 | tf_op jit(solution)/shard_map/pallas_call | solution.py:119
  117.8 1.7 %collective-permute-start.26 = (f16[2,128,512]{2,1,0:T(8,128)(2,1)S(1)}, f16[2,128,512]{2,1,0:T(8,128)(2,1)S(1)}, u32[]{:S(2)}, u32[]{:S(2)}) collective-permute-start(f16[2,128,512]{2,1,0:T(8,128)(2,1)S(1)} %get-tuple-element.19), channel_id=1, source_target_pairs={{0,64},{16,80},{32,96},{48,112},{64,0},{80,16},{96,32},{112,48},{1... | collective-permute-start | bytes 786440 | tf_op jit(solution)/shard_map/reduce_columns/ppermute | solution.py:244
  119.5 1.6 %collective-permute-start.27 = (f16[2,128,512]{2,1,0:T(8,128)(2,1)S(1)}, f16[2,128,512]{2,1,0:T(8,128)(2,1)S(1)}, u32[]{:S(2)}, u32[]{:S(2)}) collective-permute-start(f16[2,128,512]{2,1,0:T(8,128)(2,1)S(1)} %get-tuple-element.18), channel_id=1, source_target_pairs={{0,96},{16,112},{32,0},{48,16},{64,32},{80,48},{96,64},{112,80},{1... | collective-permute-start | bytes 786440 | tf_op jit(solution)/shard_map/reduce_columns/ppermute | solution.py:244
  121.5 1.2 collective-permute-start.29
  122.6 4.0 %collective-permute-done.29 = f32[512]{0:T(512)S(1)} collective-permute-done((f32[512]{0:T(512)S(1)}, f32[512]{0:T(512)S(1)}, u32[]{:S(2)}, u32[]{:S(2)}) %collective-permute-start.29) | collective-permute-done | bytes 2080 | tf_op jit(solution)/shard_map/row_total/ppermute | solution.py:154
  126.6 2.9 %collective-permute-start.30 = (f32[512]{0:T(512)S(1)}, f32[512]{0:T(512)S(1)}, u32[]{:S(2)}, u32[]{:S(2)}) collective-permute-start(f32[512]{0:T(512)S(1)} %add.388), channel_id=1, source_target_pairs={{0,64},{16,80},{32,96},{48,112},{64,0},{80,16},{96,32},{112,48},{1... | collective-permute-start | bytes 6152 | tf_op jit(solution)/shard_map/row_total/ppermute | solution.py:155
  129.5 2.2 %collective-permute-done.30 = f32[512]{0:T(512)S(1)} collective-permute-done((f32[512]{0:T(512)S(1)}, f32[512]{0:T(512)S(1)}, u32[]{:S(2)}, u32[]{:S(2)}) %collective-permute-start.30) | collective-permute-done | bytes 2080 | tf_op jit(solution)/shard_map/row_total/ppermute | solution.py:155
  131.7 2.2 %collective-permute-start.31 = (f32[512]{0:T(512)S(1)}, f32[512]{0:T(512)S(1)}, u32[]{:S(2)}, u32[]{:S(2)}) collective-permute-start(f32[512]{0:T(512)S(1)} %add.389), channel_id=1, source_target_pairs={{0,32},{16,48},{32,64},{48,80},{64,96},{80,112},{96,0},{112,16},{1... | collective-permute-start | bytes 6152 | tf_op jit(solution)/shard_map/row_total/ppermute | solution.py:156
  134.1 1.2 collective-permute-start.28
  135.3 0.7 slice_bitcast_fusion.3
  135.9 1.9 %collective-permute-done.31 = f32[512]{0:T(512)S(1)} collective-permute-done((f32[512]{0:T(512)S(1)}, f32[512]{0:T(512)S(1)}, u32[]{:S(2)}, u32[]{:S(2)}) %collective-permute-start.31) | collective-permute-done | bytes 2080 | tf_op jit(solution)/shard_map/row_total/ppermute | solution.py:156
  137.9 2.8 %collective-permute-done.28 = f16[128,512]{1,0:T(8,128)(2,1)S(1)} collective-permute-done((f16[128,512]{1,0:T(8,128)(2,1)S(1)}, f16[128,512]{1,0:T(8,128)(2,1)S(1)}, u32[]{:S(2)}, u32[]{:S(2)}) %collective-permute-start.28) | collective-permute-done | bytes 131104 | tf_op jit(solution)/shard_map/reduce_columns/ppermute | solution.py:247
  140.7 0.7 fusion.5
  (71 shorter events, 4.1 us)
Async XLA Ops:
  0.6 7.7 %collective-permute-start = (bf16[128,512]{1,0:T(8,128)(2,1)}, bf16[128,512]{1,0:T(8,128)(2,1)S(1)}, u32[]{:S(2)}, u32[]{:S(2)}) collective-permute-start(bf16[128,512]{1,0:T(8,128)(2,1)} %param.6), channel_id=1, source_target_pairs={{0,2},{1,3},{2,0},{3,1},{4,6},{5,7},{6,4},{7,5},{8,10},{9,11},{10,... | collective-permute-start | bytes 393224 | tf_op jit(solution)/shard_map/gather_in/ppermute | solution.py:178
  2.4 11.1 %collective-permute-start.6 = (bf16[128,512]{1,0:T(8,128)(2,1)}, bf16[128,512]{1,0:T(8,128)(2,1)S(1)}, u32[]{:S(2)}, u32[]{:S(2)}) collective-permute-start(bf16[128,512]{1,0:T(8,128)(2,1)} %param.7), channel_id=1, source_target_pairs={{0,16},{16,0},{32,48},{48,32},{64,80},{80,64},{96,112},{112,96},{1... | collective-permute-start | bytes 393224 | tf_op jit(solution)/shard_map/gather_in/ppermute | solution.py:179
  9.3 9.1 %collective-permute-start.1 = (bf16[2,128,512]{2,1,0:T(8,128)(2,1)S(1)}, bf16[2,128,512]{2,1,0:T(8,128)(2,1)S(1)}, u32[]{:S(2)}, u32[]{:S(2)}) collective-permute-start(bf16[2,128,512]{2,1,0:T(8,128)(2,1)S(1)} %pad_maximum_fusion), channel_id=1, source_target_pairs={{0,12},{1,13},{2,14},{3,15},{4,0},{5,1},{6,2},{7,3},{8,4},{9,5},{1... | collective-permute-start | bytes 786440 | tf_op jit(solution)/shard_map/gather_in/ppermute | solution.py:131
  13.4 8.8 %collective-permute-start.3 = (bf16[2,128,512]{2,1,0:T(8,128)(2,1)S(1)}, bf16[2,128,512]{2,1,0:T(8,128)(2,1)S(1)}, u32[]{:S(2)}, u32[]{:S(2)}) collective-permute-start(bf16[2,128,512]{2,1,0:T(8,128)(2,1)S(1)} %pad_maximum_fusion), channel_id=1, source_target_pairs={{0,4},{1,5},{2,6},{3,7},{4,8},{5,9},{6,10},{7,11},{8,12},{9,13},{1... | collective-permute-start | bytes 786440 | tf_op jit(solution)/shard_map/gather_in/ppermute | solution.py:132
  14.4 14.2 %collective-permute-start.7 = (bf16[2,128,512]{2,1,0:T(8,128)(2,1)S(1)}, bf16[2,128,512]{2,1,0:T(8,128)(2,1)S(1)}, u32[]{:S(2)}, u32[]{:S(2)}) collective-permute-start(bf16[2,128,512]{2,1,0:T(8,128)(2,1)S(1)} %pad_maximum_fusion.1), channel_id=1, source_target_pairs={{0,96},{16,112},{32,0},{48,16},{64,32},{80,48},{96,64},{112,80},{1... | collective-permute-start | bytes 786440 | tf_op jit(solution)/shard_map/gather_in/ppermute | solution.py:139
  17.2 14.3 %collective-permute-start.9 = (bf16[2,128,512]{2,1,0:T(8,128)(2,1)S(1)}, bf16[2,128,512]{2,1,0:T(8,128)(2,1)S(1)}, u32[]{:S(2)}, u32[]{:S(2)}) collective-permute-start(bf16[2,128,512]{2,1,0:T(8,128)(2,1)S(1)} %pad_maximum_fusion.1), channel_id=1, source_target_pairs={{0,32},{16,48},{32,64},{48,80},{64,96},{80,112},{96,0},{112,16},{1... | collective-permute-start | bytes 786440 | tf_op jit(solution)/shard_map/gather_in/ppermute | solution.py:140
  18.4 6.3 %collective-permute-start.2 = (bf16[128,512]{1,0:T(8,128)(2,1)S(1)}, bf16[128,512]{1,0:T(8,128)(2,1)S(1)}, u32[]{:S(2)}, u32[]{:S(2)}) collective-permute-start(bf16[128,512]{1,0:T(8,128)(2,1)S(1)} %slice_bitcast_fusion.7), channel_id=1, source_target_pairs={{0,12},{1,13},{2,14},{3,15},{4,0},{5,1},{6,2},{7,3},{8,4},{9,5},{1... | collective-permute-start | bytes 393224 | tf_op jit(solution)/shard_map/gather_in/ppermute | solution.py:133
  22.2 6.2 %collective-permute-start.4 = (bf16[128,512]{1,0:T(8,128)(2,1)S(1)}, bf16[128,512]{1,0:T(8,128)(2,1)S(1)}, u32[]{:S(2)}, u32[]{:S(2)}) collective-permute-start(bf16[128,512]{1,0:T(8,128)(2,1)S(1)} %slice_bitcast_fusion.6), channel_id=1, source_target_pairs={{0,4},{1,5},{2,6},{3,7},{4,8},{5,9},{6,10},{7,11},{8,12},{9,13},{1... | collective-permute-start | bytes 393224 | tf_op jit(solution)/shard_map/gather_in/ppermute | solution.py:134
  28.5 9.9 %collective-permute-start.5 = (bf16[8,128,512]{2,1,0:T(8,128)(2,1)S(1)}, bf16[8,128,512]{2,1,0:T(8,128)(2,1)S(1)}, u32[]{:S(2)}, u32[]{:S(2)}) collective-permute-start(bf16[8,128,512]{2,1,0:T(8,128)(2,1)S(1)} %constant_dynamic-update-slice_fusion.a), channel_id=1, source_target_pairs={{0,1},{1,0},{2,3},{3,2},{4,5},{5,4},{6,7},{7,6},{8,9},{9,8},{10,11... | collective-permute-start | bytes 3145736 | tf_op jit(solution)/shard_map/gather_in/ppermute | solution.py:182
  28.6 6.2 %collective-permute-start.8 = (bf16[128,512]{1,0:T(8,128)(2,1)S(1)}, bf16[128,512]{1,0:T(8,128)(2,1)S(1)}, u32[]{:S(2)}, u32[]{:S(2)}) collective-permute-start(bf16[128,512]{1,0:T(8,128)(2,1)S(1)} %slice_bitcast_fusion.5), channel_id=1, source_target_pairs={{0,96},{16,112},{32,0},{48,16},{64,32},{80,48},{96,64},{112,80},{1... | collective-permute-start | bytes 393224 | tf_op jit(solution)/shard_map/gather_in/ppermute | solution.py:141
  31.5 6.9 %collective-permute-start.10 = (bf16[128,512]{1,0:T(8,128)(2,1)S(1)}, bf16[128,512]{1,0:T(8,128)(2,1)S(1)}, u32[]{:S(2)}, u32[]{:S(2)}) collective-permute-start(bf16[128,512]{1,0:T(8,128)(2,1)S(1)} %slice_bitcast_fusion.4), channel_id=1, source_target_pairs={{0,32},{16,48},{32,64},{48,80},{64,96},{80,112},{96,0},{112,16},{1... | collective-permute-start | bytes 393224 | tf_op jit(solution)/shard_map/gather_in/ppermute | solution.py:142
  48.9 4.4 %collective-permute-start.11 = (f32[8,128,512]{2,1,0:T(8,128)}, f32[8,128,512]{2,1,0:T(8,128)S(1)}, u32[]{:S(2)}, u32[]{:S(2)}) collective-permute-start(f32[8,128,512]{2,1,0:T(8,128)} %get-tuple-element.7), channel_id=1, source_target_pairs={{0,1},{1,0},{2,3},{3,2},{4,5},{5,4},{6,7},{7,6},{8,9},{9,8},{10,11... | collective-permute-start | bytes 6291464 | tf_op jit(solution)/shard_map/reduce_rows/ppermute | solution.py:204
  53.8 33.5 %copy-start = (bf16[128,512]{1,0:T(8,128)(2,1)S(1)}, bf16[128,512]{1,0:T(8,128)(2,1)}, u32[]{:S(2)}) copy-start(bf16[128,512]{1,0:T(8,128)(2,1)} %param.6) | copy-start | bytes 393220
  54.0 15.2 %collective-permute-start.12 = (f16[2,128,512]{2,1,0:T(8,128)(2,1)S(1)}, f16[2,128,512]{2,1,0:T(8,128)(2,1)S(1)}, u32[]{:S(2)}, u32[]{:S(2)}) collective-permute-start(f16[2,128,512]{2,1,0:T(8,128)(2,1)S(1)} %get-tuple-element.14), channel_id=1, source_target_pairs={{0,4},{1,5},{2,6},{3,7},{4,8},{5,9},{6,10},{7,11},{8,12},{9,13},{1... | collective-permute-start | bytes 786440 | tf_op jit(solution)/shard_map/reduce_rows/ppermute | solution.py:208
  54.1 15.2 %collective-permute-start.13 = (f16[2,128,512]{2,1,0:T(8,128)(2,1)S(1)}, f16[2,128,512]{2,1,0:T(8,128)(2,1)S(1)}, u32[]{:S(2)}, u32[]{:S(2)}) collective-permute-start(f16[2,128,512]{2,1,0:T(8,128)(2,1)S(1)} %get-tuple-element.16), channel_id=1, source_target_pairs={{0,8},{1,9},{2,10},{3,11},{4,12},{5,13},{6,14},{7,15},{8,0},{9,1},... | collective-permute-start | bytes 786440 | tf_op jit(solution)/shard_map/reduce_rows/ppermute | solution.py:208
  55.5 14.4 %collective-permute-start.14 = (f16[2,128,512]{2,1,0:T(8,128)(2,1)S(1)}, f16[2,128,512]{2,1,0:T(8,128)(2,1)S(1)}, u32[]{:S(2)}, u32[]{:S(2)}) collective-permute-start(f16[2,128,512]{2,1,0:T(8,128)(2,1)S(1)} %get-tuple-element.15), channel_id=1, source_target_pairs={{0,12},{1,13},{2,14},{3,15},{4,0},{5,1},{6,2},{7,3},{8,4},{9,5},{1... | collective-permute-start | bytes 786440 | tf_op jit(solution)/shard_map/reduce_rows/ppermute | solution.py:208
  70.1 17.3 %collective-permute-start.15 = (f16[2,128,512]{2,1,0:T(8,128)(2,1)S(1)}, f16[2,128,512]{2,1,0:T(8,128)(2,1)S(1)}, u32[]{:S(2)}, u32[]{:S(2)}) collective-permute-start(f16[2,128,512]{2,1,0:T(8,128)(2,1)S(1)} %fusion), channel_id=1, source_target_pairs={{0,2},{1,3},{2,0},{3,1},{4,6},{5,7},{6,4},{7,5},{8,10},{9,11},{10,... | collective-permute-start | bytes 786440 | tf_op jit(solution)/shard_map/reduce_rows/ppermute | solution.py:212
  70.5 1.2 collective-permute-start.16
  71.7 5.7 %collective-permute-start.17 = (f32[512]{0:T(512)S(1)}, f32[512]{0:T(512)S(1)}, u32[]{:S(2)}, u32[]{:S(2)}) collective-permute-start(f32[512]{0:T(512)S(1)} %add.379), channel_id=1, source_target_pairs={{0,2},{1,3},{2,0},{3,1},{4,6},{5,7},{6,4},{7,5},{8,10},{9,11},{10,... | collective-permute-start | bytes 6152 | tf_op jit(solution)/shard_map/column_total/ppermute | solution.py:148
  77.4 5.1 %collective-permute-start.18 = (f32[512]{0:T(512)S(1)}, f32[512]{0:T(512)S(1)}, u32[]{:S(2)}, u32[]{:S(2)}) collective-permute-start(f32[512]{0:T(512)S(1)} %add.380), channel_id=1, source_target_pairs={{0,8},{1,9},{2,10},{3,11},{4,12},{5,13},{6,14},{7,15},{8,0},{9,1},... | collective-permute-start | bytes 6152 | tf_op jit(solution)/shard_map/column_total/ppermute | solution.py:149
  82.5 4.8 %collective-permute-start.19 = (f32[512]{0:T(512)S(1)}, f32[512]{0:T(512)S(1)}, u32[]{:S(2)}, u32[]{:S(2)}) collective-permute-start(f32[512]{0:T(512)S(1)} %add.381), channel_id=1, source_target_pairs={{0,4},{1,5},{2,6},{3,7},{4,8},{5,9},{6,10},{7,11},{8,12},{9,13},{1... | collective-permute-start | bytes 6152 | tf_op jit(solution)/shard_map/column_total/ppermute | solution.py:150
  87.5 7.8 %collective-permute-start.20 = (bf16[2,128,512]{2,1,0:T(8,128)(2,1)S(1)}, bf16[2,128,512]{2,1,0:T(8,128)(2,1)S(1)}, u32[]{:S(2)}, u32[]{:S(2)}) collective-permute-start(bf16[2,128,512]{2,1,0:T(8,128)(2,1)S(1)} %get-tuple-element.11), channel_id=1, source_target_pairs={{0,12},{1,13},{2,14},{3,15},{4,0},{5,1},{6,2},{7,3},{8,4},{9,5},{1... | collective-permute-start | bytes 786440 | tf_op jit(solution)/shard_map/gather_new/ppermute | solution.py:131
  89.4 8.4 %collective-permute-start.22 = (bf16[2,128,512]{2,1,0:T(8,128)(2,1)S(1)}, bf16[2,128,512]{2,1,0:T(8,128)(2,1)S(1)}, u32[]{:S(2)}, u32[]{:S(2)}) collective-permute-start(bf16[2,128,512]{2,1,0:T(8,128)(2,1)S(1)} %get-tuple-element.11), channel_id=1, source_target_pairs={{0,4},{1,5},{2,6},{3,7},{4,8},{5,9},{6,10},{7,11},{8,12},{9,13},{1... | collective-permute-start | bytes 786440 | tf_op jit(solution)/shard_map/gather_new/ppermute | solution.py:132
  95.3 5.0 %collective-permute-start.21 = (bf16[128,512]{1,0:T(8,128)(2,1)S(1)}, bf16[128,512]{1,0:T(8,128)(2,1)S(1)}, u32[]{:S(2)}, u32[]{:S(2)}) collective-permute-start(bf16[128,512]{1,0:T(8,128)(2,1)S(1)} %slice_bitcast_fusion.2), channel_id=1, source_target_pairs={{0,12},{1,13},{2,14},{3,15},{4,0},{5,1},{6,2},{7,3},{8,4},{9,5},{1... | collective-permute-start | bytes 393224 | tf_op jit(solution)/shard_map/gather_new/ppermute | solution.py:133
  97.8 6.2 %collective-permute-start.23 = (bf16[128,512]{1,0:T(8,128)(2,1)S(1)}, bf16[128,512]{1,0:T(8,128)(2,1)S(1)}, u32[]{:S(2)}, u32[]{:S(2)}) collective-permute-start(bf16[128,512]{1,0:T(8,128)(2,1)S(1)} %slice_bitcast_fusion.1), channel_id=1, source_target_pairs={{0,4},{1,5},{2,6},{3,7},{4,8},{5,9},{6,10},{7,11},{8,12},{9,13},{1... | collective-permute-start | bytes 393224 | tf_op jit(solution)/shard_map/gather_new/ppermute | solution.py:134
  104.1 2.9 %collective-permute-start.24 = (bf16[8,128,512]{2,1,0:T(8,128)(2,1)S(1)}, bf16[8,128,512]{2,1,0:T(8,128)(2,1)S(1)}, u32[]{:S(2)}, u32[]{:S(2)}) collective-permute-start(bf16[8,128,512]{2,1,0:T(8,128)(2,1)S(1)} %constant_dynamic-update-slice_fusion.8.a), channel_id=1, source_target_pairs={{0,1},{1,0},{2,3},{3,2},{4,5},{5,4},{6,7},{7,6},{8,9},{9,8},{10,11... | collective-permute-start | bytes 3145736 | tf_op jit(solution)/shard_map/gather_new/ppermute | solution.py:217
  117.7 16.2 %collective-permute-start.25 = (f16[2,128,512]{2,1,0:T(8,128)(2,1)S(1)}, f16[2,128,512]{2,1,0:T(8,128)(2,1)S(1)}, u32[]{:S(2)}, u32[]{:S(2)}) collective-permute-start(f16[2,128,512]{2,1,0:T(8,128)(2,1)S(1)} %get-tuple-element.17), channel_id=1, source_target_pairs={{0,32},{16,48},{32,64},{48,80},{64,96},{80,112},{96,0},{112,16},{1... | collective-permute-start | bytes 786440 | tf_op jit(solution)/shard_map/reduce_columns/ppermute | solution.py:244
  117.8 16.1 %collective-permute-start.26 = (f16[2,128,512]{2,1,0:T(8,128)(2,1)S(1)}, f16[2,128,512]{2,1,0:T(8,128)(2,1)S(1)}, u32[]{:S(2)}, u32[]{:S(2)}) collective-permute-start(f16[2,128,512]{2,1,0:T(8,128)(2,1)S(1)} %get-tuple-element.19), channel_id=1, source_target_pairs={{0,64},{16,80},{32,96},{48,112},{64,0},{80,16},{96,32},{112,48},{1... | collective-permute-start | bytes 786440 | tf_op jit(solution)/shard_map/reduce_columns/ppermute | solution.py:244
  119.5 21.2 %copy-start.1 = (bf16[128,512]{1,0:T(8,128)(2,1)S(1)}, bf16[128,512]{1,0:T(8,128)(2,1)}, u32[]{:S(2)}) copy-start(bf16[128,512]{1,0:T(8,128)(2,1)} %param.7) | copy-start | bytes 393220
  119.5 14.4 %collective-permute-start.27 = (f16[2,128,512]{2,1,0:T(8,128)(2,1)S(1)}, f16[2,128,512]{2,1,0:T(8,128)(2,1)S(1)}, u32[]{:S(2)}, u32[]{:S(2)}) collective-permute-start(f16[2,128,512]{2,1,0:T(8,128)(2,1)S(1)} %get-tuple-element.18), channel_id=1, source_target_pairs={{0,96},{16,112},{32,0},{48,16},{64,32},{80,48},{96,64},{112,80},{1... | collective-permute-start | bytes 786440 | tf_op jit(solution)/shard_map/reduce_columns/ppermute | solution.py:244
  121.5 5.2 %collective-permute-start.29 = (f32[512]{0:T(512)S(1)}, f32[512]{0:T(512)S(1)}, u32[]{:S(2)}, u32[]{:S(2)}) collective-permute-start(f32[512]{0:T(512)S(1)} %add.387), channel_id=1, source_target_pairs={{0,16},{16,0},{32,48},{48,32},{64,80},{80,64},{96,112},{112,96},{1... | collective-permute-start | bytes 6152 | tf_op jit(solution)/shard_map/row_total/ppermute | solution.py:154
  126.6 5.1 %collective-permute-start.30 = (f32[512]{0:T(512)S(1)}, f32[512]{0:T(512)S(1)}, u32[]{:S(2)}, u32[]{:S(2)}) collective-permute-start(f32[512]{0:T(512)S(1)} %add.388), channel_id=1, source_target_pairs={{0,64},{16,80},{32,96},{48,112},{64,0},{80,16},{96,32},{112,48},{1... | collective-permute-start | bytes 6152 | tf_op jit(solution)/shard_map/row_total/ppermute | solution.py:155
  131.7 6.1 %collective-permute-start.31 = (f32[512]{0:T(512)S(1)}, f32[512]{0:T(512)S(1)}, u32[]{:S(2)}, u32[]{:S(2)}) collective-permute-start(f32[512]{0:T(512)S(1)} %add.389), channel_id=1, source_target_pairs={{0,32},{16,48},{32,64},{48,80},{64,96},{80,112},{96,0},{112,16},{1... | collective-permute-start | bytes 6152 | tf_op jit(solution)/shard_map/row_total/ppermute | solution.py:156
  134.1 6.6 %collective-permute-start.28 = (f16[128,512]{1,0:T(8,128)(2,1)S(1)}, f16[128,512]{1,0:T(8,128)(2,1)S(1)}, u32[]{:S(2)}, u32[]{:S(2)}) collective-permute-start(f16[128,512]{1,0:T(8,128)(2,1)S(1)} %fusion.6), channel_id=1, source_target_pairs={{0,16},{16,0},{32,48},{48,32},{64,80},{80,64},{96,112},{112,96},{1... | collective-permute-start | bytes 393224 | tf_op jit(solution)/shard_map/reduce_columns/ppermute | solution.py:247

commit v2 on v1

v2 whole, which is shorter than its diff:
```python
import functools

import jax
import jax.numpy as jnp
from jax import lax
from jax.experimental import pallas as pl
from jax.experimental.pallas import tpu as pltpu
from jax.sharding import PartitionSpec as P

WIRE = jnp.float16
ROW_SCALE = 2.0**-6
COLUMN_SCALE = 2.0**-9
COARSE_SCALE = 2.0**-5
FINE_SCALE = 2.0**14
FINE_LIMIT = 61440.0
BLOCK = 128
TILE = 256
F32 = jnp.float32


CHIP_GROUPS = [list(range(core, 16, 2)) for core in range(2)]
SWAP_CORE = [(j, j ^ 1) for j in range(16)]
PAD = 8


def contract_last(a, b):
    return lax.dot_general(a, b, (((1,), (1,)), ((), ())), preferred_element_type=F32)


def tile_ratios(counts, predicted, live_ref, row_tile, tiles_across):
    parts = []
    for j in range(tiles_across):
        window = slice(j * TILE, (j + 1) * TILE)
        live = live_ref[row_tile * tiles_across + j] > 0
        value = counts[:, window].astype(F32) / predicted[:, window]
        parts.append(jnp.where(live, value, 0.0).astype(jnp.bfloat16))
    return parts


def rows_kernel(tiles_across, rows_ref, live_ref, c0, c1, a, b, panel, keep, send):
    step = pl.program_id(0)
    columns = panel[...].reshape(-1, panel.shape[-1])
    left = jnp.concatenate([a[0], b[0]], axis=0)
    counts = jnp.concatenate([c0[...], c1[...]], axis=0)
    predicted = contract_last(left, columns)
    ratios = tile_ratios(counts, predicted, live_ref, step, tiles_across)
    total = jnp.dot(jnp.concatenate(ratios, axis=1), columns, preferred_element_type=F32)
    keep[0] = total[:BLOCK]
    send[0] = total[BLOCK:]


def columns_kernel(tiles_across, rows_ref, live_ref, c0, c1, a, b, panel, sums, rows_total):
    step = pl.program_id(0)

    @pl.when(step == 0)
    def _():
        sums[...] = jnp.zeros_like(sums)
        rows_total[...] = jnp.zeros_like(rows_total)

    columns = panel[...].reshape(-1, panel.shape[-1])
    left = jnp.concatenate([a[0], b[0]], axis=0)
    counts = jnp.concatenate([c0[...], c1[...]], axis=0)
    predicted = contract_last(left, columns)
    ratios = tile_ratios(counts, predicted, live_ref, step, tiles_across)
    rows_total[...] += jnp.sum(left.astype(F32).reshape(-1, 8, left.shape[-1]), axis=0)
    for j in range(tiles_across):
        term = lax.dot_general(
            ratios[j], left, (((0,), (0,)), ((), ())), preferred_element_type=F32
        )
        sums[2 * j] += term[:BLOCK]
        sums[2 * j + 1] += term[BLOCK:]


def sweep(kernel, rows_at, live, counts, own, other, panel, out_shape, out_specs):
    width = own.shape[-1]
    across = counts.shape[1]

    def counts_spec(half):
        return pl.BlockSpec((BLOCK, across), lambda g, rows, live: (rows[2 * g + half], 0))

    block = pl.BlockSpec((1, BLOCK, width), lambda g, rows, live: (g, 0, 0))
    grid_spec = pltpu.PrefetchScalarGridSpec(
        num_scalar_prefetch=2,
        grid=(8,),
        in_specs=[
            counts_spec(0),
            counts_spec(1),
            block,
            block,
            pl.BlockSpec(panel.shape, lambda g, rows, live: (0, 0, 0)),
        ],
        out_specs=out_specs,
    )
    flops = 4 * counts.shape[0] * across * width
    return pl.pallas_call(
        functools.partial(kernel, across // TILE),
        grid_spec=grid_spec,
        out_shape=out_shape,
        cost_estimate=pl.CostEstimate(
            flops=flops, bytes_accessed=4 * counts.size + 8 * own.size, transcendentals=0
        ),
        compiler_params=pltpu.CompilerParams(vmem_limit_bytes=48 * 2**20),
    )(rows_at, live, counts, counts, own, other, panel)


def exchange(blocks, axis):
    groups = CHIP_GROUPS if axis == "col" else None
    flat = blocks.reshape(-1, blocks.shape[-1])
    flat = lax.all_to_all(flat, axis, 0, 0, axis_index_groups=groups, tiled=True)
    return flat.reshape(blocks.shape)


def gather(block, axis):
    return exchange(jnp.broadcast_to(block[None], (8,) + block.shape), axis)


def split(value):
    high = lax.reduce_precision(value, exponent_bits=5, mantissa_bits=10)
    return [high.astype(WIRE), (value - high).astype(WIRE)]


def join(high, low):
    return high.astype(F32) + low.astype(F32)


def pack(blocks, extra):
    rows = jnp.stack(extra + [jnp.zeros_like(extra[0])] * (PAD - len(extra)))
    rows = jnp.broadcast_to(rows[None], (8,) + rows.shape)
    return jnp.concatenate([blocks.astype(WIRE), rows], axis=1)


def local(click_counts, tile_pattern, row_factors, column_factors):
    width = row_factors.shape[1]
    core = lax.axis_index("col") % 2
    steps = jnp.arange(8, dtype=jnp.int32)
    rows_at = jnp.stack([2 * steps + core, 2 * steps + 1 - core], axis=1).reshape(-1)
    live = tile_pattern.reshape(-1)

    with jax.named_scope("gather_in"):
        own = gather(row_factors, "col")
        other = lax.ppermute(own, "col", SWAP_CORE)
        panel = gather(column_factors, "row")
        column_total = jnp.sum(panel.astype(F32), axis=(0, 1))

    block = pl.BlockSpec((1, BLOCK, width), lambda g, rows, live: (g, 0, 0))
    keep, send = sweep(
        rows_kernel,
        rows_at,
        live,
        click_counts,
        own,
        other,
        panel,
        (
            jax.ShapeDtypeStruct((8, BLOCK, width), F32),
            jax.ShapeDtypeStruct((8, BLOCK, width), F32),
        ),
        (block, block),
    )
    with jax.named_scope("reduce_rows"):
        came = lax.ppermute(send, "col", SWAP_CORE)
        other_total = lax.ppermute(column_total, "col", SWAP_CORE)
        packed = pack((keep + came) * ROW_SCALE, split(column_total + other_total))
        came = exchange(packed, "col")
        share = jnp.sum(came[:, :BLOCK].astype(F32), axis=0) * (1 / ROW_SCALE)
        column_total = jnp.sum(join(came[:, BLOCK], came[:, BLOCK + 1]), axis=0)
        updated_rows = (row_factors.astype(F32) * share / column_total).astype(jnp.bfloat16)
    with jax.named_scope("gather_new"):
        own = gather(updated_rows, "col")
        other = lax.ppermute(own, "col", SWAP_CORE)
    sums, row_total = sweep(
        columns_kernel,
        rows_at,
        live,
        click_counts,
        own,
        other,
        panel,
        (
            jax.ShapeDtypeStruct((8, BLOCK, width), F32),
            jax.ShapeDtypeStruct((8, width), F32),
        ),
        (
            pl.BlockSpec((8, BLOCK, width), lambda g, rows, live: (0, 0, 0)),
            pl.BlockSpec((8, width), lambda g, rows, live: (0, 0)),
        ),
    )
    with jax.named_scope("reduce_columns"):
        row_total = jnp.sum(row_total, axis=0)
        fine = jnp.minimum(row_total * FINE_SCALE, FINE_LIMIT)
        packed = pack(sums * COLUMN_SCALE, split(row_total * COARSE_SCALE) + split(fine))
        came = exchange(packed, "row")
        share = jnp.sum(came[:, :BLOCK].astype(F32), axis=0) * (1 / COLUMN_SCALE)
        coarse = join(came[:, BLOCK], came[:, BLOCK + 1]) * (1 / COARSE_SCALE)
        fine = join(came[:, BLOCK + 2], came[:, BLOCK + 3])
        totals = jnp.where(fine < FINE_LIMIT, fine * (1 / FINE_SCALE), coarse)
        row_total = jnp.sum(totals, axis=0)
    updated_columns = (column_factors.astype(F32) * share / row_total).astype(jnp.bfloat16)
    return (updated_rows, updated_columns)


def solution(mesh):
    in_specs = (P("row", "col"), P("row", "col"), P(("row", "col"), None), P(("col", "row"), None))
    out_specs = (P(("row", "col"), None), P(("col", "row"), None))
    return jax.shard_map(local, mesh=mesh, in_specs=in_specs, out_specs=out_specs, check_vma=False)
```

time: 143 us -> 139 us (0.972)
  blocking collectives: 0 us -> 81.3 us
  waiting for transfers between devices: 69 us -> 23.1 us
  starting transfers between devices: 41.8 us -> 7.22 us
  other arithmetic: 4.49 us -> 2.89 us
    all_to_all x0 -> x4, blocking collectives: none -> 81.3 us  [exchange(): lax.all_to_all(flat, axis, 0, 0, axis_index_groups=groups, tiled=True)]
    ppermute x29 -> x1, waiting for transfers between devices: 62 us -> 3.15 us  [local(): other_total = lax.ppermute(column_total, 'col', SWAP_CORE)]
    ppermute x29 -> x1, starting transfers between devices: 41.5 us -> 0.58 us  [local(): other_total = lax.ppermute(column_total, 'col', SWAP_CORE)]
    all_to_all x0 -> x1, waiting for transfers between devices: none -> 17.1 us  [exchange(): lax.all_to_all(flat, axis, 0, 0, axis_index_groups=groups, tiled=True)]
    all_to_all x0 -> x1, starting transfers between devices: none -> 6.64 us  [exchange(): lax.all_to_all(flat, axis, 0, 0, axis_index_groups=groups, tiled=True)]
    ppermute x1, waiting for transfers between devices: 4.37 us -> 0.21 us  [local(): came = lax.ppermute(send, 'col', SWAP_CORE)]
    unnamed x18 -> x9, local copies, waits for them, and re-layouts: 2.73 us -> 0.1 us
    broadcast_in_dim x0 -> x5, local copies, waits for them, and re-layouts: none -> 2.21 us  [the longest x3 2.18 us: gather(): return exchange(jnp.broadcast_to(block[None], (8,) + block.shape), axis)]
  transfers between devices with their start and end apart: 32 -> 5, of which waited for: 21 -> 4; matrix products, arithmetic and copies ran while one was open for 5% -> 1% of each run, Pallas kernels for 0% -> 0%
where the time goes in v2:
time: 139 us; the launch traced here: 138 us
  blocking collectives  81.3 us (58%)
  waiting for transfers between devices  23.1 us (17%)
  Pallas kernels  20.3 us (15%)
  starting transfers between devices  7.22 us (5%)
  other arithmetic  2.89 us (2%)
  local copies, waits for them, and re-layouts  2.7 us (2%)
    all_to_all x4, blocking collectives, exchange(): lax.all_to_all(flat, axis, 0, 0, axis_index_groups=groups, tiled=True)  81.3 us
    pallas_call x2, Pallas kernels, sweep(): pl.pallas_call(functools.partial(kernel, across // TILE), grid_spec=grid_...  20.3 us
    all_to_all x1, waiting for transfers between devices, exchange(): lax.all_to_all(flat, axis, 0, 0, axis_index_groups=groups, tiled=True)  17.1 us
    all_to_all x1, starting transfers between devices, exchange(): lax.all_to_all(flat, axis, 0, 0, axis_index_groups=groups, tiled=True)  6.64 us
    ppermute x1, waiting for transfers between devices, local(): other_total = lax.ppermute(column_total, 'col', SWAP_CORE)  3.15 us
  transfers between devices with their start and end apart: 5, of which 4 were waited for; matrix products, arithmetic and copies ran while one was open for 1% of the time, Pallas kernels for 0%

profile of v2, /device:TPU:0, one launch (start us, length us, event | category | flops | bytes accessed | tf_op | source)
XLA Modules:
  0.0 138.3 jit_solution(2960964016948281127)
XLA Ops:
  0.6 0.0 copy-start.1
  0.6 1.0 broadcast_in_dim.10
  1.7 22.0 %all_to_all.30.a = bf16[8,128,512]{2,1,0:T(8,128)(2,1)S(1)} all-to-all(bf16[8,128,512]{2,1,0:T(8,128)(2,1)S(1)} %broadcast_in_dim.10), channel_id=1, replica_groups={{0,2,4,6,8,10,12,14},{1,3,5,7,9,11,13,15},{16,18,20,22,24,26,28,30},{17..., dimensions={0} | all-to-all | bytes 2097152 | tf_op jit(solution)/shard_map/gather_in/all_to_all | solution.py:109
  23.7 0.0 copy-start.3
  23.7 0.0 collective-permute-start
  23.7 0.0 copy-done.1
  23.7 1.1 broadcast_in_dim.11
  24.8 6.6 %all-to-all-start.1 = ((bf16[8,128,512]{2,1,0:T(8,128)(2,1)}), bf16[8,128,512]{2,1,0:T(8,128)(2,1)S(1)}, u32[]{:S(2)}, u32[]{:S(2)}) async-start(bf16[8,128,512]{2,1,0:T(8,128)(2,1)} %broadcast_in_dim.11), calls=%async_computation.1 | async-start | bytes 2097152 | tf_op jit(solution)/shard_map/gather_in/all_to_all | solution.py:109
  31.5 0.1 copy.8
  31.5 0.1 reshape.135.rows_ref
  31.6 0.0 copy-done.3
  31.6 0.1 copy.9
  31.7 0.1 reshape.136.live_ref
  31.8 17.1 %all-to-all-done.1.panel = bf16[8,128,512]{2,1,0:T(8,128)(2,1)S(1)} async-done(((bf16[8,128,512]{2,1,0:T(8,128)(2,1)}), bf16[8,128,512]{2,1,0:T(8,128)(2,1)S(1)}, u32[]{:S(2)}, u32[]{:S(2)}) %all-to-all-start.1) | async-done | bytes 1048608 | tf_op jit(solution)/shard_map/gather_in/all_to_all | solution.py:109
  48.9 0.0 collective-permute-done.b
  48.9 10.4 %shard_map.59 = (f32[8,128,512]{2,1,0:T(8,128)S(1)}, f32[8,128,512]{2,1,0:T(8,128)}) custom-call(s32[16]{0:T(128)S(1)} %reshape.135.rows_ref, s32[32]{0:T(128)S(1)} %reshape.136.live_ref, s32[2048,1024]{1,0:T(8,128)} %c1.3, s32[2048,1024]{1,0:T(8,128)} %c1.3, bf16[8,128,512]{2,1,0:T(8,128)(2,1)S(1)} %all_to_all.30.a, ...), custom_call_target="tpu_custom_call" | custom-call | flops 4294967296 | bytes 12582912 | tf_op jit(solution)/shard_map/pallas_call | solution.py:95
  59.3 0.0 collective-permute-start.1
  59.3 0.2 convert_reduce_fusion.2
  59.5 0.6 collective-permute-start.2
  60.1 0.1 pad.6.clone
  60.1 3.2 %collective-permute-done.2 = f32[512]{0:T(512)S(1)} collective-permute-done((f32[512]{0:T(512)S(1)}, f32[512]{0:T(512)S(1)}, u32[]{:S(2)}, u32[]{:S(2)}) %collective-permute-start.2) | collective-permute-done | bytes 2080 | tf_op jit(solution)/shard_map/reduce_rows/ppermute | solution.py:162
  63.3 0.1 pad_maximum_fusion.2
  63.4 0.2 collective-permute-done.1
  63.6 0.5 multiply_convert_fusion.1
  64.2 0.3 pad_maximum_fusion
  64.5 0.0 copy-start
  64.5 19.6 %all_to_all.31 = f16[8,136,512]{2,1,0:T(8,128)(2,1)S(1)} all-to-all(f16[8,136,512]{2,1,0:T(8,128)(2,1)S(1)} %pad_maximum_fusion), channel_id=1, replica_groups={{0,2,4,6,8,10,12,14},{1,3,5,7,9,11,13,15},{16,18,20,22,24,26,28,30},{17..., dimensions={0} | all-to-all | bytes 2228224 | tf_op jit(solution)/shard_map/reduce_rows/all_to_all | solution.py:109
  84.1 0.1 convert_reduce_fusion.1
  84.3 0.0 copy-done
  84.4 0.0 copy-start.2
  84.4 0.1 broadcast_in_dim.13
  84.5 17.9 %all_to_all.32.a = bf16[8,128,512]{2,1,0:T(8,128)(2,1)S(1)} all-to-all(bf16[8,128,512]{2,1,0:T(8,128)(2,1)S(1)} %broadcast_in_dim.13), channel_id=1, replica_groups={{0,2,4,6,8,10,12,14},{1,3,5,7,9,11,13,15},{16,18,20,22,24,26,28,30},{17..., dimensions={0} | all-to-all | bytes 2097152 | tf_op jit(solution)/shard_map/gather_new/all_to_all | solution.py:109
  102.3 0.0 collective-permute-start.3
  102.3 2.7 %collective-permute-done.3.b = bf16[8,128,512]{2,1,0:T(8,128)(2,1)S(1)} collective-permute-done((bf16[8,128,512]{2,1,0:T(8,128)(2,1)S(1)}, bf16[8,128,512]{2,1,0:T(8,128)(2,1)S(1)}, u32[]{:S(2)}, u32[]{:S(2)}) %collective-permute-start.3) | collective-permute-done | bytes 1048608 | tf_op jit(solution)/shard_map/gather_new/ppermute | solution.py:170
  105.0 9.9 %shard_map.60 = (f32[8,128,512]{2,1,0:T(8,128)S(1)}, f32[8,512]{1,0:T(8,128)S(1)}) custom-call(s32[16]{0:T(128)S(1)} %reshape.135.rows_ref, s32[32]{0:T(128)S(1)} %reshape.136.live_ref, s32[2048,1024]{1,0:T(8,128)} %c1.3, s32[2048,1024]{1,0:T(8,128)} %c1.3, bf16[8,128,512]{2,1,0:T(8,128)(2,1)S(1)} %all_to_all.32.a, ...), custom_call_target="tpu_custom_call" | custom-call | flops 4294967296 | bytes 12582912 | tf_op jit(solution)/shard_map/pallas_call | solution.py:95
  114.9 0.0 copy-done.2
  114.9 0.3 multiply_convert_fusion
  115.3 0.3 pad_maximum_fusion.1
  115.6 21.7 %all_to_all.33 = f16[8,136,512]{2,1,0:T(8,128)(2,1)S(1)} all-to-all(f16[8,136,512]{2,1,0:T(8,128)(2,1)S(1)} %pad_maximum_fusion.1), channel_id=1, replica_groups=mesh['row'=8,'col'=16] {'row'}, dimensions={0} | all-to-all | bytes 2228224 | tf_op jit(solution)/shard_map/reduce_columns/all_to_all | solution.py:109
  137.3 0.1 convert_reduce_fusion
  137.5 0.1 fusion.5
  137.6 0.7 divide_convert_fusion
  (16 shorter events, 0.3 us)
Async XLA Ops:
  0.6 23.1 %copy-start.1 = (bf16[128,512]{1,0:T(8,128)(2,1)S(1)}, bf16[128,512]{1,0:T(8,128)(2,1)}, u32[]{:S(2)}) copy-start(bf16[128,512]{1,0:T(8,128)(2,1)} %param.7) | copy-start | bytes 393220
  23.7 7.9 %copy-start.3 = (s32[8,4]{0,1:T(4,128)S(1)}, s32[8,4]{0,1:T(4,128)}, u32[]{:S(2)}) copy-start(s32[8,4]{0,1:T(4,128)} %param.5) | copy-start | bytes 388
  23.7 25.1 %collective-permute-start = (bf16[8,128,512]{2,1,0:T(8,128)(2,1)S(1)}, bf16[8,128,512]{2,1,0:T(8,128)(2,1)S(1)}, u32[]{:S(2)}, u32[]{:S(2)}) collective-permute-start(bf16[8,128,512]{2,1,0:T(8,128)(2,1)S(1)} %all_to_all.30.a), channel_id=1, source_target_pairs={{0,1},{1,0},{2,3},{3,2},{4,5},{5,4},{6,7},{7,6},{8,9},{9,8},{10,11... | collective-permute-start | bytes 3145736 | tf_op jit(solution)/shard_map/gather_in/ppermute | solution.py:141
  24.8 24.1 %all-to-all-start.1 = ((bf16[8,128,512]{2,1,0:T(8,128)(2,1)}), bf16[8,128,512]{2,1,0:T(8,128)(2,1)S(1)}, u32[]{:S(2)}, u32[]{:S(2)}) async-start(bf16[8,128,512]{2,1,0:T(8,128)(2,1)} %broadcast_in_dim.11), calls=%async_computation.1 | async-start | bytes 2097152 | tf_op jit(solution)/shard_map/gather_in/all_to_all | solution.py:109
  59.3 4.4 %collective-permute-start.1 = (f32[8,128,512]{2,1,0:T(8,128)}, f32[8,128,512]{2,1,0:T(8,128)S(1)}, u32[]{:S(2)}, u32[]{:S(2)}) collective-permute-start(f32[8,128,512]{2,1,0:T(8,128)} %get-tuple-element.7), channel_id=1, source_target_pairs={{0,1},{1,0},{2,3},{3,2},{4,5},{5,4},{6,7},{7,6},{8,9},{9,8},{10,11... | collective-permute-start | bytes 6291464 | tf_op jit(solution)/shard_map/reduce_rows/ppermute | solution.py:161
  59.5 3.8 %collective-permute-start.2 = (f32[512]{0:T(512)S(1)}, f32[512]{0:T(512)S(1)}, u32[]{:S(2)}, u32[]{:S(2)}) collective-permute-start(f32[512]{0:T(512)S(1)} %convert_reduce_fusion.2), channel_id=1, source_target_pairs={{0,1},{1,0},{2,3},{3,2},{4,5},{5,4},{6,7},{7,6},{8,9},{9,8},{10,11... | collective-permute-start | bytes 6152 | tf_op jit(solution)/shard_map/reduce_rows/ppermute | solution.py:162
  64.5 19.8 %copy-start = (bf16[128,512]{1,0:T(8,128)(2,1)S(1)}, bf16[128,512]{1,0:T(8,128)(2,1)}, u32[]{:S(2)}) copy-start(bf16[128,512]{1,0:T(8,128)(2,1)} %param.6) | copy-start | bytes 393220
  84.4 30.6 %copy-start.2 = (bf16[128,512]{1,0:T(8,128)(2,1)}, bf16[128,512]{1,0:T(8,128)(2,1)S(1)}, u32[]{:S(2)}) copy-start(bf16[128,512]{1,0:T(8,128)(2,1)S(1)} %divide_convert_fusion.1) | copy-start | bytes 393220
  102.3 2.7 %collective-permute-start.3 = (bf16[8,128,512]{2,1,0:T(8,128)(2,1)S(1)}, bf16[8,128,512]{2,1,0:T(8,128)(2,1)S(1)}, u32[]{:S(2)}, u32[]{:S(2)}) collective-permute-start(bf16[8,128,512]{2,1,0:T(8,128)(2,1)S(1)} %all_to_all.32.a), channel_id=1, source_target_pairs={{0,1},{1,0},{2,3},{3,2},{4,5},{5,4},{6,7},{7,6},{8,9},{9,8},{10,11... | collective-permute-start | bytes 3145736 | tf_op jit(solution)/shard_map/gather_new/ppermute | solution.py:170

commit v3 on v0

v3 whole, which is shorter than its diff:
```python
import functools

import jax
import jax.numpy as jnp
from jax import lax
from jax.experimental import pallas as pl
from jax.experimental.pallas import tpu as pltpu
from jax.sharding import PartitionSpec as P

WIRE = jnp.float16
ROW_SCALE = 2.0**-6
COLUMN_SCALE = 2.0**-9
COLUMN_STEPS = ((2.0**5, 1.0),)
ROW_STEPS = (
    (2.0**12, 2.0**-8),
    (2.0**4, 1.0),
    (2.0**-4, 2.0**8),
    (2.0**-12, 2.0**16),
    (2.0**-20, 2.0**24),
)
TINY = 1e-30
BLOCK = 128
TILE = 256
PAD = 8
F32 = jnp.float32
BF16 = jnp.bfloat16


def along_z(step):
    return [(j, (j // 4 + step) % 4 * 4 + j % 4) for j in range(16)]


def along_x(step):
    return [(i, (i // 2 + step) % 4 * 2 + i % 2) for i in range(8)]


def to_col(dz, dl):
    return [(j, (j // 4 + dz) % 4 * 4 + (j ^ (2 * dl)) % 4) for j in range(16)]


def to_row(dx, dh):
    return [(i, (i // 2 + dx) % 4 * 2 + (i ^ dh) % 2) for i in range(8)]


SWAP_CORE = [(j, j ^ 1) for j in range(16)]


AWAY = [(2, 1), (2, 0), (1, 1), (3, 1), (1, 0), (3, 0), (0, 1)]


def swap_core(value):
    return lax.ppermute(value, "col", SWAP_CORE)


def contract_last(a, b):
    return lax.dot_general(a, b, (((1,), (1,)), ((), ())), preferred_element_type=F32)


def contract_first(a, b):
    return lax.dot_general(a, b, (((0,), (0,)), ((), ())), preferred_element_type=F32)


def stage_kernel(tiles_across, rows_ref, live_ref, place_ref, counts, staged):
    step = pl.program_id(0)
    row_tile = rows_ref[step] // 2
    for k in range(2 * tiles_across):
        place = place_ref[k]
        start = pl.multiple_of(place * BLOCK, BLOCK)
        live = live_ref[row_tile * tiles_across + place // 2] > 0
        value = counts[:, pl.ds(start, BLOCK)].astype(F32)
        staged[0, :, k * BLOCK : (k + 1) * BLOCK] = jnp.where(live, value, 0.0)


def stage_counts(rows_at, live, columns_at, counts):
    across = counts.shape[1]
    grid_spec = pltpu.PrefetchScalarGridSpec(
        num_scalar_prefetch=3,
        grid=(16,),
        in_specs=[pl.BlockSpec((BLOCK, across), lambda g, rows, live, place: (rows[g], 0))],
        out_specs=pl.BlockSpec((1, BLOCK, across), lambda g, rows, live, place: (g, 0, 0)),
    )
    return pl.pallas_call(
        functools.partial(stage_kernel, across // TILE),
        grid_spec=grid_spec,
        out_shape=jax.ShapeDtypeStruct((16, BLOCK, across), F32),
        cost_estimate=pl.CostEstimate(
            flops=counts.size, bytes_accessed=8 * counts.size, transcendentals=0
        ),
        compiler_params=pltpu.CompilerParams(vmem_limit_bytes=8 * 2**20),
    )(rows_at, live, columns_at, counts)


def ratios_of(counts, left, columns):
    predicted = contract_last(left, columns)
    return (counts / jnp.maximum(predicted, TINY)).astype(BF16)


def total_rows(total, steps, last_scale):
    rows = []
    for unit, scale in steps:
        shift = 1.5 * 2.0**23 * unit
        part = (total + shift) - shift
        rows.append(part * scale)
        total = total - part
    rows.append(total * last_scale)
    rows += [jnp.zeros_like(total)] * (PAD - len(rows))
    return jnp.concatenate(rows, axis=0)


def join_total(rows, steps, last_scale, scale):
    scales = [s for _, s in steps] + [last_scale]
    return sum(rows[k].astype(F32) * (1 / (s * scale)) for k, s in enumerate(scales))


def rows_kernel(first, counts, a0, a1, b0, b1, panel, *refs):
    keep, send = refs[-2:]
    columns = panel[...].reshape(-1, panel.shape[-1])
    for e, (a, b) in enumerate(((a0, b0), (a1, b1))):
        left = jnp.concatenate([a[...], b[...]], axis=0)
        block = counts[first + 2 * e : first + 2 * e + 2].reshape(TILE, -1)
        total = jnp.dot(ratios_of(block, left, columns), columns, preferred_element_type=F32)
        keep[e, :BLOCK] = total[:BLOCK]
        send[e, :BLOCK] = total[BLOCK:]
    total = jnp.sum(columns.astype(F32), axis=0, keepdims=True)
    rows = total_rows(total, COLUMN_STEPS, 1.0)
    for e in range(2):
        keep[e, BLOCK:] = rows
        send[e, BLOCK:] = rows


def columns_kernel(at, first, last, counts, a0, a1, b0, b1, panel, *refs):
    if first:
        sums, rows_total = refs
    else:
        sums_in, total_in, sums, rows_total = refs
    columns = panel[...].reshape(-1, panel.shape[-1])
    left = jnp.concatenate([a0[...], b0[...], a1[...], b1[...]], axis=0)
    total = jnp.sum(left.astype(F32).reshape(-1, 8, left.shape[-1]), axis=0)
    if not first:
        total = total + total_in[...]
    rows_total[...] = total
    ratios = []
    for e in range(2):
        block = counts[at[e] : at[e] + 2].reshape(TILE, -1)
        ratios.append(ratios_of(block, left[e * TILE : (e + 1) * TILE], columns))
    ratios = jnp.concatenate(ratios, axis=0)
    for j in range(4):
        term = contract_first(ratios[:, j * TILE : (j + 1) * TILE], left)
        for k in range(2):
            part = term[k * BLOCK : (k + 1) * BLOCK]
            sums[2 * j + k, :BLOCK] = part if first else part + sums_in[2 * j + k, :BLOCK]
    if last:
        total = jnp.sum(total, axis=0, keepdims=True)
        rows = total_rows(total, ROW_STEPS, 2.0**24)
        for k in range(8):
            sums[k, BLOCK:] = rows * (1 / COLUMN_SCALE)


def call(kernel, operands, out_shape, aliases, after=()):
    vmem = pl.BlockSpec(memory_space=pltpu.VMEM)
    return pl.pallas_call(
        kernel,
        in_specs=[vmem] * len(operands) + [pl.BlockSpec(memory_space=pl.ANY)] * len(after),
        out_specs=(vmem,) * len(out_shape),
        out_shape=out_shape,
        input_output_aliases=aliases,
        cost_estimate=pl.CostEstimate(flops=2**20, bytes_accessed=2**16, transcendentals=0),
        compiler_params=pltpu.CompilerParams(vmem_limit_bytes=24 * 2**20),
    )(*operands, *after)


def after(value, other):
    return lax.optimization_barrier((value, other))[0]


def local(click_counts, tile_pattern, row_factors, column_factors):
    width = row_factors.shape[1]
    at_row, at_col = lax.axis_index("row"), lax.axis_index("col")
    z, pair, core = at_col // 4, at_col // 2 % 2, at_col % 2
    x, far = at_row // 2, at_row % 2
    rows_at = jnp.stack(
        [
            (z + dz) % 4 * 4 + (pair + dl) % 2 * 2 + (core + dc) % 2
            for dz in range(4)
            for dl in range(2)
            for dc in range(2)
        ]
    ).astype(jnp.int32)
    columns_at = jnp.stack(
        [(x + dx) % 4 * 2 + (far + dh) % 2 for dx in range(4) for dh in range(2)]
    ).astype(jnp.int32)
    live = tile_pattern.reshape(-1)

    counts = stage_counts(rows_at, live, columns_at, click_counts)
    with jax.named_scope("gather_in"):
        column_pair = jnp.stack([column_factors, lax.ppermute(column_factors, "row", to_row(0, 1))])
        row_pair = jnp.stack([row_factors, lax.ppermute(row_factors, "col", to_col(0, 1))])
        row_pair = after(row_pair, counts)
        own, panel = {0: row_pair}, {0: column_pair}
        for d in (2, 1, 3):
            panel[d] = lax.ppermute(column_pair, "row", along_x(-d))
            own[d] = lax.ppermute(row_pair, "col", along_z(-d))
        other = {d: swap_core(own[d]) for d in range(4)}
        panel = jnp.concatenate([panel[d] for d in range(4)])
    with jax.named_scope("reduce_rows"):
        piece = jax.ShapeDtypeStruct((2, BLOCK + PAD, width), F32)
        came, arrived, waits = {}, [], ()
        for d in (2, 1, 3, 0):
            a, b = own[d], other[d]
            keep, send = call(
                functools.partial(rows_kernel, 4 * d),
                (counts, a[0], a[1], b[0], b[1], panel),
                (piece, piece),
                {},
                waits,
            )
            came[d] = swap_core(send)
            partial = (keep + came[d]) * ROW_SCALE
            for e in (1, 0):
                if d or e:
                    arrived.append(lax.ppermute(partial[e].astype(WIRE), "col", to_col(d, e)))
            waits = {2: (keep,), 1: (came.get(2),), 3: (came.get(1),)}.get(d)
        partial = partial[0]
        for a in arrived:
            partial = partial + a.astype(F32)
        share = partial[:BLOCK] * (1 / ROW_SCALE)
        column_total = join_total(partial[BLOCK:], COLUMN_STEPS, 1.0, ROW_SCALE)
        updated_rows = (row_factors.astype(F32) * share / column_total).astype(BF16)
    with jax.named_scope("gather_new"):
        own = {(0, 0): updated_rows}
        for d, e in AWAY:
            own[d, e] = lax.ppermute(updated_rows, "col", to_col(-d, e))
        out_shape = (
            jax.ShapeDtypeStruct((8, BLOCK + PAD, width), F32),
            jax.ShapeDtypeStruct((8, width), F32),
        )
        steps = [((0, 0), AWAY[0]), AWAY[1:3], AWAY[3:5], AWAY[5:7]]
        other, history = {}, []
        for i, step in enumerate(steps):
            for k in step:
                ready = after(own[k], history[i - 2][0]) if i > 1 else own[k]
                other[k] = swap_core(ready)
            blocks = [own[k] for k in step] + [other[k] for k in step]
            sums = call(
                functools.partial(
                    columns_kernel, tuple(4 * d + 2 * e for d, e in step), i == 0, i == 3
                ),
                [counts] + blocks + [panel] + (list(history[-1]) if i else []),
                out_shape,
                {6: 0, 7: 1} if i else {},
            )
            history.append(sums)
        sums = sums[0]
    with jax.named_scope("reduce_columns"):
        partial = sums[0] * COLUMN_SCALE
        for d, e in AWAY:
            a = (sums[2 * d + e] * COLUMN_SCALE).astype(WIRE)
            partial = partial + lax.ppermute(a, "row", to_row(d, e)).astype(F32)
        share = partial[:BLOCK] * (1 / COLUMN_SCALE)
        row_total = join_total(partial[BLOCK:], ROW_STEPS, 2.0**24, 1.0)
        updated_columns = (column_factors.astype(F32) * share / row_total).astype(BF16)
    return (updated_rows, updated_columns)


def solution(mesh):
    in_specs = (P("row", "col"), P("row", "col"), P(("row", "col"), None), P(("col", "row"), None))
    out_specs = (P(("row", "col"), None), P(("col", "row"), None))
    return jax.shard_map(local, mesh=mesh, in_specs=in_specs, out_specs=out_specs, check_vma=False)
```

time: 641 us -> 110 us (0.17)
  blocking collectives: 393 us -> 0 us
  waiting for transfers between devices: 129 us -> 31.8 us
  starting transfers between devices: 0.2 us -> 55.8 us
  loops' own time: 51.3 us -> 0 us
  matrix products: 33.4 us -> 0 us
  between operations: 14.5 us -> 1.28 us
  Pallas kernels: 0 us -> 12.8 us
    psum x2 -> x0, blocking collectives: 393 us -> none  [the longest x1 206 us: local(): lax.psum(jnp.sum(column_factors.astype(jnp.float32), axis=0), ('row', 'co...]
    all_gather x3 -> x0, waiting for transfers between devices: 115 us -> none  [the longest x1 46.9 us: local(): column_panel = lax.all_gather(column_factors, 'row', axis=0, tiled=True)]
    ppermute x0 -> x45, starting transfers between devices: none -> 55.8 us  [the longest x7 14.8 us: local(): partial = partial + lax.ppermute(a, 'row', to_row(d, e)).astype(F32)]
    another operation x2 -> x0, loops' own time: 51.3 us -> none  [sweep(): return lax.fori_loop(0, group_count, visit, initial)]
    dot_general x16 -> x0, matrix products: 33.4 us -> none  [the longest x8 19.6 us: add_rows(): term = jnp.dot(ratios, right_tile, preferred_element_type=jnp.float32)]
    ppermute x0 -> x45, waiting for transfers between devices: none -> 31.8 us  [the longest x3 10.5 us: local(): own[d] = lax.ppermute(row_pair, 'col', along_z(-d))]
    reduce_scatter x2 -> x0, waiting for transfers between devices: 13.1 us -> none  [the longest x1 8.62 us: local(): lax.psum_scatter(column_sums, 'row', scatter_dimension=0, tiled=True)]
    pallas_call x0 -> x9, Pallas kernels: none -> 12.8 us  [the longest x8 10.6 us: call(): pl.pallas_call(kernel, in_specs=[vmem] * len(operands) + [pl.BlockSpec(me...]
  transfers between devices with their start and end apart: 5 -> 45, of which waited for: 5 -> 16; matrix products, arithmetic and copies ran while one was open for 1% -> 3% of each run, Pallas kernels for 0% -> 10%
where the time goes in v3:
time: 110 us; the launch traced here: 109 us
  starting transfers between devices  55.8 us (51%)
  waiting for transfers between devices  31.8 us (29%)
  Pallas kernels  12.8 us (12%)
  local copies, waits for them, and re-layouts  5.72 us (5%)
  other arithmetic  1.96 us (2%)
  between operations  1.28 us (1%)
    ppermute x7, starting transfers between devices, local(): partial = partial + lax.ppermute(a, 'row', to_row(d, e)).astype(F32)  14.8 us
    pallas_call x8, Pallas kernels, call(): pl.pallas_call(kernel, in_specs=[vmem] * len(operands) + [pl.BlockSpec(me...  10.6 us
    ppermute x3, waiting for transfers between devices, local(): own[d] = lax.ppermute(row_pair, 'col', along_z(-d))  10.5 us
    ppermute x7, starting transfers between devices, local(): own[d, e] = lax.ppermute(updated_rows, 'col', to_col(-d, e))  10.3 us
    ppermute x7, starting transfers between devices, local(): arrived.append(lax.ppermute(partial[e].astype(WIRE), 'col', to_col(d, e)))  9.75 us
    ppermute x3, starting transfers between devices, local(): own[d] = lax.ppermute(row_pair, 'col', along_z(-d))  8.59 us
    ppermute x7, waiting for transfers between devices, local(): arrived.append(lax.ppermute(partial[e].astype(WIRE), 'col', to_col(d, e)))  7.57 us
    ppermute x7, waiting for transfers between devices, local(): own[d, e] = lax.ppermute(updated_rows, 'col', to_col(-d, e))  6.97 us
  transfers between devices with their start and end apart: 45, of which 16 were waited for; matrix products, arithmetic and copies ran while one was open for 3% of the time, Pallas kernels for 10%

profile of v3, /device:TPU:0, one launch (start us, length us, event | category | flops | bytes accessed | tf_op | source)
XLA Modules:
  0.0 109.3 jit_solution(11480838528920096181)
XLA Ops:
  0.6 1.7 %collective-permute-start = (bf16[128,512]{1,0:T(8,128)(2,1)}, bf16[128,512]{1,0:T(8,128)(2,1)S(1)}, u32[]{:S(2)}, u32[]{:S(2)}) collective-permute-start(bf16[128,512]{1,0:T(8,128)(2,1)} %param.6), channel_id=1, source_target_pairs={{0,2},{1,3},{2,0},{3,1},{4,6},{5,7},{6,4},{7,5},{8,10},{9,11},{10,... | collective-permute-start | bytes 393224 | tf_op jit(solution)/shard_map/gather_in/ppermute | solution.py:197
  2.4 2.9 %collective-permute-start.2 = (bf16[128,512]{1,0:T(8,128)(2,1)}, bf16[128,512]{1,0:T(8,128)(2,1)S(1)}, u32[]{:S(2)}, u32[]{:S(2)}) collective-permute-start(bf16[128,512]{1,0:T(8,128)(2,1)} %param.7), channel_id=1, source_target_pairs={{0,16},{16,0},{32,48},{48,32},{64,80},{80,64},{96,112},{112,96},{1... | collective-permute-start | bytes 393224 | tf_op jit(solution)/shard_map/gather_in/ppermute | solution.py:196
  5.3 0.9 constant_dynamic-update-slice_fusion.4
  6.5 0.8 copy.13
  7.5 3.4 %copy-done = s32[2048,1024]{1,0:T(8,128)S(1)} copy-done((s32[2048,1024]{1,0:T(8,128)S(1)}, s32[2048,1024]{1,0:T(8,128)}, u32[]{:S(2)}) %copy-start) | copy-done | bytes 8388632
  10.9 2.1 %shard_map.59.counts = f32[16,128,1024]{2,1,0:T(8,128)S(1)} custom-call(s32[16]{0:T(128)S(1)} %stack.112.rows_ref, s32[32]{0:T(128)S(1)} %reshape.37.live_ref, s32[8]{0:T(128)S(1)} %stack.121.place_ref, s32[2048,1024]{1,0:T(8,128)S(1)} %copy-done), custom_call_target="tpu_custom_call" | custom-call | flops 2097152 | bytes 16777216 | tf_op jit(solution)/shard_map/pallas_call | solution.py:82
  13.1 2.8 %collective-permute-start.3 = (bf16[2,128,512]{2,1,0:T(8,128)(2,1)S(1)}, bf16[2,128,512]{2,1,0:T(8,128)(2,1)S(1)}, u32[]{:S(2)}, u32[]{:S(2)}) collective-permute-start(bf16[2,128,512]{2,1,0:T(8,128)(2,1)S(1)} %pad_maximum_fusion.1), channel_id=1, source_target_pairs={{0,96},{16,112},{32,0},{48,16},{64,32},{80,48},{96,64},{112,80},{1... | collective-permute-start | bytes 786440 | tf_op jit(solution)/shard_map/gather_in/ppermute | solution.py:201
  15.8 0.8 collective-permute-start.4
  16.6 0.9 collective-permute-start.5
  17.6 4.0 %collective-permute-start.8 = (bf16[2,128,512]{2,1,0:T(8,128)(2,1)S(1)}, bf16[2,128,512]{2,1,0:T(8,128)(2,1)S(1)}, u32[]{:S(2)}, u32[]{:S(2)}) collective-permute-start(bf16[2,128,512]{2,1,0:T(8,128)(2,1)S(1)} %pad_maximum_fusion), channel_id=1, source_target_pairs={{0,8},{1,9},{2,10},{3,11},{4,12},{5,13},{6,14},{7,15},{8,0},{9,1},... | collective-permute-start | bytes 786440 | tf_op jit(solution)/shard_map/gather_in/ppermute | solution.py:202
  22.3 4.2 %collective-permute-done.8 = bf16[2,128,512]{2,1,0:T(8,128)(2,1)S(1)} collective-permute-done((bf16[2,128,512]{2,1,0:T(8,128)(2,1)S(1)}, bf16[2,128,512]{2,1,0:T(8,128)(2,1)S(1)}, u32[]{:S(2)}, u32[]{:S(2)}) %collective-permute-start.8) | collective-permute-done | bytes 262176 | tf_op jit(solution)/shard_map/gather_in/ppermute | solution.py:202
  26.4 3.9 %collective-permute-start.17 = (bf16[2,128,512]{2,1,0:T(8,128)(2,1)S(1)}, bf16[2,128,512]{2,1,0:T(8,128)(2,1)S(1)}, u32[]{:S(2)}, u32[]{:S(2)}) collective-permute-start(bf16[2,128,512]{2,1,0:T(8,128)(2,1)S(1)} %pad_maximum_fusion), channel_id=1, source_target_pairs={{0,4},{1,5},{2,6},{3,7},{4,8},{5,9},{6,10},{7,11},{8,12},{9,13},{1... | collective-permute-start | bytes 786440 | tf_op jit(solution)/shard_map/gather_in/ppermute | solution.py:202
  30.4 2.4 %collective-permute-done.6 = bf16[2,128,512]{2,1,0:T(8,128)(2,1)S(1)} collective-permute-done((bf16[2,128,512]{2,1,0:T(8,128)(2,1)S(1)}, bf16[2,128,512]{2,1,0:T(8,128)(2,1)S(1)}, u32[]{:S(2)}, u32[]{:S(2)}) %collective-permute-start.6) | collective-permute-done | bytes 262176 | tf_op jit(solution)/shard_map/gather_in/ppermute | solution.py:202
  32.8 3.9 %collective-permute-done.17 = bf16[2,128,512]{2,1,0:T(8,128)(2,1)S(1)} collective-permute-done((bf16[2,128,512]{2,1,0:T(8,128)(2,1)S(1)}, bf16[2,128,512]{2,1,0:T(8,128)(2,1)S(1)}, u32[]{:S(2)}, u32[]{:S(2)}) %collective-permute-start.17) | collective-permute-done | bytes 262176 | tf_op jit(solution)/shard_map/gather_in/ppermute | solution.py:202
  38.3 1.3 %reduce_rows.4 = (f32[2,136,512]{2,1,0:T(8,128)S(1)}, f32[2,136,512]{2,1,0:T(8,128)S(1)}) custom-call(f32[16,128,1024]{2,1,0:T(8,128)S(1)} %shard_map.59.counts, bf16[128,512]{1,0:T(8,128)(2,1)S(1)} %get-tuple-element.62.a0, bf16[128,512]{1,0:T(8,128)(2,1)S(1)} %get-tuple-element.61.a1, bf16[128,512]{1,0:T(8,128)(2,1)S(1)} %get-tuple-element.60.b0, ...), custom_call_target="tpu_custom_call" | custom-call | flops 1048576 | bytes 65536 | tf_op jit(solution)/shard_map/reduce_rows/pallas_call | solution.py:161
  39.9 1.3 %reduce_rows.5 = (f32[2,136,512]{2,1,0:T(8,128)S(1)}, f32[2,136,512]{2,1,0:T(8,128)S(1)}) custom-call(f32[16,128,1024]{2,1,0:T(8,128)S(1)} %shard_map.59.counts, bf16[128,512]{1,0:T(8,128)(2,1)S(1)} %get-tuple-element.66.a0, bf16[128,512]{1,0:T(8,128)(2,1)S(1)} %get-tuple-element.65.a1, bf16[128,512]{1,0:T(8,128)(2,1)S(1)} %get-tuple-element.64.b0, ...), custom_call_target="tpu_custom_call" | custom-call | flops 1048576 | bytes 65536 | tf_op jit(solution)/shard_map/reduce_rows/pallas_call | solution.py:161
  41.7 1.3 %reduce_rows.7 = (f32[2,136,512]{2,1,0:T(8,128)S(1)}, f32[2,136,512]{2,1,0:T(8,128)S(1)}) custom-call(f32[16,128,1024]{2,1,0:T(8,128)S(1)} %shard_map.59.counts, bf16[128,512]{1,0:T(8,128)(2,1)S(1)} %get-tuple-element.58.a0, bf16[128,512]{1,0:T(8,128)(2,1)S(1)} %get-tuple-element.57.a1, bf16[128,512]{1,0:T(8,128)(2,1)S(1)} %get-tuple-element.56.b0, ...), custom_call_target="tpu_custom_call" | custom-call | flops 1048576 | bytes 65536 | tf_op jit(solution)/shard_map/reduce_rows/pallas_call | solution.py:161
  44.1 2.5 %collective-permute-start.14 = (f16[136,512]{1,0:T(8,128)(2,1)S(1)}, f16[136,512]{1,0:T(8,128)(2,1)S(1)}, u32[]{:S(2)}, u32[]{:S(2)}) collective-permute-start(f16[136,512]{1,0:T(8,128)(2,1)S(1)} %get-tuple-element.50), channel_id=1, source_target_pairs={{0,8},{1,9},{2,10},{3,11},{4,12},{5,13},{6,14},{7,15},{8,0},{9,1},... | collective-permute-start | bytes 417800 | tf_op jit(solution)/shard_map/reduce_rows/ppermute | solution.py:221
  46.6 1.3 %reduce_rows.6 = (f32[2,136,512]{2,1,0:T(8,128)S(1)}, f32[2,136,512]{2,1,0:T(8,128)S(1)}) custom-call(f32[16,128,1024]{2,1,0:T(8,128)S(1)} %shard_map.59.counts, bf16[128,512]{1,0:T(8,128)(2,1)S(1)} %get-tuple-element.70.a0, bf16[128,512]{1,0:T(8,128)(2,1)S(1)} %get-tuple-element.69.a1, bf16[128,512]{1,0:T(8,128)(2,1)S(1)} %get-tuple-element.68.b0, ...), custom_call_target="tpu_custom_call" | custom-call | flops 1048576 | bytes 65536 | tf_op jit(solution)/shard_map/reduce_rows/pallas_call | solution.py:161
  48.2 1.3 %collective-permute-start.15 = (f16[136,512]{1,0:T(8,128)(2,1)S(1)}, f16[136,512]{1,0:T(8,128)(2,1)S(1)}, u32[]{:S(2)}, u32[]{:S(2)}) collective-permute-start(f16[136,512]{1,0:T(8,128)(2,1)S(1)} %get-tuple-element.51), channel_id=1, source_target_pairs={{0,6},{1,7},{2,4},{3,5},{4,10},{5,11},{6,8},{7,9},{8,14},{9,15},{1... | collective-permute-start | bytes 417800 | tf_op jit(solution)/shard_map/reduce_rows/ppermute | solution.py:221
  49.5 1.0 collective-permute-start.16
  50.7 2.6 %collective-permute-start.20 = (f16[136,512]{1,0:T(8,128)(2,1)S(1)}, f16[136,512]{1,0:T(8,128)(2,1)S(1)}, u32[]{:S(2)}, u32[]{:S(2)}) collective-permute-start(f16[136,512]{1,0:T(8,128)(2,1)S(1)} %get-tuple-element.53), channel_id=1, source_target_pairs={{0,14},{1,15},{2,12},{3,13},{4,2},{5,3},{6,0},{7,1},{8,6},{9,7},{1... | collective-permute-start | bytes 417800 | tf_op jit(solution)/shard_map/reduce_rows/ppermute | solution.py:221
  53.5 1.6 %collective-permute-start.21 = (f16[136,512]{1,0:T(8,128)(2,1)S(1)}, f16[136,512]{1,0:T(8,128)(2,1)S(1)}, u32[]{:S(2)}, u32[]{:S(2)}) collective-permute-start(f16[136,512]{1,0:T(8,128)(2,1)S(1)} %get-tuple-element.54), channel_id=1, source_target_pairs={{0,12},{1,13},{2,14},{3,15},{4,0},{5,1},{6,2},{7,3},{8,4},{9,5},{1... | collective-permute-start | bytes 417800 | tf_op jit(solution)/shard_map/reduce_rows/ppermute | solution.py:221
  55.1 2.5 %collective-permute-done.14 = f16[136,512]{1,0:T(8,128)(2,1)S(1)} collective-permute-done((f16[136,512]{1,0:T(8,128)(2,1)S(1)}, f16[136,512]{1,0:T(8,128)(2,1)S(1)}, u32[]{:S(2)}, u32[]{:S(2)}) %collective-permute-start.14) | collective-permute-done | bytes 139296 | tf_op jit(solution)/shard_map/reduce_rows/ppermute | solution.py:221
  57.6 2.6 %collective-permute-done.16 = f16[136,512]{1,0:T(8,128)(2,1)S(1)} collective-permute-done((f16[136,512]{1,0:T(8,128)(2,1)S(1)}, f16[136,512]{1,0:T(8,128)(2,1)S(1)}, u32[]{:S(2)}, u32[]{:S(2)}) %collective-permute-start.16) | collective-permute-done | bytes 139296 | tf_op jit(solution)/shard_map/reduce_rows/ppermute | solution.py:221
  60.2 1.1 %collective-permute-done.21 = f16[136,512]{1,0:T(8,128)(2,1)S(1)} collective-permute-done((f16[136,512]{1,0:T(8,128)(2,1)S(1)}, f16[136,512]{1,0:T(8,128)(2,1)S(1)}, u32[]{:S(2)}, u32[]{:S(2)}) %collective-permute-start.21) | collective-permute-done | bytes 139296 | tf_op jit(solution)/shard_map/reduce_rows/ppermute | solution.py:221
  61.3 1.3 %collective-permute-done.22 = f16[136,512]{1,0:T(8,128)(2,1)S(1)} collective-permute-done((f16[136,512]{1,0:T(8,128)(2,1)S(1)}, f16[136,512]{1,0:T(8,128)(2,1)S(1)}, u32[]{:S(2)}, u32[]{:S(2)}) %collective-permute-start.22) | collective-permute-done | bytes 139296 | tf_op jit(solution)/shard_map/reduce_rows/ppermute | solution.py:221
  62.9 2.3 %collective-permute-start.29 = (bf16[128,512]{1,0:T(8,128)(2,1)S(1)}, bf16[128,512]{1,0:T(8,128)(2,1)S(1)}, u32[]{:S(2)}, u32[]{:S(2)}) collective-permute-start(bf16[128,512]{1,0:T(8,128)(2,1)S(1)} %fusion.17.a0), channel_id=1, source_target_pairs={{0,10},{1,11},{2,8},{3,9},{4,14},{5,15},{6,12},{7,13},{8,2},{9,3},... | collective-permute-start | bytes 393224 | tf_op jit(solution)/shard_map/gather_new/ppermute | solution.py:232
  65.2 0.8 collective-permute-start.25
  66.0 3.0 %collective-permute-start.26 = (bf16[128,512]{1,0:T(8,128)(2,1)S(1)}, bf16[128,512]{1,0:T(8,128)(2,1)S(1)}, u32[]{:S(2)}, u32[]{:S(2)}) collective-permute-start(bf16[128,512]{1,0:T(8,128)(2,1)S(1)} %fusion.17.a0), channel_id=1, source_target_pairs={{0,14},{1,15},{2,12},{3,13},{4,2},{5,3},{6,0},{7,1},{8,6},{9,7},{1... | collective-permute-start | bytes 393224 | tf_op jit(solution)/shard_map/gather_new/ppermute | solution.py:232
  69.0 1.5 %collective-permute-done.29.a1 = bf16[128,512]{1,0:T(8,128)(2,1)S(1)} collective-permute-done((bf16[128,512]{1,0:T(8,128)(2,1)S(1)}, bf16[128,512]{1,0:T(8,128)(2,1)S(1)}, u32[]{:S(2)}, u32[]{:S(2)}) %collective-permute-start.29) | collective-permute-done | bytes 131104 | tf_op jit(solution)/shard_map/gather_new/ppermute | solution.py:232
  70.4 2.0 %collective-permute-start.35 = (bf16[128,512]{1,0:T(8,128)(2,1)S(1)}, bf16[128,512]{1,0:T(8,128)(2,1)S(1)}, u32[]{:S(2)}, u32[]{:S(2)}) collective-permute-start(bf16[128,512]{1,0:T(8,128)(2,1)S(1)} %fusion.17.a0), channel_id=1, source_target_pairs={{0,12},{1,13},{2,14},{3,15},{4,0},{5,1},{6,2},{7,3},{8,4},{9,5},{1... | collective-permute-start | bytes 393224 | tf_op jit(solution)/shard_map/gather_new/ppermute | solution.py:232
  73.7 2.9 %collective-permute-done.34.a0 = bf16[128,512]{1,0:T(8,128)(2,1)S(1)} collective-permute-done((bf16[128,512]{1,0:T(8,128)(2,1)S(1)}, bf16[128,512]{1,0:T(8,128)(2,1)S(1)}, u32[]{:S(2)}, u32[]{:S(2)}) %collective-permute-start.34) | collective-permute-done | bytes 131104 | tf_op jit(solution)/shard_map/gather_new/ppermute | solution.py:232
  76.6 1.2 %collective-permute-start.24 = (bf16[128,512]{1,0:T(8,128)(2,1)S(1)}, bf16[128,512]{1,0:T(8,128)(2,1)S(1)}, u32[]{:S(2)}, u32[]{:S(2)}) collective-permute-start(bf16[128,512]{1,0:T(8,128)(2,1)S(1)} %fusion.17.a0), channel_id=1, source_target_pairs={{0,2},{1,3},{2,0},{3,1},{4,6},{5,7},{6,4},{7,5},{8,10},{9,11},{10,... | collective-permute-start | bytes 393224 | tf_op jit(solution)/shard_map/gather_new/ppermute | solution.py:232
  77.9 1.0 collective-permute-start.23
  78.9 1.3 %gather_new.4 = (f32[8,136,512]{2,1,0:T(8,128)S(1)}, f32[8,512]{1,0:T(8,128)S(1)}) custom-call(f32[16,128,1024]{2,1,0:T(8,128)S(1)} %shard_map.59.counts, bf16[128,512]{1,0:T(8,128)(2,1)S(1)} %fusion.17.a0, bf16[128,512]{1,0:T(8,128)(2,1)S(1)} %collective-permute-done.29.a1, bf16[128,512]{1,0:T(8,128)(2,1)S(1)} %collective-permute-done.30.b0, ...), custom_call_target="tpu_custom_call" | custom-call | flops 1048576 | bytes 65536 | tf_op jit(solution)/shard_map/gather_new/pallas_call | solution.py:161
  80.2 1.4 %gather_new.5 = (f32[8,136,512]{2,1,0:T(8,128)S(1)}, f32[8,512]{1,0:T(8,128)S(1)}) custom-call(f32[16,128,1024]{2,1,0:T(8,128)S(1)} %shard_map.59.counts, bf16[128,512]{1,0:T(8,128)(2,1)S(1)} %collective-permute-done.25.a0, bf16[128,512]{1,0:T(8,128)(2,1)S(1)} %collective-permute-done.26.a1, ...), custom_call_target="tpu_custom_call", output_to_operand_aliasing={{0}: (6, {}), {1}: (7, {})} | custom-call | flops 1048576 | bytes 65536 | tf_op jit(solution)/shard_map/gather_new/pallas_call | solution.py:161
  82.2 1.8 %collective-permute-done.23.a0 = bf16[128,512]{1,0:T(8,128)(2,1)S(1)} collective-permute-done((bf16[128,512]{1,0:T(8,128)(2,1)S(1)}, bf16[128,512]{1,0:T(8,128)(2,1)S(1)}, u32[]{:S(2)}, u32[]{:S(2)}) %collective-permute-start.23) | collective-permute-done | bytes 131104 | tf_op jit(solution)/shard_map/gather_new/ppermute | solution.py:232
  84.6 1.4 %gather_new.6 = (f32[8,136,512]{2,1,0:T(8,128)S(1)}, f32[8,512]{1,0:T(8,128)S(1)}) custom-call(f32[16,128,1024]{2,1,0:T(8,128)S(1)} %shard_map.59.counts, bf16[128,512]{1,0:T(8,128)(2,1)S(1)} %collective-permute-done.34.a0, bf16[128,512]{1,0:T(8,128)(2,1)S(1)} %collective-permute-done.35.a1, ...), custom_call_target="tpu_custom_call", output_to_operand_aliasing={{0}: (6, {}), {1}: (7, {})} | custom-call | flops 1048576 | bytes 65536 | tf_op jit(solution)/shard_map/gather_new/pallas_call | solution.py:161
  86.0 1.4 %gather_new.7 = (f32[8,136,512]{2,1,0:T(8,128)S(1)}, f32[8,512]{1,0:T(8,128)S(1)}) custom-call(f32[16,128,1024]{2,1,0:T(8,128)S(1)} %shard_map.59.counts, bf16[128,512]{1,0:T(8,128)(2,1)S(1)} %collective-permute-done.23.a0, bf16[128,512]{1,0:T(8,128)(2,1)S(1)} %collective-permute-done.24.a1, ...), custom_call_target="tpu_custom_call", output_to_operand_aliasing={{0}: (6, {}), {1}: (7, {})} | custom-call | flops 1048576 | bytes 65536 | tf_op jit(solution)/shard_map/gather_new/pallas_call | solution.py:161
  87.6 2.0 %collective-permute-start.38 = (f16[136,512]{1,0:T(8,128)(2,1)S(1)}, f16[136,512]{1,0:T(8,128)(2,1)S(1)}, u32[]{:S(2)}, u32[]{:S(2)}) collective-permute-start(f16[136,512]{1,0:T(8,128)(2,1)S(1)} %get-tuple-element.42), channel_id=1, source_target_pairs={{0,80},{16,64},{32,112},{48,96},{64,16},{80,0},{96,48},{112,32},{1... | collective-permute-start | bytes 417800 | tf_op jit(solution)/shard_map/reduce_columns/ppermute | solution.py:258
  89.7 1.5 %collective-permute-start.39 = (f16[136,512]{1,0:T(8,128)(2,1)S(1)}, f16[136,512]{1,0:T(8,128)(2,1)S(1)}, u32[]{:S(2)}, u32[]{:S(2)}) collective-permute-start(f16[136,512]{1,0:T(8,128)(2,1)S(1)} %get-tuple-element.48), channel_id=1, source_target_pairs={{0,64},{16,80},{32,96},{48,112},{64,0},{80,16},{96,32},{112,48},{1... | collective-permute-start | bytes 417800 | tf_op jit(solution)/shard_map/reduce_columns/ppermute | solution.py:258
  91.2 4.3 %collective-permute-start.40 = (f16[136,512]{1,0:T(8,128)(2,1)S(1)}, f16[136,512]{1,0:T(8,128)(2,1)S(1)}, u32[]{:S(2)}, u32[]{:S(2)}) collective-permute-start(f16[136,512]{1,0:T(8,128)(2,1)S(1)} %get-tuple-element.47), channel_id=1, source_target_pairs={{0,48},{16,32},{32,80},{48,64},{64,112},{80,96},{96,16},{112,0},{1... | collective-permute-start | bytes 417800 | tf_op jit(solution)/shard_map/reduce_columns/ppermute | solution.py:258
  95.4 1.4 %collective-permute-start.41 = (f16[136,512]{1,0:T(8,128)(2,1)S(1)}, f16[136,512]{1,0:T(8,128)(2,1)S(1)}, u32[]{:S(2)}, u32[]{:S(2)}) collective-permute-start(f16[136,512]{1,0:T(8,128)(2,1)S(1)} %get-tuple-element.46), channel_id=1, source_target_pairs={{0,112},{16,96},{32,16},{48,0},{64,48},{80,32},{96,80},{112,64},{1... | collective-permute-start | bytes 417800 | tf_op jit(solution)/shard_map/reduce_columns/ppermute | solution.py:258
  98.3 2.3 %collective-permute-start.43 = (f16[136,512]{1,0:T(8,128)(2,1)S(1)}, f16[136,512]{1,0:T(8,128)(2,1)S(1)}, u32[]{:S(2)}, u32[]{:S(2)}) collective-permute-start(f16[136,512]{1,0:T(8,128)(2,1)S(1)} %get-tuple-element.44), channel_id=1, source_target_pairs={{0,96},{16,112},{32,0},{48,16},{64,32},{80,48},{96,64},{112,80},{1... | collective-permute-start | bytes 417800 | tf_op jit(solution)/shard_map/reduce_columns/ppermute | solution.py:258
  100.5 2.6 %collective-permute-start.44 = (f16[136,512]{1,0:T(8,128)(2,1)S(1)}, f16[136,512]{1,0:T(8,128)(2,1)S(1)}, u32[]{:S(2)}, u32[]{:S(2)}) collective-permute-start(f16[136,512]{1,0:T(8,128)(2,1)S(1)} %get-tuple-element.43), channel_id=1, source_target_pairs={{0,16},{16,0},{32,48},{48,32},{64,80},{80,64},{96,112},{112,96},{1... | collective-permute-start | bytes 417800 | tf_op jit(solution)/shard_map/reduce_columns/ppermute | solution.py:258
  103.1 1.9 %collective-permute-done.40 = f16[136,512]{1,0:T(8,128)(2,1)S(1)} collective-permute-done((f16[136,512]{1,0:T(8,128)(2,1)S(1)}, f16[136,512]{1,0:T(8,128)(2,1)S(1)}, u32[]{:S(2)}, u32[]{:S(2)}) %collective-permute-start.40) | collective-permute-done | bytes 139296 | tf_op jit(solution)/shard_map/reduce_columns/ppermute | solution.py:258
  105.5 2.9 %collective-permute-done.44 = f16[136,512]{1,0:T(8,128)(2,1)S(1)} collective-permute-done((f16[136,512]{1,0:T(8,128)(2,1)S(1)}, f16[136,512]{1,0:T(8,128)(2,1)S(1)}, u32[]{:S(2)}, u32[]{:S(2)}) %collective-permute-start.44) | collective-permute-done | bytes 139296 | tf_op jit(solution)/shard_map/reduce_columns/ppermute | solution.py:258
  (93 shorter events, 10.8 us)
Async XLA Ops:
  0.6 16.9 %collective-permute-start = (bf16[128,512]{1,0:T(8,128)(2,1)}, bf16[128,512]{1,0:T(8,128)(2,1)S(1)}, u32[]{:S(2)}, u32[]{:S(2)}) collective-permute-start(bf16[128,512]{1,0:T(8,128)(2,1)} %param.6), channel_id=1, source_target_pairs={{0,2},{1,3},{2,0},{3,1},{4,6},{5,7},{6,4},{7,5},{8,10},{9,11},{10,... | collective-permute-start | bytes 393224 | tf_op jit(solution)/shard_map/gather_in/ppermute | solution.py:197
  2.4 10.6 %collective-permute-start.2 = (bf16[128,512]{1,0:T(8,128)(2,1)}, bf16[128,512]{1,0:T(8,128)(2,1)S(1)}, u32[]{:S(2)}, u32[]{:S(2)}) collective-permute-start(bf16[128,512]{1,0:T(8,128)(2,1)} %param.7), channel_id=1, source_target_pairs={{0,16},{16,0},{32,48},{48,32},{64,80},{80,64},{96,112},{112,96},{1... | collective-permute-start | bytes 393224 | tf_op jit(solution)/shard_map/gather_in/ppermute | solution.py:196
  7.5 3.4 %copy-start = (s32[2048,1024]{1,0:T(8,128)S(1)}, s32[2048,1024]{1,0:T(8,128)}, u32[]{:S(2)}) copy-start(s32[2048,1024]{1,0:T(8,128)} %counts.1) | copy-start | bytes 25165828
  10.9 6.7 %copy-start.3 = (bf16[128,512]{1,0:T(8,128)(2,1)S(1)}, bf16[128,512]{1,0:T(8,128)(2,1)}, u32[]{:S(2)}) copy-start(bf16[128,512]{1,0:T(8,128)(2,1)} %param.6) | copy-start | bytes 393220
  13.1 23.8 %collective-permute-start.3 = (bf16[2,128,512]{2,1,0:T(8,128)(2,1)S(1)}, bf16[2,128,512]{2,1,0:T(8,128)(2,1)S(1)}, u32[]{:S(2)}, u32[]{:S(2)}) collective-permute-start(bf16[2,128,512]{2,1,0:T(8,128)(2,1)S(1)} %pad_maximum_fusion.1), channel_id=1, source_target_pairs={{0,96},{16,112},{32,0},{48,16},{64,32},{80,48},{96,64},{112,80},{1... | collective-permute-start | bytes 786440 | tf_op jit(solution)/shard_map/gather_in/ppermute | solution.py:201
  15.8 21.6 %collective-permute-start.4 = (bf16[2,128,512]{2,1,0:T(8,128)(2,1)S(1)}, bf16[2,128,512]{2,1,0:T(8,128)(2,1)S(1)}, u32[]{:S(2)}, u32[]{:S(2)}) collective-permute-start(bf16[2,128,512]{2,1,0:T(8,128)(2,1)S(1)} %pad_maximum_fusion.1), channel_id=1, source_target_pairs={{0,64},{16,80},{32,96},{48,112},{64,0},{80,16},{96,32},{112,48},{1... | collective-permute-start | bytes 786440 | tf_op jit(solution)/shard_map/gather_in/ppermute | solution.py:201
  16.6 20.9 %collective-permute-start.5 = (bf16[2,128,512]{2,1,0:T(8,128)(2,1)S(1)}, bf16[2,128,512]{2,1,0:T(8,128)(2,1)S(1)}, u32[]{:S(2)}, u32[]{:S(2)}) collective-permute-start(bf16[2,128,512]{2,1,0:T(8,128)(2,1)S(1)} %pad_maximum_fusion.1), channel_id=1, source_target_pairs={{0,32},{16,48},{32,64},{48,80},{64,96},{80,112},{96,0},{112,16},{1... | collective-permute-start | bytes 786440 | tf_op jit(solution)/shard_map/gather_in/ppermute | solution.py:201
  17.6 8.9 %collective-permute-start.8 = (bf16[2,128,512]{2,1,0:T(8,128)(2,1)S(1)}, bf16[2,128,512]{2,1,0:T(8,128)(2,1)S(1)}, u32[]{:S(2)}, u32[]{:S(2)}) collective-permute-start(bf16[2,128,512]{2,1,0:T(8,128)(2,1)S(1)} %pad_maximum_fusion), channel_id=1, source_target_pairs={{0,8},{1,9},{2,10},{3,11},{4,12},{5,13},{6,14},{7,15},{8,0},{9,1},... | collective-permute-start | bytes 786440 | tf_op jit(solution)/shard_map/gather_in/ppermute | solution.py:202
  21.5 11.3 %collective-permute-start.6 = (bf16[2,128,512]{2,1,0:T(8,128)(2,1)S(1)}, bf16[2,128,512]{2,1,0:T(8,128)(2,1)S(1)}, u32[]{:S(2)}, u32[]{:S(2)}) collective-permute-start(bf16[2,128,512]{2,1,0:T(8,128)(2,1)S(1)} %pad_maximum_fusion), channel_id=1, source_target_pairs={{0,12},{1,13},{2,14},{3,15},{4,0},{5,1},{6,2},{7,3},{8,4},{9,5},{1... | collective-permute-start | bytes 786440 | tf_op jit(solution)/shard_map/gather_in/ppermute | solution.py:202
  26.4 10.4 %collective-permute-start.17 = (bf16[2,128,512]{2,1,0:T(8,128)(2,1)S(1)}, bf16[2,128,512]{2,1,0:T(8,128)(2,1)S(1)}, u32[]{:S(2)}, u32[]{:S(2)}) collective-permute-start(bf16[2,128,512]{2,1,0:T(8,128)(2,1)S(1)} %pad_maximum_fusion), channel_id=1, source_target_pairs={{0,4},{1,5},{2,6},{3,7},{4,8},{5,9},{6,10},{7,11},{8,12},{9,13},{1... | collective-permute-start | bytes 786440 | tf_op jit(solution)/shard_map/gather_in/ppermute | solution.py:202
  32.8 7.0 %collective-permute-start.1 = (bf16[2,128,512]{2,1,0:T(8,128)(2,1)S(1)}, bf16[2,128,512]{2,1,0:T(8,128)(2,1)S(1)}, u32[]{:S(2)}, u32[]{:S(2)}) collective-permute-start(bf16[2,128,512]{2,1,0:T(8,128)(2,1)S(1)} %pad_maximum_fusion), channel_id=1, source_target_pairs={{0,1},{1,0},{2,3},{3,2},{4,5},{5,4},{6,7},{7,6},{8,9},{9,8},{10,11... | collective-permute-start | bytes 786440 | tf_op jit(solution)/shard_map/gather_in/ppermute | solution.py:52
  36.8 1.5 %collective-permute-start.9 = (bf16[2,128,512]{2,1,0:T(8,128)(2,1)S(1)}, bf16[2,128,512]{2,1,0:T(8,128)(2,1)S(1)}, u32[]{:S(2)}, u32[]{:S(2)}) collective-permute-start(bf16[2,128,512]{2,1,0:T(8,128)(2,1)S(1)} %collective-permute-done.8), channel_id=1, source_target_pairs={{0,1},{1,0},{2,3},{3,2},{4,5},{5,4},{6,7},{7,6},{8,9},{9,8},{10,11... | collective-permute-start | bytes 786440 | tf_op jit(solution)/shard_map/gather_in/ppermute | solution.py:52
  36.8 3.1 %collective-permute-start.7 = (bf16[2,128,512]{2,1,0:T(8,128)(2,1)S(1)}, bf16[2,128,512]{2,1,0:T(8,128)(2,1)S(1)}, u32[]{:S(2)}, u32[]{:S(2)}) collective-permute-start(bf16[2,128,512]{2,1,0:T(8,128)(2,1)S(1)} %collective-permute-done.6), channel_id=1, source_target_pairs={{0,1},{1,0},{2,3},{3,2},{4,5},{5,4},{6,7},{7,6},{8,9},{9,8},{10,11... | collective-permute-start | bytes 786440 | tf_op jit(solution)/shard_map/gather_in/ppermute | solution.py:52
  37.4 4.2 %collective-permute-start.18 = (bf16[2,128,512]{2,1,0:T(8,128)(2,1)S(1)}, bf16[2,128,512]{2,1,0:T(8,128)(2,1)S(1)}, u32[]{:S(2)}, u32[]{:S(2)}) collective-permute-start(bf16[2,128,512]{2,1,0:T(8,128)(2,1)S(1)} %collective-permute-done.17), channel_id=1, source_target_pairs={{0,1},{1,0},{2,3},{3,2},{4,5},{5,4},{6,7},{7,6},{8,9},{9,8},{10,11... | collective-permute-start | bytes 786440 | tf_op jit(solution)/shard_map/gather_in/ppermute | solution.py:52
  39.6 2.1 %collective-permute-start.12 = (f32[2,136,512]{2,1,0:T(8,128)S(1)}, f32[2,136,512]{2,1,0:T(8,128)S(1)}, u32[]{:S(2)}, u32[]{:S(2)}) collective-permute-start(f32[2,136,512]{2,1,0:T(8,128)S(1)} %get-tuple-element.27), channel_id=1, source_target_pairs={{0,1},{1,0},{2,3},{3,2},{4,5},{5,4},{6,7},{7,6},{8,9},{9,8},{10,11... | collective-permute-start | bytes 1671176 | tf_op jit(solution)/shard_map/reduce_rows/ppermute | solution.py:52
  41.2 5.4 %collective-permute-start.10 = (f32[2,136,512]{2,1,0:T(8,128)S(1)}, f32[2,136,512]{2,1,0:T(8,128)S(1)}, u32[]{:S(2)}, u32[]{:S(2)}) collective-permute-start(f32[2,136,512]{2,1,0:T(8,128)S(1)} %get-tuple-element.24), channel_id=1, source_target_pairs={{0,1},{1,0},{2,3},{3,2},{4,5},{5,4},{6,7},{7,6},{8,9},{9,8},{10,11... | collective-permute-start | bytes 1671176 | tf_op jit(solution)/shard_map/reduce_rows/ppermute | solution.py:52
  43.0 6.5 %collective-permute-start.19 = (f32[2,136,512]{2,1,0:T(8,128)S(1)}, f32[2,136,512]{2,1,0:T(8,128)S(1)}, u32[]{:S(2)}, u32[]{:S(2)}) collective-permute-start(f32[2,136,512]{2,1,0:T(8,128)S(1)} %get-tuple-element.30), channel_id=1, source_target_pairs={{0,1},{1,0},{2,3},{3,2},{4,5},{5,4},{6,7},{7,6},{8,9},{9,8},{10,11... | collective-permute-start | bytes 1671176 | tf_op jit(solution)/shard_map/reduce_rows/ppermute | solution.py:52
  43.4 10.1 %collective-permute-start.13 = (f16[136,512]{1,0:T(8,128)(2,1)S(1)}, f16[136,512]{1,0:T(8,128)(2,1)S(1)}, u32[]{:S(2)}, u32[]{:S(2)}) collective-permute-start(f16[136,512]{1,0:T(8,128)(2,1)S(1)} %get-tuple-element.49), channel_id=1, source_target_pairs={{0,10},{1,11},{2,8},{3,9},{4,14},{5,15},{6,12},{7,13},{8,2},{9,3},... | collective-permute-start | bytes 417800 | tf_op jit(solution)/shard_map/reduce_rows/ppermute | solution.py:221
  44.1 13.5 %collective-permute-start.14 = (f16[136,512]{1,0:T(8,128)(2,1)S(1)}, f16[136,512]{1,0:T(8,128)(2,1)S(1)}, u32[]{:S(2)}, u32[]{:S(2)}) collective-permute-start(f16[136,512]{1,0:T(8,128)(2,1)S(1)} %get-tuple-element.50), channel_id=1, source_target_pairs={{0,8},{1,9},{2,10},{3,11},{4,12},{5,13},{6,14},{7,15},{8,0},{9,1},... | collective-permute-start | bytes 417800 | tf_op jit(solution)/shard_map/reduce_rows/ppermute | solution.py:221
  47.9 2.8 %collective-permute-start.11 = (f32[2,136,512]{2,1,0:T(8,128)S(1)}, f32[2,136,512]{2,1,0:T(8,128)S(1)}, u32[]{:S(2)}, u32[]{:S(2)}) collective-permute-start(f32[2,136,512]{2,1,0:T(8,128)S(1)} %get-tuple-element.26), channel_id=1, source_target_pairs={{0,1},{1,0},{2,3},{3,2},{4,5},{5,4},{6,7},{7,6},{8,9},{9,8},{10,11... | collective-permute-start | bytes 1671176 | tf_op jit(solution)/shard_map/reduce_rows/ppermute | solution.py:52
  48.2 9.4 %collective-permute-start.15 = (f16[136,512]{1,0:T(8,128)(2,1)S(1)}, f16[136,512]{1,0:T(8,128)(2,1)S(1)}, u32[]{:S(2)}, u32[]{:S(2)}) collective-permute-start(f16[136,512]{1,0:T(8,128)(2,1)S(1)} %get-tuple-element.51), channel_id=1, source_target_pairs={{0,6},{1,7},{2,4},{3,5},{4,10},{5,11},{6,8},{7,9},{8,14},{9,15},{1... | collective-permute-start | bytes 417800 | tf_op jit(solution)/shard_map/reduce_rows/ppermute | solution.py:221
  49.5 10.7 %collective-permute-start.16 = (f16[136,512]{1,0:T(8,128)(2,1)S(1)}, f16[136,512]{1,0:T(8,128)(2,1)S(1)}, u32[]{:S(2)}, u32[]{:S(2)}) collective-permute-start(f16[136,512]{1,0:T(8,128)(2,1)S(1)} %get-tuple-element.52), channel_id=1, source_target_pairs={{0,4},{1,5},{2,6},{3,7},{4,8},{5,9},{6,10},{7,11},{8,12},{9,13},{1... | collective-permute-start | bytes 417800 | tf_op jit(solution)/shard_map/reduce_rows/ppermute | solution.py:221
  50.7 9.5 %collective-permute-start.20 = (f16[136,512]{1,0:T(8,128)(2,1)S(1)}, f16[136,512]{1,0:T(8,128)(2,1)S(1)}, u32[]{:S(2)}, u32[]{:S(2)}) collective-permute-start(f16[136,512]{1,0:T(8,128)(2,1)S(1)} %get-tuple-element.53), channel_id=1, source_target_pairs={{0,14},{1,15},{2,12},{3,13},{4,2},{5,3},{6,0},{7,1},{8,6},{9,7},{1... | collective-permute-start | bytes 417800 | tf_op jit(solution)/shard_map/reduce_rows/ppermute | solution.py:221
  53.5 7.9 %collective-permute-start.21 = (f16[136,512]{1,0:T(8,128)(2,1)S(1)}, f16[136,512]{1,0:T(8,128)(2,1)S(1)}, u32[]{:S(2)}, u32[]{:S(2)}) collective-permute-start(f16[136,512]{1,0:T(8,128)(2,1)S(1)} %get-tuple-element.54), channel_id=1, source_target_pairs={{0,12},{1,13},{2,14},{3,15},{4,0},{5,1},{6,2},{7,3},{8,4},{9,5},{1... | collective-permute-start | bytes 417800 | tf_op jit(solution)/shard_map/reduce_rows/ppermute | solution.py:221
  57.6 5.1 %collective-permute-start.22 = (f16[136,512]{1,0:T(8,128)(2,1)S(1)}, f16[136,512]{1,0:T(8,128)(2,1)S(1)}, u32[]{:S(2)}, u32[]{:S(2)}) collective-permute-start(f16[136,512]{1,0:T(8,128)(2,1)S(1)} %fusion.26), channel_id=1, source_target_pairs={{0,2},{1,3},{2,0},{3,1},{4,6},{5,7},{6,4},{7,5},{8,10},{9,11},{10,... | collective-permute-start | bytes 417800 | tf_op jit(solution)/shard_map/reduce_rows/ppermute | solution.py:221
  62.9 17.3 %copy-start.1 = (bf16[128,512]{1,0:T(8,128)(2,1)}, bf16[128,512]{1,0:T(8,128)(2,1)S(1)}, u32[]{:S(2)}) copy-start(bf16[128,512]{1,0:T(8,128)(2,1)S(1)} %fusion.17.a0) | copy-start | bytes 393220
  62.9 7.5 %collective-permute-start.29 = (bf16[128,512]{1,0:T(8,128)(2,1)S(1)}, bf16[128,512]{1,0:T(8,128)(2,1)S(1)}, u32[]{:S(2)}, u32[]{:S(2)}) collective-permute-start(bf16[128,512]{1,0:T(8,128)(2,1)S(1)} %fusion.17.a0), channel_id=1, source_target_pairs={{0,10},{1,11},{2,8},{3,9},{4,14},{5,15},{6,12},{7,13},{8,2},{9,3},... | collective-permute-start | bytes 393224 | tf_op jit(solution)/shard_map/gather_new/ppermute | solution.py:232
  65.2 5.3 %collective-permute-start.30 = (bf16[128,512]{1,0:T(8,128)(2,1)S(1)}, bf16[128,512]{1,0:T(8,128)(2,1)S(1)}, u32[]{:S(2)}, u32[]{:S(2)}) collective-permute-start(bf16[128,512]{1,0:T(8,128)(2,1)S(1)} %fusion.17.a0), channel_id=1, source_target_pairs={{0,1},{1,0},{2,3},{3,2},{4,5},{5,4},{6,7},{7,6},{8,9},{9,8},{10,11... | collective-permute-start | bytes 393224 | tf_op jit(solution)/shard_map/gather_new/ppermute | solution.py:52
  65.2 8.0 %collective-permute-start.25 = (bf16[128,512]{1,0:T(8,128)(2,1)S(1)}, bf16[128,512]{1,0:T(8,128)(2,1)S(1)}, u32[]{:S(2)}, u32[]{:S(2)}) collective-permute-start(bf16[128,512]{1,0:T(8,128)(2,1)S(1)} %fusion.17.a0), channel_id=1, source_target_pairs={{0,8},{1,9},{2,10},{3,11},{4,12},{5,13},{6,14},{7,15},{8,0},{9,1},... | collective-permute-start | bytes 393224 | tf_op jit(solution)/shard_map/gather_new/ppermute | solution.py:232
  66.0 7.3 %collective-permute-start.26 = (bf16[128,512]{1,0:T(8,128)(2,1)S(1)}, bf16[128,512]{1,0:T(8,128)(2,1)S(1)}, u32[]{:S(2)}, u32[]{:S(2)}) collective-permute-start(bf16[128,512]{1,0:T(8,128)(2,1)S(1)} %fusion.17.a0), channel_id=1, source_target_pairs={{0,14},{1,15},{2,12},{3,13},{4,2},{5,3},{6,0},{7,1},{8,6},{9,7},{1... | collective-permute-start | bytes 393224 | tf_op jit(solution)/shard_map/gather_new/ppermute | solution.py:232
  69.0 7.7 %collective-permute-start.34 = (bf16[128,512]{1,0:T(8,128)(2,1)S(1)}, bf16[128,512]{1,0:T(8,128)(2,1)S(1)}, u32[]{:S(2)}, u32[]{:S(2)}) collective-permute-start(bf16[128,512]{1,0:T(8,128)(2,1)S(1)} %fusion.17.a0), channel_id=1, source_target_pairs={{0,6},{1,7},{2,4},{3,5},{4,10},{5,11},{6,8},{7,9},{8,14},{9,15},{1... | collective-permute-start | bytes 393224 | tf_op jit(solution)/shard_map/gather_new/ppermute | solution.py:232
  70.4 7.4 %collective-permute-start.31 = (bf16[128,512]{1,0:T(8,128)(2,1)S(1)}, bf16[128,512]{1,0:T(8,128)(2,1)S(1)}, u32[]{:S(2)}, u32[]{:S(2)}) collective-permute-start(bf16[128,512]{1,0:T(8,128)(2,1)S(1)} %collective-permute-done.29.a1), channel_id=1, source_target_pairs={{0,1},{1,0},{2,3},{3,2},{4,5},{5,4},{6,7},{7,6},{8,9},{9,8},{10,11... | collective-permute-start | bytes 393224 | tf_op jit(solution)/shard_map/gather_new/ppermute | solution.py:52
  70.4 9.7 %collective-permute-start.35 = (bf16[128,512]{1,0:T(8,128)(2,1)S(1)}, bf16[128,512]{1,0:T(8,128)(2,1)S(1)}, u32[]{:S(2)}, u32[]{:S(2)}) collective-permute-start(bf16[128,512]{1,0:T(8,128)(2,1)S(1)} %fusion.17.a0), channel_id=1, source_target_pairs={{0,12},{1,13},{2,14},{3,15},{4,0},{5,1},{6,2},{7,3},{8,4},{9,5},{1... | collective-permute-start | bytes 393224 | tf_op jit(solution)/shard_map/gather_new/ppermute | solution.py:232
  73.2 7.0 %collective-permute-start.27 = (bf16[128,512]{1,0:T(8,128)(2,1)S(1)}, bf16[128,512]{1,0:T(8,128)(2,1)S(1)}, u32[]{:S(2)}, u32[]{:S(2)}) collective-permute-start(bf16[128,512]{1,0:T(8,128)(2,1)S(1)} %collective-permute-done.25.a0), channel_id=1, source_target_pairs={{0,1},{1,0},{2,3},{3,2},{4,5},{5,4},{6,7},{7,6},{8,9},{9,8},{10,11... | collective-permute-start | bytes 393224 | tf_op jit(solution)/shard_map/gather_new/ppermute | solution.py:52
  73.3 7.0 %collective-permute-start.28 = (bf16[128,512]{1,0:T(8,128)(2,1)S(1)}, bf16[128,512]{1,0:T(8,128)(2,1)S(1)}, u32[]{:S(2)}, u32[]{:S(2)}) collective-permute-start(bf16[128,512]{1,0:T(8,128)(2,1)S(1)} %collective-permute-done.26.a1), channel_id=1, source_target_pairs={{0,1},{1,0},{2,3},{3,2},{4,5},{5,4},{6,7},{7,6},{8,9},{9,8},{10,11... | collective-permute-start | bytes 393224 | tf_op jit(solution)/shard_map/gather_new/ppermute | solution.py:52
  76.6 5.0 %collective-permute-start.24 = (bf16[128,512]{1,0:T(8,128)(2,1)S(1)}, bf16[128,512]{1,0:T(8,128)(2,1)S(1)}, u32[]{:S(2)}, u32[]{:S(2)}) collective-permute-start(bf16[128,512]{1,0:T(8,128)(2,1)S(1)} %fusion.17.a0), channel_id=1, source_target_pairs={{0,2},{1,3},{2,0},{3,1},{4,6},{5,7},{6,4},{7,5},{8,10},{9,11},{10,... | collective-permute-start | bytes 393224 | tf_op jit(solution)/shard_map/gather_new/ppermute | solution.py:232
  77.9 6.2 %collective-permute-start.23 = (bf16[128,512]{1,0:T(8,128)(2,1)S(1)}, bf16[128,512]{1,0:T(8,128)(2,1)S(1)}, u32[]{:S(2)}, u32[]{:S(2)}) collective-permute-start(bf16[128,512]{1,0:T(8,128)(2,1)S(1)} %fusion.17.a0), channel_id=1, source_target_pairs={{0,4},{1,5},{2,6},{3,7},{4,8},{5,9},{6,10},{7,11},{8,12},{9,13},{1... | collective-permute-start | bytes 393224 | tf_op jit(solution)/shard_map/gather_new/ppermute | solution.py:232
  81.6 2.9 %collective-permute-start.36 = (bf16[128,512]{1,0:T(8,128)(2,1)S(1)}, bf16[128,512]{1,0:T(8,128)(2,1)S(1)}, u32[]{:S(2)}, u32[]{:S(2)}) collective-permute-start(bf16[128,512]{1,0:T(8,128)(2,1)S(1)} %collective-permute-done.34.a0), channel_id=1, source_target_pairs={{0,1},{1,0},{2,3},{3,2},{4,5},{5,4},{6,7},{7,6},{8,9},{9,8},{10,11... | collective-permute-start | bytes 393224 | tf_op jit(solution)/shard_map/gather_new/ppermute | solution.py:52
  81.7 2.8 %collective-permute-start.37 = (bf16[128,512]{1,0:T(8,128)(2,1)S(1)}, bf16[128,512]{1,0:T(8,128)(2,1)S(1)}, u32[]{:S(2)}, u32[]{:S(2)}) collective-permute-start(bf16[128,512]{1,0:T(8,128)(2,1)S(1)} %collective-permute-done.35.a1), channel_id=1, source_target_pairs={{0,1},{1,0},{2,3},{3,2},{4,5},{5,4},{6,7},{7,6},{8,9},{9,8},{10,11... | collective-permute-start | bytes 393224 | tf_op jit(solution)/shard_map/gather_new/ppermute | solution.py:52
  84.0 1.9 %collective-permute-start.33 = (bf16[128,512]{1,0:T(8,128)(2,1)S(1)}, bf16[128,512]{1,0:T(8,128)(2,1)S(1)}, u32[]{:S(2)}, u32[]{:S(2)}) collective-permute-start(bf16[128,512]{1,0:T(8,128)(2,1)S(1)} %collective-permute-done.24.a1), channel_id=1, source_target_pairs={{0,1},{1,0},{2,3},{3,2},{4,5},{5,4},{6,7},{7,6},{8,9},{9,8},{10,11... | collective-permute-start | bytes 393224 | tf_op jit(solution)/shard_map/gather_new/ppermute | solution.py:52
  84.0 1.9 %collective-permute-start.32 = (bf16[128,512]{1,0:T(8,128)(2,1)S(1)}, bf16[128,512]{1,0:T(8,128)(2,1)S(1)}, u32[]{:S(2)}, u32[]{:S(2)}) collective-permute-start(bf16[128,512]{1,0:T(8,128)(2,1)S(1)} %collective-permute-done.23.a0), channel_id=1, source_target_pairs={{0,1},{1,0},{2,3},{3,2},{4,5},{5,4},{6,7},{7,6},{8,9},{9,8},{10,11... | collective-permute-start | bytes 393224 | tf_op jit(solution)/shard_map/gather_new/ppermute | solution.py:52
  87.6 10.6 %collective-permute-start.38 = (f16[136,512]{1,0:T(8,128)(2,1)S(1)}, f16[136,512]{1,0:T(8,128)(2,1)S(1)}, u32[]{:S(2)}, u32[]{:S(2)}) collective-permute-start(f16[136,512]{1,0:T(8,128)(2,1)S(1)} %get-tuple-element.42), channel_id=1, source_target_pairs={{0,80},{16,64},{32,112},{48,96},{64,16},{80,0},{96,48},{112,32},{1... | collective-permute-start | bytes 417800 | tf_op jit(solution)/shard_map/reduce_columns/ppermute | solution.py:258
  89.7 10.9 %collective-permute-start.39 = (f16[136,512]{1,0:T(8,128)(2,1)S(1)}, f16[136,512]{1,0:T(8,128)(2,1)S(1)}, u32[]{:S(2)}, u32[]{:S(2)}) collective-permute-start(f16[136,512]{1,0:T(8,128)(2,1)S(1)} %get-tuple-element.48), channel_id=1, source_target_pairs={{0,64},{16,80},{32,96},{48,112},{64,0},{80,16},{96,32},{112,48},{1... | collective-permute-start | bytes 417800 | tf_op jit(solution)/shard_map/reduce_columns/ppermute | solution.py:258
  91.2 13.8 %collective-permute-start.40 = (f16[136,512]{1,0:T(8,128)(2,1)S(1)}, f16[136,512]{1,0:T(8,128)(2,1)S(1)}, u32[]{:S(2)}, u32[]{:S(2)}) collective-permute-start(f16[136,512]{1,0:T(8,128)(2,1)S(1)} %get-tuple-element.47), channel_id=1, source_target_pairs={{0,48},{16,32},{32,80},{48,64},{64,112},{80,96},{96,16},{112,0},{1... | collective-permute-start | bytes 417800 | tf_op jit(solution)/shard_map/reduce_columns/ppermute | solution.py:258
  95.4 10.1 %collective-permute-start.41 = (f16[136,512]{1,0:T(8,128)(2,1)S(1)}, f16[136,512]{1,0:T(8,128)(2,1)S(1)}, u32[]{:S(2)}, u32[]{:S(2)}) collective-permute-start(f16[136,512]{1,0:T(8,128)(2,1)S(1)} %get-tuple-element.46), channel_id=1, source_target_pairs={{0,112},{16,96},{32,16},{48,0},{64,48},{80,32},{96,80},{112,64},{1... | collective-permute-start | bytes 417800 | tf_op jit(solution)/shard_map/reduce_columns/ppermute | solution.py:258
  96.8 8.7 %collective-permute-start.42 = (f16[136,512]{1,0:T(8,128)(2,1)S(1)}, f16[136,512]{1,0:T(8,128)(2,1)S(1)}, u32[]{:S(2)}, u32[]{:S(2)}) collective-permute-start(f16[136,512]{1,0:T(8,128)(2,1)S(1)} %get-tuple-element.45), channel_id=1, source_target_pairs={{0,32},{16,48},{32,64},{48,80},{64,96},{80,112},{96,0},{112,16},{1... | collective-permute-start | bytes 417800 | tf_op jit(solution)/shard_map/reduce_columns/ppermute | solution.py:258
  98.3 7.3 %collective-permute-start.43 = (f16[136,512]{1,0:T(8,128)(2,1)S(1)}, f16[136,512]{1,0:T(8,128)(2,1)S(1)}, u32[]{:S(2)}, u32[]{:S(2)}) collective-permute-start(f16[136,512]{1,0:T(8,128)(2,1)S(1)} %get-tuple-element.44), channel_id=1, source_target_pairs={{0,96},{16,112},{32,0},{48,16},{64,32},{80,48},{96,64},{112,80},{1... | collective-permute-start | bytes 417800 | tf_op jit(solution)/shard_map/reduce_columns/ppermute | solution.py:258
  100.5 7.9 %collective-permute-start.44 = (f16[136,512]{1,0:T(8,128)(2,1)S(1)}, f16[136,512]{1,0:T(8,128)(2,1)S(1)}, u32[]{:S(2)}, u32[]{:S(2)}) collective-permute-start(f16[136,512]{1,0:T(8,128)(2,1)S(1)} %get-tuple-element.43), channel_id=1, source_target_pairs={{0,16},{16,0},{32,48},{48,32},{64,80},{80,64},{96,112},{112,96},{1... | collective-permute-start | bytes 417800 | tf_op jit(solution)/shard_map/reduce_columns/ppermute | solution.py:258
  (1 other events, 2.1 us)

commit v4 on v3

--- a/solution.py
+++ b/solution.py
@@ -60,34 +60,42 @@
     return lax.dot_general(a, b, (((0,), (0,)), ((), ())), preferred_element_type=F32)
 
 
-def stage_kernel(tiles_across, rows_ref, live_ref, place_ref, counts, staged):
-    step = pl.program_id(0)
-    row_tile = rows_ref[step] // 2
-    for k in range(2 * tiles_across):
-        place = place_ref[k]
-        start = pl.multiple_of(place * BLOCK, BLOCK)
-        live = live_ref[row_tile * tiles_across + place // 2] > 0
-        value = counts[:, pl.ds(start, BLOCK)].astype(F32)
-        staged[0, :, k * BLOCK : (k + 1) * BLOCK] = jnp.where(live, value, 0.0)
-
-
-def stage_counts(rows_at, live, columns_at, counts):
+def stage_kernel(rows_ref, place_ref, live_ref, counts, staged, held, sems):
+    copies = [
+        pltpu.make_async_copy(
+            counts.at[pl.ds(pl.multiple_of(rows_ref[g] * BLOCK, BLOCK), BLOCK)], held.at[g], sems.at[g]
+        )
+        for g in range(16)
+    ]
+    for copy in copies:
+        copy.start()
+    for g in range(16):
+        copies[g].wait()
+        for k in range(8):
+            place = place_ref[k]
+            start = pl.multiple_of(place * BLOCK, BLOCK)
+            live = live_ref[place // 2, rows_ref[g] // 2] > 0
+            value = held[g, :, pl.ds(start, BLOCK)].astype(F32)
+            staged[g, :, k * BLOCK : (k + 1) * BLOCK] = jnp.where(live, value, 0.0)
+
+
+def stage_counts(rows_at, columns_at, live, counts):
     across = counts.shape[1]
-    grid_spec = pltpu.PrefetchScalarGridSpec(
-        num_scalar_prefetch=3,
-        grid=(16,),
-        in_specs=[pl.BlockSpec((BLOCK, across), lambda g, rows, live, place: (rows[g], 0))],
-        out_specs=pl.BlockSpec((1, BLOCK, across), lambda g, rows, live, place: (g, 0, 0)),
-    )
+    smem = pl.BlockSpec(memory_space=pltpu.SMEM)
     return pl.pallas_call(
-        functools.partial(stage_kernel, across // TILE),
-        grid_spec=grid_spec,
+        stage_kernel,
+        in_specs=[smem, smem, smem, pl.BlockSpec(memory_space=pltpu.HBM)],
+        out_specs=pl.BlockSpec(memory_space=pltpu.VMEM),
         out_shape=jax.ShapeDtypeStruct((16, BLOCK, across), F32),
+        scratch_shapes=[
+            pltpu.VMEM((16, BLOCK, across), jnp.int32),
+            pltpu.SemaphoreType.DMA((16,)),
+        ],
         cost_estimate=pl.CostEstimate(
             flops=counts.size, bytes_accessed=8 * counts.size, transcendentals=0
         ),
-        compiler_params=pltpu.CompilerParams(vmem_limit_bytes=8 * 2**20),
-    )(rows_at, live, columns_at, counts)
+        compiler_params=pltpu.CompilerParams(vmem_limit_bytes=44 * 2**20),
+    )(rows_at, columns_at, live, counts)
 
 
 def ratios_of(counts, left, columns):
@@ -112,18 +120,17 @@
     return sum(rows[k].astype(F32) * (1 / (s * scale)) for k, s in enumerate(scales))
 
 
-def rows_kernel(first, counts, a0, a1, b0, b1, panel, *refs):
+def rows_kernel(at, counts, panel, *refs):
     keep, send = refs[-2:]
     columns = panel[...].reshape(-1, panel.shape[-1])
-    for e, (a, b) in enumerate(((a0, b0), (a1, b1))):
-        left = jnp.concatenate([a[...], b[...]], axis=0)
-        block = counts[first + 2 * e : first + 2 * e + 2].reshape(TILE, -1)
+    total = jnp.sum(columns.astype(F32), axis=0, keepdims=True)
+    rows = total_rows(total, COLUMN_STEPS, 1.0)
+    for e, first in enumerate(at):
+        left = jnp.concatenate([refs[2 * e][...], refs[2 * e + 1][...]], axis=0)
+        block = counts[first : first + 2].reshape(TILE, -1)
         total = jnp.dot(ratios_of(block, left, columns), columns, preferred_element_type=F32)
         keep[e, :BLOCK] = total[:BLOCK]
         send[e, :BLOCK] = total[BLOCK:]
-    total = jnp.sum(columns.astype(F32), axis=0, keepdims=True)
-    rows = total_rows(total, COLUMN_STEPS, 1.0)
-    for e in range(2):
         keep[e, BLOCK:] = rows
         send[e, BLOCK:] = rows
 
@@ -189,38 +196,37 @@
     columns_at = jnp.stack(
         [(x + dx) % 4 * 2 + (far + dh) % 2 for dx in range(4) for dh in range(2)]
     ).astype(jnp.int32)
-    live = tile_pattern.reshape(-1)
-
-    counts = stage_counts(rows_at, live, columns_at, click_counts)
+
+    counts = stage_counts(rows_at, columns_at, tile_pattern.T, click_counts)
     with jax.named_scope("gather_in"):
         column_pair = jnp.stack([column_factors, lax.ppermute(column_factors, "row", to_row(0, 1))])
         row_pair = jnp.stack([row_factors, lax.ppermute(row_factors, "col", to_col(0, 1))])
-        row_pair = after(row_pair, counts)
+        row_pair, column_pair, counts = lax.optimization_barrier((row_pair, column_pair, counts))
         own, panel = {0: row_pair}, {0: column_pair}
         for d in (2, 1, 3):
             panel[d] = lax.ppermute(column_pair, "row", along_x(-d))
             own[d] = lax.ppermute(row_pair, "col", along_z(-d))
+        panel = jnp.concatenate([panel[d] for d in range(4)])
         other = {d: swap_core(own[d]) for d in range(4)}
-        panel = jnp.concatenate([panel[d] for d in range(4)])
     with jax.named_scope("reduce_rows"):
-        piece = jax.ShapeDtypeStruct((2, BLOCK + PAD, width), F32)
-        came, arrived, waits = {}, [], ()
-        for d in (2, 1, 3, 0):
-            a, b = own[d], other[d]
+        came, arrived, waits = [], [], ()
+        for step in ([(2, 1)], [(2, 0), (1, 1)], [(1, 0), (3, 1)], [(3, 0), (0, 1), (0, 0)]):
+            piece = jax.ShapeDtypeStruct((len(step), BLOCK + PAD, width), F32)
+            blocks = [b for d, e in step for b in (own[d][e], other[d][e])]
             keep, send = call(
-                functools.partial(rows_kernel, 4 * d),
-                (counts, a[0], a[1], b[0], b[1], panel),
+                functools.partial(rows_kernel, tuple(4 * d + 2 * e for d, e in step)),
+                [counts, panel] + blocks,
                 (piece, piece),
                 {},
                 waits,
             )
-            came[d] = swap_core(send)
-            partial = (keep + came[d]) * ROW_SCALE
-            for e in (1, 0):
+            came.append(swap_core(send))
+            partial = (keep + came[-1]) * ROW_SCALE
+            for k, (d, e) in enumerate(step):
                 if d or e:
-                    arrived.append(lax.ppermute(partial[e].astype(WIRE), "col", to_col(d, e)))
-            waits = {2: (keep,), 1: (came.get(2),), 3: (came.get(1),)}.get(d)
-        partial = partial[0]
+                    arrived.append(lax.ppermute(partial[k].astype(WIRE), "col", to_col(d, e)))
+            waits = (came[-2],) if len(came) > 1 else (keep,)
+        partial = partial[2]
         for a in arrived:
             partial = partial + a.astype(F32)
         share = partial[:BLOCK] * (1 / ROW_SCALE)

time: 110 us -> 105 us (0.955)
  local copies, waits for them, and re-layouts: 5.72 us -> 1.24 us
  waiting for transfers between devices: 31.8 us -> 28.9 us
  Pallas kernels: 12.8 us -> 15.5 us
    unnamed x13 -> x11, local copies, waits for them, and re-layouts: 5.14 us -> 0.75 us
    ppermute x3, waiting for transfers between devices: 10.5 us -> 6.38 us  [local(): own[d] = lax.ppermute(row_pair, 'col', along_z(-d))]
    pallas_call x1, Pallas kernels: 2.12 us -> 4.17 us  [stage_counts(): pl.pallas_call(stage_kernel, in_specs=[smem, smem, smem, pl.BlockSpec(mem...]
    ppermute x1, waiting for transfers between devices: 0.01 us -> 1.12 us  [local(): lax.ppermute(column_factors, 'row', to_row(0, 1))]
    ppermute x7, starting transfers between devices: 10.3 us -> 9.16 us  [local(): own[d, e] = lax.ppermute(updated_rows, 'col', to_col(-d, e))]
  transfers between devices with their start and end apart: 45 -> 45, of which waited for: 16 -> 16; matrix products, arithmetic and copies ran while one was open for 3% -> 1% of each run, Pallas kernels for 10% -> 14%
where the time goes in v4:
time: 105 us; the launch traced here: 104 us
  starting transfers between devices  55 us (52%)
  waiting for transfers between devices  28.9 us (28%)
  Pallas kernels  15.5 us (15%)
  other arithmetic  1.98 us (2%)
  local copies, waits for them, and re-layouts  1.24 us (1%)
    ppermute x7, starting transfers between devices, local(): partial = partial + lax.ppermute(a, 'row', to_row(d, e)).astype(F32)  15.5 us
    pallas_call x8, Pallas kernels, call(): pl.pallas_call(kernel, in_specs=[vmem] * len(operands) + [pl.BlockSpec(me...  11.4 us
    ppermute x7, starting transfers between devices, local(): arrived.append(lax.ppermute(partial[k].astype(WIRE), 'col', to_col(d, e)))  9.77 us
    ppermute x7, starting transfers between devices, local(): own[d, e] = lax.ppermute(updated_rows, 'col', to_col(-d, e))  9.16 us
    ppermute x7, waiting for transfers between devices, local(): own[d, e] = lax.ppermute(updated_rows, 'col', to_col(-d, e))  7.73 us
    ppermute x3, starting transfers between devices, local(): own[d] = lax.ppermute(row_pair, 'col', along_z(-d))  7.62 us
    ppermute x7, waiting for transfers between devices, local(): arrived.append(lax.ppermute(partial[k].astype(WIRE), 'col', to_col(d, e)))  7.55 us
    ppermute x3, waiting for transfers between devices, local(): own[d] = lax.ppermute(row_pair, 'col', along_z(-d))  6.38 us
  transfers between devices with their start and end apart: 45, of which 16 were waited for; matrix products, arithmetic and copies ran while one was open for 1% of the time, Pallas kernels for 14%

profile of v4, /device:TPU:0, one launch (start us, length us, event | category | flops | bytes accessed | tf_op | source)
XLA Modules:
  0.0 103.7 jit_solution(9971859102864361896)
XLA Ops:
  0.6 1.7 %collective-permute-start = (bf16[128,512]{1,0:T(8,128)(2,1)}, bf16[128,512]{1,0:T(8,128)(2,1)S(1)}, u32[]{:S(2)}, u32[]{:S(2)}) collective-permute-start(bf16[128,512]{1,0:T(8,128)(2,1)} %param.6), channel_id=1, source_target_pairs={{0,2},{1,3},{2,0},{3,1},{4,6},{5,7},{6,4},{7,5},{8,10},{9,11},{10,... | collective-permute-start | bytes 393224 | tf_op jit(solution)/shard_map/gather_in/ppermute | solution.py:203
  2.4 2.9 %collective-permute-start.1 = (bf16[128,512]{1,0:T(8,128)(2,1)}, bf16[128,512]{1,0:T(8,128)(2,1)S(1)}, u32[]{:S(2)}, u32[]{:S(2)}) collective-permute-start(bf16[128,512]{1,0:T(8,128)(2,1)} %param.7), channel_id=1, source_target_pairs={{0,16},{16,0},{32,48},{48,32},{64,80},{80,64},{96,112},{112,96},{1... | collective-permute-start | bytes 393224 | tf_op jit(solution)/shard_map/gather_in/ppermute | solution.py:202
  6.1 4.2 %shard_map.59.counts = f32[16,128,1024]{2,1,0:T(8,128)S(1)} custom-call(s32[16]{0:T(128)S(1)} %stack.118.rows_ref, s32[8]{0:T(128)S(1)} %stack.127.place_ref, s32[4,8]{1,0:T(4,128)S(1)} %bitcast.121, s32[2048,1024]{1,0:T(8,128)} %counts.1), custom_call_target="tpu_custom_call" | custom-call | flops 2097152 | bytes 16777216 | tf_op jit(solution)/shard_map/pallas_call | solution.py:85
  10.4 1.1 %collective-permute-done.1 = bf16[128,512]{1,0:T(8,128)(2,1)S(1)} collective-permute-done((bf16[128,512]{1,0:T(8,128)(2,1)}, bf16[128,512]{1,0:T(8,128)(2,1)S(1)}, u32[]{:S(2)}, u32[]{:S(2)}) %collective-permute-start.1) | collective-permute-done | bytes 131104 | tf_op jit(solution)/shard_map/gather_in/ppermute | solution.py:202
  11.5 4.0 %collective-permute-start.8 = (bf16[2,128,512]{2,1,0:T(8,128)(2,1)S(1)}, bf16[2,128,512]{2,1,0:T(8,128)(2,1)S(1)}, u32[]{:S(2)}, u32[]{:S(2)}) collective-permute-start(bf16[2,128,512]{2,1,0:T(8,128)(2,1)S(1)} %pad_maximum_fusion), channel_id=1, source_target_pairs={{0,8},{1,9},{2,10},{3,11},{4,12},{5,13},{6,14},{7,15},{8,0},{9,1},... | collective-permute-start | bytes 786440 | tf_op jit(solution)/shard_map/gather_in/ppermute | solution.py:208
  15.5 0.7 collective-permute-start.10
  16.2 3.0 %collective-permute-start.3 = (bf16[2,128,512]{2,1,0:T(8,128)(2,1)S(1)}, bf16[2,128,512]{2,1,0:T(8,128)(2,1)S(1)}, u32[]{:S(2)}, u32[]{:S(2)}) collective-permute-start(bf16[2,128,512]{2,1,0:T(8,128)(2,1)S(1)} %pad_maximum_fusion.1), channel_id=1, source_target_pairs={{0,64},{16,80},{32,96},{48,112},{64,0},{80,16},{96,32},{112,48},{1... | collective-permute-start | bytes 786440 | tf_op jit(solution)/shard_map/gather_in/ppermute | solution.py:207
  19.3 1.2 %collective-permute-start.2 = (bf16[2,128,512]{2,1,0:T(8,128)(2,1)S(1)}, bf16[2,128,512]{2,1,0:T(8,128)(2,1)S(1)}, u32[]{:S(2)}, u32[]{:S(2)}) collective-permute-start(bf16[2,128,512]{2,1,0:T(8,128)(2,1)S(1)} %pad_maximum_fusion.1), channel_id=1, source_target_pairs={{0,96},{16,112},{32,0},{48,16},{64,32},{80,48},{96,64},{112,80},{1... | collective-permute-start | bytes 786440 | tf_op jit(solution)/shard_map/gather_in/ppermute | solution.py:207
  20.5 0.9 collective-permute-start.4
  21.4 2.9 %collective-permute-start.5 = (bf16[2,128,512]{2,1,0:T(8,128)(2,1)S(1)}, bf16[2,128,512]{2,1,0:T(8,128)(2,1)S(1)}, u32[]{:S(2)}, u32[]{:S(2)}) collective-permute-start(bf16[2,128,512]{2,1,0:T(8,128)(2,1)S(1)} %pad_maximum_fusion), channel_id=1, source_target_pairs={{0,4},{1,5},{2,6},{3,7},{4,8},{5,9},{6,10},{7,11},{8,12},{9,13},{1... | collective-permute-start | bytes 786440 | tf_op jit(solution)/shard_map/gather_in/ppermute | solution.py:208
  24.3 3.0 %collective-permute-done.10 = bf16[2,128,512]{2,1,0:T(8,128)(2,1)S(1)} collective-permute-done((bf16[2,128,512]{2,1,0:T(8,128)(2,1)S(1)}, bf16[2,128,512]{2,1,0:T(8,128)(2,1)S(1)}, u32[]{:S(2)}, u32[]{:S(2)}) %collective-permute-start.10) | collective-permute-done | bytes 262176 | tf_op jit(solution)/shard_map/gather_in/ppermute | solution.py:208
  27.3 3.4 %collective-permute-done.5 = bf16[2,128,512]{2,1,0:T(8,128)(2,1)S(1)} collective-permute-done((bf16[2,128,512]{2,1,0:T(8,128)(2,1)S(1)}, bf16[2,128,512]{2,1,0:T(8,128)(2,1)S(1)}, u32[]{:S(2)}, u32[]{:S(2)}) %collective-permute-start.5) | collective-permute-done | bytes 262176 | tf_op jit(solution)/shard_map/gather_in/ppermute | solution.py:208
  31.6 0.7 collective-permute-done.9
  32.3 0.8 reduce_rows.4
  33.3 1.3 %reduce_rows.5 = (f32[2,136,512]{2,1,0:T(8,128)S(1)}, f32[2,136,512]{2,1,0:T(8,128)S(1)}) custom-call(f32[16,128,1024]{2,1,0:T(8,128)S(1)} %shard_map.59.counts, bf16[8,128,512]{2,1,0:T(8,128)(2,1)S(1)} %constant_dynamic-update-slice_fusion.panel, bf16[128,512]{1,0:T(8,128)(2,1)S(1)} %get-tuple-element.72.refs_0_, ...), custom_call_target="tpu_custom_call" | custom-call | flops 1048576 | bytes 65536 | tf_op jit(solution)/shard_map/reduce_rows/pallas_call | solution.py:168
  35.2 1.3 %reduce_rows.7 = (f32[2,136,512]{2,1,0:T(8,128)S(1)}, f32[2,136,512]{2,1,0:T(8,128)S(1)}) custom-call(f32[16,128,1024]{2,1,0:T(8,128)S(1)} %shard_map.59.counts, bf16[8,128,512]{2,1,0:T(8,128)(2,1)S(1)} %constant_dynamic-update-slice_fusion.panel, bf16[128,512]{1,0:T(8,128)(2,1)S(1)} %get-tuple-element.67.refs_0_, ...), custom_call_target="tpu_custom_call" | custom-call | flops 1048576 | bytes 65536 | tf_op jit(solution)/shard_map/reduce_rows/pallas_call | solution.py:168
  37.5 1.9 %reduce_rows.6 = (f32[3,136,512]{2,1,0:T(8,128)S(1)}, f32[3,136,512]{2,1,0:T(8,128)S(1)}) custom-call(f32[16,128,1024]{2,1,0:T(8,128)S(1)} %shard_map.59.counts, bf16[8,128,512]{2,1,0:T(8,128)(2,1)S(1)} %constant_dynamic-update-slice_fusion.panel, bf16[128,512]{1,0:T(8,128)(2,1)S(1)} %get-tuple-element.64.refs_0_, ...), custom_call_target="tpu_custom_call" | custom-call | flops 1048576 | bytes 65536 | tf_op jit(solution)/shard_map/reduce_rows/pallas_call | solution.py:168
  39.8 2.6 %collective-permute-start.16 = (f16[136,512]{1,0:T(8,128)(2,1)S(1)}, f16[136,512]{1,0:T(8,128)(2,1)S(1)}, u32[]{:S(2)}, u32[]{:S(2)}) collective-permute-start(f16[136,512]{1,0:T(8,128)(2,1)S(1)} %get-tuple-element.57), channel_id=1, source_target_pairs={{0,8},{1,9},{2,10},{3,11},{4,12},{5,13},{6,14},{7,15},{8,0},{9,1},... | collective-permute-start | bytes 417800 | tf_op jit(solution)/shard_map/reduce_rows/ppermute | solution.py:227
  42.4 1.3 %collective-permute-start.17 = (f16[136,512]{1,0:T(8,128)(2,1)S(1)}, f16[136,512]{1,0:T(8,128)(2,1)S(1)}, u32[]{:S(2)}, u32[]{:S(2)}) collective-permute-start(f16[136,512]{1,0:T(8,128)(2,1)S(1)} %get-tuple-element.58), channel_id=1, source_target_pairs={{0,6},{1,7},{2,4},{3,5},{4,10},{5,11},{6,8},{7,9},{8,14},{9,15},{1... | collective-permute-start | bytes 417800 | tf_op jit(solution)/shard_map/reduce_rows/ppermute | solution.py:227
  43.8 1.1 %collective-permute-start.19 = (f16[136,512]{1,0:T(8,128)(2,1)S(1)}, f16[136,512]{1,0:T(8,128)(2,1)S(1)}, u32[]{:S(2)}, u32[]{:S(2)}) collective-permute-start(f16[136,512]{1,0:T(8,128)(2,1)S(1)} %get-tuple-element.59), channel_id=1, source_target_pairs={{0,4},{1,5},{2,6},{3,7},{4,8},{5,9},{6,10},{7,11},{8,12},{9,13},{1... | collective-permute-start | bytes 417800 | tf_op jit(solution)/shard_map/reduce_rows/ppermute | solution.py:227
  44.9 2.3 %collective-permute-start.20 = (f16[136,512]{1,0:T(8,128)(2,1)S(1)}, f16[136,512]{1,0:T(8,128)(2,1)S(1)}, u32[]{:S(2)}, u32[]{:S(2)}) collective-permute-start(f16[136,512]{1,0:T(8,128)(2,1)S(1)} %get-tuple-element.60), channel_id=1, source_target_pairs={{0,14},{1,15},{2,12},{3,13},{4,2},{5,3},{6,0},{7,1},{8,6},{9,7},{1... | collective-permute-start | bytes 417800 | tf_op jit(solution)/shard_map/reduce_rows/ppermute | solution.py:227
  47.5 1.7 %collective-permute-start.21 = (f16[136,512]{1,0:T(8,128)(2,1)S(1)}, f16[136,512]{1,0:T(8,128)(2,1)S(1)}, u32[]{:S(2)}, u32[]{:S(2)}) collective-permute-start(f16[136,512]{1,0:T(8,128)(2,1)S(1)} %get-tuple-element.55), channel_id=1, source_target_pairs={{0,12},{1,13},{2,14},{3,15},{4,0},{5,1},{6,2},{7,3},{8,4},{9,5},{1... | collective-permute-start | bytes 417800 | tf_op jit(solution)/shard_map/reduce_rows/ppermute | solution.py:227
  49.1 2.3 %collective-permute-done.16 = f16[136,512]{1,0:T(8,128)(2,1)S(1)} collective-permute-done((f16[136,512]{1,0:T(8,128)(2,1)S(1)}, f16[136,512]{1,0:T(8,128)(2,1)S(1)}, u32[]{:S(2)}, u32[]{:S(2)}) %collective-permute-start.16) | collective-permute-done | bytes 139296 | tf_op jit(solution)/shard_map/reduce_rows/ppermute | solution.py:227
  51.6 2.6 %collective-permute-done.19 = f16[136,512]{1,0:T(8,128)(2,1)S(1)} collective-permute-done((f16[136,512]{1,0:T(8,128)(2,1)S(1)}, f16[136,512]{1,0:T(8,128)(2,1)S(1)}, u32[]{:S(2)}, u32[]{:S(2)}) %collective-permute-start.19) | collective-permute-done | bytes 139296 | tf_op jit(solution)/shard_map/reduce_rows/ppermute | solution.py:227
  54.2 0.8 collective-permute-done.21
  55.0 1.9 %collective-permute-done.22 = f16[136,512]{1,0:T(8,128)(2,1)S(1)} collective-permute-done((f16[136,512]{1,0:T(8,128)(2,1)S(1)}, f16[136,512]{1,0:T(8,128)(2,1)S(1)}, u32[]{:S(2)}, u32[]{:S(2)}) %collective-permute-start.22) | collective-permute-done | bytes 139296 | tf_op jit(solution)/shard_map/reduce_rows/ppermute | solution.py:227
  57.2 3.3 %collective-permute-start.29 = (bf16[128,512]{1,0:T(8,128)(2,1)S(1)}, bf16[128,512]{1,0:T(8,128)(2,1)S(1)}, u32[]{:S(2)}, u32[]{:S(2)}) collective-permute-start(bf16[128,512]{1,0:T(8,128)(2,1)S(1)} %fusion.17.a0), channel_id=1, source_target_pairs={{0,10},{1,11},{2,8},{3,9},{4,14},{5,15},{6,12},{7,13},{8,2},{9,3},... | collective-permute-start | bytes 393224 | tf_op jit(solution)/shard_map/gather_new/ppermute | solution.py:238
  60.5 2.1 %collective-permute-start.26 = (bf16[128,512]{1,0:T(8,128)(2,1)S(1)}, bf16[128,512]{1,0:T(8,128)(2,1)S(1)}, u32[]{:S(2)}, u32[]{:S(2)}) collective-permute-start(bf16[128,512]{1,0:T(8,128)(2,1)S(1)} %fusion.17.a0), channel_id=1, source_target_pairs={{0,14},{1,15},{2,12},{3,13},{4,2},{5,3},{6,0},{7,1},{8,6},{9,7},{1... | collective-permute-start | bytes 393224 | tf_op jit(solution)/shard_map/gather_new/ppermute | solution.py:238
  62.6 0.8 collective-permute-start.34
  63.4 1.3 %collective-permute-done.29.a1 = bf16[128,512]{1,0:T(8,128)(2,1)S(1)} collective-permute-done((bf16[128,512]{1,0:T(8,128)(2,1)S(1)}, bf16[128,512]{1,0:T(8,128)(2,1)S(1)}, u32[]{:S(2)}, u32[]{:S(2)}) %collective-permute-start.29) | collective-permute-done | bytes 131104 | tf_op jit(solution)/shard_map/gather_new/ppermute | solution.py:238
  64.7 1.7 %collective-permute-start.35 = (bf16[128,512]{1,0:T(8,128)(2,1)S(1)}, bf16[128,512]{1,0:T(8,128)(2,1)S(1)}, u32[]{:S(2)}, u32[]{:S(2)}) collective-permute-start(bf16[128,512]{1,0:T(8,128)(2,1)S(1)} %fusion.17.a0), channel_id=1, source_target_pairs={{0,12},{1,13},{2,14},{3,15},{4,0},{5,1},{6,2},{7,3},{8,4},{9,5},{1... | collective-permute-start | bytes 393224 | tf_op jit(solution)/shard_map/gather_new/ppermute | solution.py:238
  66.4 1.4 %collective-permute-done.25.a0 = bf16[128,512]{1,0:T(8,128)(2,1)S(1)} collective-permute-done((bf16[128,512]{1,0:T(8,128)(2,1)S(1)}, bf16[128,512]{1,0:T(8,128)(2,1)S(1)}, u32[]{:S(2)}, u32[]{:S(2)}) %collective-permute-start.25) | collective-permute-done | bytes 131104 | tf_op jit(solution)/shard_map/gather_new/ppermute | solution.py:238
  68.4 3.5 %collective-permute-done.34.a0 = bf16[128,512]{1,0:T(8,128)(2,1)S(1)} collective-permute-done((bf16[128,512]{1,0:T(8,128)(2,1)S(1)}, bf16[128,512]{1,0:T(8,128)(2,1)S(1)}, u32[]{:S(2)}, u32[]{:S(2)}) %collective-permute-start.34) | collective-permute-done | bytes 131104 | tf_op jit(solution)/shard_map/gather_new/ppermute | solution.py:238
  71.9 1.2 %collective-permute-start.23 = (bf16[128,512]{1,0:T(8,128)(2,1)S(1)}, bf16[128,512]{1,0:T(8,128)(2,1)S(1)}, u32[]{:S(2)}, u32[]{:S(2)}) collective-permute-start(bf16[128,512]{1,0:T(8,128)(2,1)S(1)} %fusion.17.a0), channel_id=1, source_target_pairs={{0,4},{1,5},{2,6},{3,7},{4,8},{5,9},{6,10},{7,11},{8,12},{9,13},{1... | collective-permute-start | bytes 393224 | tf_op jit(solution)/shard_map/gather_new/ppermute | solution.py:238
  73.1 1.4 %gather_new.4 = (f32[8,136,512]{2,1,0:T(8,128)S(1)}, f32[8,512]{1,0:T(8,128)S(1)}) custom-call(f32[16,128,1024]{2,1,0:T(8,128)S(1)} %shard_map.59.counts, bf16[128,512]{1,0:T(8,128)(2,1)S(1)} %fusion.17.a0, bf16[128,512]{1,0:T(8,128)(2,1)S(1)} %collective-permute-done.29.a1, bf16[128,512]{1,0:T(8,128)(2,1)S(1)} %collective-permute-done.30.b0, ...), custom_call_target="tpu_custom_call" | custom-call | flops 1048576 | bytes 65536 | tf_op jit(solution)/shard_map/gather_new/pallas_call | solution.py:168
  74.5 1.5 %gather_new.5 = (f32[8,136,512]{2,1,0:T(8,128)S(1)}, f32[8,512]{1,0:T(8,128)S(1)}) custom-call(f32[16,128,1024]{2,1,0:T(8,128)S(1)} %shard_map.59.counts, bf16[128,512]{1,0:T(8,128)(2,1)S(1)} %collective-permute-done.25.a0, bf16[128,512]{1,0:T(8,128)(2,1)S(1)} %collective-permute-done.26.a1, ...), custom_call_target="tpu_custom_call", output_to_operand_aliasing={{0}: (6, {}), {1}: (7, {})} | custom-call | flops 1048576 | bytes 65536 | tf_op jit(solution)/shard_map/gather_new/pallas_call | solution.py:168
  76.1 0.8 collective-permute-done.24.a1
  77.4 0.7 collective-permute-done.23.a0
  78.6 1.5 %gather_new.6 = (f32[8,136,512]{2,1,0:T(8,128)S(1)}, f32[8,512]{1,0:T(8,128)S(1)}) custom-call(f32[16,128,1024]{2,1,0:T(8,128)S(1)} %shard_map.59.counts, bf16[128,512]{1,0:T(8,128)(2,1)S(1)} %collective-permute-done.34.a0, bf16[128,512]{1,0:T(8,128)(2,1)S(1)} %collective-permute-done.35.a1, ...), custom_call_target="tpu_custom_call", output_to_operand_aliasing={{0}: (6, {}), {1}: (7, {})} | custom-call | flops 1048576 | bytes 65536 | tf_op jit(solution)/shard_map/gather_new/pallas_call | solution.py:168
  80.1 1.5 %gather_new.7 = (f32[8,136,512]{2,1,0:T(8,128)S(1)}, f32[8,512]{1,0:T(8,128)S(1)}) custom-call(f32[16,128,1024]{2,1,0:T(8,128)S(1)} %shard_map.59.counts, bf16[128,512]{1,0:T(8,128)(2,1)S(1)} %collective-permute-done.23.a0, bf16[128,512]{1,0:T(8,128)(2,1)S(1)} %collective-permute-done.24.a1, ...), custom_call_target="tpu_custom_call", output_to_operand_aliasing={{0}: (6, {}), {1}: (7, {})} | custom-call | flops 1048576 | bytes 65536 | tf_op jit(solution)/shard_map/gather_new/pallas_call | solution.py:168
  81.9 4.2 %collective-permute-start.38 = (f16[136,512]{1,0:T(8,128)(2,1)S(1)}, f16[136,512]{1,0:T(8,128)(2,1)S(1)}, u32[]{:S(2)}, u32[]{:S(2)}) collective-permute-start(f16[136,512]{1,0:T(8,128)(2,1)S(1)} %get-tuple-element.48), channel_id=1, source_target_pairs={{0,80},{16,64},{32,112},{48,96},{64,16},{80,0},{96,48},{112,32},{1... | collective-permute-start | bytes 417800 | tf_op jit(solution)/shard_map/reduce_columns/ppermute | solution.py:264
  86.7 2.8 %collective-permute-start.40 = (f16[136,512]{1,0:T(8,128)(2,1)S(1)}, f16[136,512]{1,0:T(8,128)(2,1)S(1)}, u32[]{:S(2)}, u32[]{:S(2)}) collective-permute-start(f16[136,512]{1,0:T(8,128)(2,1)S(1)} %get-tuple-element.53), channel_id=1, source_target_pairs={{0,48},{16,32},{32,80},{48,64},{64,112},{80,96},{96,16},{112,0},{1... | collective-permute-start | bytes 417800 | tf_op jit(solution)/shard_map/reduce_columns/ppermute | solution.py:264
  89.4 2.9 %collective-permute-start.41 = (f16[136,512]{1,0:T(8,128)(2,1)S(1)}, f16[136,512]{1,0:T(8,128)(2,1)S(1)}, u32[]{:S(2)}, u32[]{:S(2)}) collective-permute-start(f16[136,512]{1,0:T(8,128)(2,1)S(1)} %get-tuple-element.52), channel_id=1, source_target_pairs={{0,112},{16,96},{32,16},{48,0},{64,48},{80,32},{96,80},{112,64},{1... | collective-permute-start | bytes 417800 | tf_op jit(solution)/shard_map/reduce_columns/ppermute | solution.py:264
  92.5 3.0 %collective-permute-start.43 = (f16[136,512]{1,0:T(8,128)(2,1)S(1)}, f16[136,512]{1,0:T(8,128)(2,1)S(1)}, u32[]{:S(2)}, u32[]{:S(2)}) collective-permute-start(f16[136,512]{1,0:T(8,128)(2,1)S(1)} %get-tuple-element.50), channel_id=1, source_target_pairs={{0,96},{16,112},{32,0},{48,16},{64,32},{80,48},{96,64},{112,80},{1... | collective-permute-start | bytes 417800 | tf_op jit(solution)/shard_map/reduce_columns/ppermute | solution.py:264
  95.5 1.8 %collective-permute-start.44 = (f16[136,512]{1,0:T(8,128)(2,1)S(1)}, f16[136,512]{1,0:T(8,128)(2,1)S(1)}, u32[]{:S(2)}, u32[]{:S(2)}) collective-permute-start(f16[136,512]{1,0:T(8,128)(2,1)S(1)} %get-tuple-element.49), channel_id=1, source_target_pairs={{0,16},{16,0},{32,48},{48,32},{64,80},{80,64},{96,112},{112,96},{1... | collective-permute-start | bytes 417800 | tf_op jit(solution)/shard_map/reduce_columns/ppermute | solution.py:264
  97.4 1.9 %collective-permute-done.40 = f16[136,512]{1,0:T(8,128)(2,1)S(1)} collective-permute-done((f16[136,512]{1,0:T(8,128)(2,1)S(1)}, f16[136,512]{1,0:T(8,128)(2,1)S(1)}, u32[]{:S(2)}, u32[]{:S(2)}) %collective-permute-start.40) | collective-permute-done | bytes 139296 | tf_op jit(solution)/shard_map/reduce_columns/ppermute | solution.py:264
  99.8 2.9 %collective-permute-done.44 = f16[136,512]{1,0:T(8,128)(2,1)S(1)} collective-permute-done((f16[136,512]{1,0:T(8,128)(2,1)S(1)}, f16[136,512]{1,0:T(8,128)(2,1)S(1)}, u32[]{:S(2)}, u32[]{:S(2)}) %collective-permute-start.44) | collective-permute-done | bytes 139296 | tf_op jit(solution)/shard_map/reduce_columns/ppermute | solution.py:264
  103.0 0.7 fusion.18
  (89 shorter events, 8.1 us)
Async XLA Ops:
  0.6 9.7 %collective-permute-start = (bf16[128,512]{1,0:T(8,128)(2,1)}, bf16[128,512]{1,0:T(8,128)(2,1)S(1)}, u32[]{:S(2)}, u32[]{:S(2)}) collective-permute-start(bf16[128,512]{1,0:T(8,128)(2,1)} %param.6), channel_id=1, source_target_pairs={{0,2},{1,3},{2,0},{3,1},{4,6},{5,7},{6,4},{7,5},{8,10},{9,11},{10,... | collective-permute-start | bytes 393224 | tf_op jit(solution)/shard_map/gather_in/ppermute | solution.py:203
  2.4 9.1 %collective-permute-start.1 = (bf16[128,512]{1,0:T(8,128)(2,1)}, bf16[128,512]{1,0:T(8,128)(2,1)S(1)}, u32[]{:S(2)}, u32[]{:S(2)}) collective-permute-start(bf16[128,512]{1,0:T(8,128)(2,1)} %param.7), channel_id=1, source_target_pairs={{0,16},{16,0},{32,48},{48,32},{64,80},{80,64},{96,112},{112,96},{1... | collective-permute-start | bytes 393224 | tf_op jit(solution)/shard_map/gather_in/ppermute | solution.py:202
  6.1 4.2 %copy-start.2 = (bf16[128,512]{1,0:T(8,128)(2,1)S(1)}, bf16[128,512]{1,0:T(8,128)(2,1)}, u32[]{:S(2)}) copy-start(bf16[128,512]{1,0:T(8,128)(2,1)} %param.6) | copy-start | bytes 393220
  6.1 5.4 %copy-start.3 = (bf16[128,512]{1,0:T(8,128)(2,1)S(1)}, bf16[128,512]{1,0:T(8,128)(2,1)}, u32[]{:S(2)}) copy-start(bf16[128,512]{1,0:T(8,128)(2,1)} %param.7) | copy-start | bytes 393220
  11.5 9.8 %collective-permute-start.8 = (bf16[2,128,512]{2,1,0:T(8,128)(2,1)S(1)}, bf16[2,128,512]{2,1,0:T(8,128)(2,1)S(1)}, u32[]{:S(2)}, u32[]{:S(2)}) collective-permute-start(bf16[2,128,512]{2,1,0:T(8,128)(2,1)S(1)} %pad_maximum_fusion), channel_id=1, source_target_pairs={{0,8},{1,9},{2,10},{3,11},{4,12},{5,13},{6,14},{7,15},{8,0},{9,1},... | collective-permute-start | bytes 786440 | tf_op jit(solution)/shard_map/gather_in/ppermute | solution.py:208
  15.5 11.8 %collective-permute-start.10 = (bf16[2,128,512]{2,1,0:T(8,128)(2,1)S(1)}, bf16[2,128,512]{2,1,0:T(8,128)(2,1)S(1)}, u32[]{:S(2)}, u32[]{:S(2)}) collective-permute-start(bf16[2,128,512]{2,1,0:T(8,128)(2,1)S(1)} %pad_maximum_fusion), channel_id=1, source_target_pairs={{0,12},{1,13},{2,14},{3,15},{4,0},{5,1},{6,2},{7,3},{8,4},{9,5},{1... | collective-permute-start | bytes 786440 | tf_op jit(solution)/shard_map/gather_in/ppermute | solution.py:208
  16.2 15.2 %collective-permute-start.3 = (bf16[2,128,512]{2,1,0:T(8,128)(2,1)S(1)}, bf16[2,128,512]{2,1,0:T(8,128)(2,1)S(1)}, u32[]{:S(2)}, u32[]{:S(2)}) collective-permute-start(bf16[2,128,512]{2,1,0:T(8,128)(2,1)S(1)} %pad_maximum_fusion.1), channel_id=1, source_target_pairs={{0,64},{16,80},{32,96},{48,112},{64,0},{80,16},{96,32},{112,48},{1... | collective-permute-start | bytes 786440 | tf_op jit(solution)/shard_map/gather_in/ppermute | solution.py:207
  19.3 11.5 %collective-permute-start.2 = (bf16[2,128,512]{2,1,0:T(8,128)(2,1)S(1)}, bf16[2,128,512]{2,1,0:T(8,128)(2,1)S(1)}, u32[]{:S(2)}, u32[]{:S(2)}) collective-permute-start(bf16[2,128,512]{2,1,0:T(8,128)(2,1)S(1)} %pad_maximum_fusion.1), channel_id=1, source_target_pairs={{0,96},{16,112},{32,0},{48,16},{64,32},{80,48},{96,64},{112,80},{1... | collective-permute-start | bytes 786440 | tf_op jit(solution)/shard_map/gather_in/ppermute | solution.py:207
  20.5 11.0 %collective-permute-start.4 = (bf16[2,128,512]{2,1,0:T(8,128)(2,1)S(1)}, bf16[2,128,512]{2,1,0:T(8,128)(2,1)S(1)}, u32[]{:S(2)}, u32[]{:S(2)}) collective-permute-start(bf16[2,128,512]{2,1,0:T(8,128)(2,1)S(1)} %pad_maximum_fusion.1), channel_id=1, source_target_pairs={{0,32},{16,48},{32,64},{48,80},{64,96},{80,112},{96,0},{112,16},{1... | collective-permute-start | bytes 786440 | tf_op jit(solution)/shard_map/gather_in/ppermute | solution.py:207
  21.4 9.4 %collective-permute-start.5 = (bf16[2,128,512]{2,1,0:T(8,128)(2,1)S(1)}, bf16[2,128,512]{2,1,0:T(8,128)(2,1)S(1)}, u32[]{:S(2)}, u32[]{:S(2)}) collective-permute-start(bf16[2,128,512]{2,1,0:T(8,128)(2,1)S(1)} %pad_maximum_fusion), channel_id=1, source_target_pairs={{0,4},{1,5},{2,6},{3,7},{4,8},{5,9},{6,10},{7,11},{8,12},{9,13},{1... | collective-permute-start | bytes 786440 | tf_op jit(solution)/shard_map/gather_in/ppermute | solution.py:208
  27.3 7.8 %collective-permute-start.7 = (bf16[2,128,512]{2,1,0:T(8,128)(2,1)S(1)}, bf16[2,128,512]{2,1,0:T(8,128)(2,1)S(1)}, u32[]{:S(2)}, u32[]{:S(2)}) collective-permute-start(bf16[2,128,512]{2,1,0:T(8,128)(2,1)S(1)} %pad_maximum_fusion), channel_id=1, source_target_pairs={{0,1},{1,0},{2,3},{3,2},{4,5},{5,4},{6,7},{7,6},{8,9},{9,8},{10,11... | collective-permute-start | bytes 786440 | tf_op jit(solution)/shard_map/gather_in/ppermute | solution.py:52
  30.7 1.5 %collective-permute-start.9 = (bf16[2,128,512]{2,1,0:T(8,128)(2,1)S(1)}, bf16[2,128,512]{2,1,0:T(8,128)(2,1)S(1)}, u32[]{:S(2)}, u32[]{:S(2)}) collective-permute-start(bf16[2,128,512]{2,1,0:T(8,128)(2,1)S(1)} %collective-permute-done.8), channel_id=1, source_target_pairs={{0,1},{1,0},{2,3},{3,2},{4,5},{5,4},{6,7},{7,6},{8,9},{9,8},{10,11... | collective-permute-start | bytes 786440 | tf_op jit(solution)/shard_map/gather_in/ppermute | solution.py:52
  30.8 2.5 %collective-permute-start.11 = (bf16[2,128,512]{2,1,0:T(8,128)(2,1)S(1)}, bf16[2,128,512]{2,1,0:T(8,128)(2,1)S(1)}, u32[]{:S(2)}, u32[]{:S(2)}) collective-permute-start(bf16[2,128,512]{2,1,0:T(8,128)(2,1)S(1)} %collective-permute-done.10), channel_id=1, source_target_pairs={{0,1},{1,0},{2,3},{3,2},{4,5},{5,4},{6,7},{7,6},{8,9},{9,8},{10,11... | collective-permute-start | bytes 786440 | tf_op jit(solution)/shard_map/gather_in/ppermute | solution.py:52
  31.4 3.8 %collective-permute-start.6 = (bf16[2,128,512]{2,1,0:T(8,128)(2,1)S(1)}, bf16[2,128,512]{2,1,0:T(8,128)(2,1)S(1)}, u32[]{:S(2)}, u32[]{:S(2)}) collective-permute-start(bf16[2,128,512]{2,1,0:T(8,128)(2,1)S(1)} %collective-permute-done.5), channel_id=1, source_target_pairs={{0,1},{1,0},{2,3},{3,2},{4,5},{5,4},{6,7},{7,6},{8,9},{9,8},{10,11... | collective-permute-start | bytes 786440 | tf_op jit(solution)/shard_map/gather_in/ppermute | solution.py:52
  33.1 2.1 %collective-permute-start.14 = (f32[1,136,512]{2,1,0:T(8,128)S(1)}, f32[1,136,512]{2,1,0:T(8,128)S(1)}, u32[]{:S(2)}, u32[]{:S(2)}) collective-permute-start(f32[1,136,512]{2,1,0:T(8,128)S(1)} %get-tuple-element.31), channel_id=1, source_target_pairs={{0,1},{1,0},{2,3},{3,2},{4,5},{5,4},{6,7},{7,6},{8,9},{9,8},{10,11... | collective-permute-start | bytes 835592 | tf_op jit(solution)/shard_map/reduce_rows/ppermute | solution.py:52
  34.7 2.8 %collective-permute-start.12 = (f32[2,136,512]{2,1,0:T(8,128)S(1)}, f32[2,136,512]{2,1,0:T(8,128)S(1)}, u32[]{:S(2)}, u32[]{:S(2)}) collective-permute-start(f32[2,136,512]{2,1,0:T(8,128)S(1)} %get-tuple-element.28), channel_id=1, source_target_pairs={{0,1},{1,0},{2,3},{3,2},{4,5},{5,4},{6,7},{7,6},{8,9},{9,8},{10,11... | collective-permute-start | bytes 1671176 | tf_op jit(solution)/shard_map/reduce_rows/ppermute | solution.py:52
  36.6 7.1 %collective-permute-start.18 = (f32[2,136,512]{2,1,0:T(8,128)S(1)}, f32[2,136,512]{2,1,0:T(8,128)S(1)}, u32[]{:S(2)}, u32[]{:S(2)}) collective-permute-start(f32[2,136,512]{2,1,0:T(8,128)S(1)} %get-tuple-element.34), channel_id=1, source_target_pairs={{0,1},{1,0},{2,3},{3,2},{4,5},{5,4},{6,7},{7,6},{8,9},{9,8},{10,11... | collective-permute-start | bytes 1671176 | tf_op jit(solution)/shard_map/reduce_rows/ppermute | solution.py:52
  36.8 10.6 %collective-permute-start.15 = (f16[136,512]{1,0:T(8,128)(2,1)S(1)}, f16[136,512]{1,0:T(8,128)(2,1)S(1)}, u32[]{:S(2)}, u32[]{:S(2)}) collective-permute-start(f16[136,512]{1,0:T(8,128)(2,1)S(1)} %fusion.19), channel_id=1, source_target_pairs={{0,10},{1,11},{2,8},{3,9},{4,14},{5,15},{6,12},{7,13},{8,2},{9,3},... | collective-permute-start | bytes 417800 | tf_op jit(solution)/shard_map/reduce_rows/ppermute | solution.py:227
  39.4 5.5 %collective-permute-start.13 = (f32[3,136,512]{2,1,0:T(8,128)S(1)}, f32[3,136,512]{2,1,0:T(8,128)S(1)}, u32[]{:S(2)}, u32[]{:S(2)}) collective-permute-start(f32[3,136,512]{2,1,0:T(8,128)S(1)} %get-tuple-element.30), channel_id=1, source_target_pairs={{0,1},{1,0},{2,3},{3,2},{4,5},{5,4},{6,7},{7,6},{8,9},{9,8},{10,11... | collective-permute-start | bytes 2506760 | tf_op jit(solution)/shard_map/reduce_rows/ppermute | solution.py:52
  39.8 11.6 %collective-permute-start.16 = (f16[136,512]{1,0:T(8,128)(2,1)S(1)}, f16[136,512]{1,0:T(8,128)(2,1)S(1)}, u32[]{:S(2)}, u32[]{:S(2)}) collective-permute-start(f16[136,512]{1,0:T(8,128)(2,1)S(1)} %get-tuple-element.57), channel_id=1, source_target_pairs={{0,8},{1,9},{2,10},{3,11},{4,12},{5,13},{6,14},{7,15},{8,0},{9,1},... | collective-permute-start | bytes 417800 | tf_op jit(solution)/shard_map/reduce_rows/ppermute | solution.py:227
  42.4 9.2 %collective-permute-start.17 = (f16[136,512]{1,0:T(8,128)(2,1)S(1)}, f16[136,512]{1,0:T(8,128)(2,1)S(1)}, u32[]{:S(2)}, u32[]{:S(2)}) collective-permute-start(f16[136,512]{1,0:T(8,128)(2,1)S(1)} %get-tuple-element.58), channel_id=1, source_target_pairs={{0,6},{1,7},{2,4},{3,5},{4,10},{5,11},{6,8},{7,9},{8,14},{9,15},{1... | collective-permute-start | bytes 417800 | tf_op jit(solution)/shard_map/reduce_rows/ppermute | solution.py:227
  43.8 10.4 %collective-permute-start.19 = (f16[136,512]{1,0:T(8,128)(2,1)S(1)}, f16[136,512]{1,0:T(8,128)(2,1)S(1)}, u32[]{:S(2)}, u32[]{:S(2)}) collective-permute-start(f16[136,512]{1,0:T(8,128)(2,1)S(1)} %get-tuple-element.59), channel_id=1, source_target_pairs={{0,4},{1,5},{2,6},{3,7},{4,8},{5,9},{6,10},{7,11},{8,12},{9,13},{1... | collective-permute-start | bytes 417800 | tf_op jit(solution)/shard_map/reduce_rows/ppermute | solution.py:227
  44.9 9.3 %collective-permute-start.20 = (f16[136,512]{1,0:T(8,128)(2,1)S(1)}, f16[136,512]{1,0:T(8,128)(2,1)S(1)}, u32[]{:S(2)}, u32[]{:S(2)}) collective-permute-start(f16[136,512]{1,0:T(8,128)(2,1)S(1)} %get-tuple-element.60), channel_id=1, source_target_pairs={{0,14},{1,15},{2,12},{3,13},{4,2},{5,3},{6,0},{7,1},{8,6},{9,7},{1... | collective-permute-start | bytes 417800 | tf_op jit(solution)/shard_map/reduce_rows/ppermute | solution.py:227
  47.5 7.5 %collective-permute-start.21 = (f16[136,512]{1,0:T(8,128)(2,1)S(1)}, f16[136,512]{1,0:T(8,128)(2,1)S(1)}, u32[]{:S(2)}, u32[]{:S(2)}) collective-permute-start(f16[136,512]{1,0:T(8,128)(2,1)S(1)} %get-tuple-element.55), channel_id=1, source_target_pairs={{0,12},{1,13},{2,14},{3,15},{4,0},{5,1},{6,2},{7,3},{8,4},{9,5},{1... | collective-permute-start | bytes 417800 | tf_op jit(solution)/shard_map/reduce_rows/ppermute | solution.py:227
  51.4 5.5 %collective-permute-start.22 = (f16[136,512]{1,0:T(8,128)(2,1)S(1)}, f16[136,512]{1,0:T(8,128)(2,1)S(1)}, u32[]{:S(2)}, u32[]{:S(2)}) collective-permute-start(f16[136,512]{1,0:T(8,128)(2,1)S(1)} %get-tuple-element.56), channel_id=1, source_target_pairs={{0,2},{1,3},{2,0},{3,1},{4,6},{5,7},{6,4},{7,5},{8,10},{9,11},{10,... | collective-permute-start | bytes 417800 | tf_op jit(solution)/shard_map/reduce_rows/ppermute | solution.py:227
  57.1 17.4 %copy-start = (bf16[128,512]{1,0:T(8,128)(2,1)}, bf16[128,512]{1,0:T(8,128)(2,1)S(1)}, u32[]{:S(2)}) copy-start(bf16[128,512]{1,0:T(8,128)(2,1)S(1)} %fusion.17.a0) | copy-start | bytes 393220
  57.2 7.5 %collective-permute-start.29 = (bf16[128,512]{1,0:T(8,128)(2,1)S(1)}, bf16[128,512]{1,0:T(8,128)(2,1)S(1)}, u32[]{:S(2)}, u32[]{:S(2)}) collective-permute-start(bf16[128,512]{1,0:T(8,128)(2,1)S(1)} %fusion.17.a0), channel_id=1, source_target_pairs={{0,10},{1,11},{2,8},{3,9},{4,14},{5,15},{6,12},{7,13},{8,2},{9,3},... | collective-permute-start | bytes 393224 | tf_op jit(solution)/shard_map/gather_new/ppermute | solution.py:238
  60.4 4.3 %collective-permute-start.30 = (bf16[128,512]{1,0:T(8,128)(2,1)S(1)}, bf16[128,512]{1,0:T(8,128)(2,1)S(1)}, u32[]{:S(2)}, u32[]{:S(2)}) collective-permute-start(bf16[128,512]{1,0:T(8,128)(2,1)S(1)} %fusion.17.a0), channel_id=1, source_target_pairs={{0,1},{1,0},{2,3},{3,2},{4,5},{5,4},{6,7},{7,6},{8,9},{9,8},{10,11... | collective-permute-start | bytes 393224 | tf_op jit(solution)/shard_map/gather_new/ppermute | solution.py:52
  60.4 7.4 %collective-permute-start.25 = (bf16[128,512]{1,0:T(8,128)(2,1)S(1)}, bf16[128,512]{1,0:T(8,128)(2,1)S(1)}, u32[]{:S(2)}, u32[]{:S(2)}) collective-permute-start(bf16[128,512]{1,0:T(8,128)(2,1)S(1)} %fusion.17.a0), channel_id=1, source_target_pairs={{0,8},{1,9},{2,10},{3,11},{4,12},{5,13},{6,14},{7,15},{8,0},{9,1},... | collective-permute-start | bytes 393224 | tf_op jit(solution)/shard_map/gather_new/ppermute | solution.py:238
  60.5 7.4 %collective-permute-start.26 = (bf16[128,512]{1,0:T(8,128)(2,1)S(1)}, bf16[128,512]{1,0:T(8,128)(2,1)S(1)}, u32[]{:S(2)}, u32[]{:S(2)}) collective-permute-start(bf16[128,512]{1,0:T(8,128)(2,1)S(1)} %fusion.17.a0), channel_id=1, source_target_pairs={{0,14},{1,15},{2,12},{3,13},{4,2},{5,3},{6,0},{7,1},{8,6},{9,7},{1... | collective-permute-start | bytes 393224 | tf_op jit(solution)/shard_map/gather_new/ppermute | solution.py:238
  62.6 9.3 %collective-permute-start.34 = (bf16[128,512]{1,0:T(8,128)(2,1)S(1)}, bf16[128,512]{1,0:T(8,128)(2,1)S(1)}, u32[]{:S(2)}, u32[]{:S(2)}) collective-permute-start(bf16[128,512]{1,0:T(8,128)(2,1)S(1)} %fusion.17.a0), channel_id=1, source_target_pairs={{0,6},{1,7},{2,4},{3,5},{4,10},{5,11},{6,8},{7,9},{8,14},{9,15},{1... | collective-permute-start | bytes 393224 | tf_op jit(solution)/shard_map/gather_new/ppermute | solution.py:238
  64.7 7.2 %collective-permute-start.31 = (bf16[128,512]{1,0:T(8,128)(2,1)S(1)}, bf16[128,512]{1,0:T(8,128)(2,1)S(1)}, u32[]{:S(2)}, u32[]{:S(2)}) collective-permute-start(bf16[128,512]{1,0:T(8,128)(2,1)S(1)} %collective-permute-done.29.a1), channel_id=1, source_target_pairs={{0,1},{1,0},{2,3},{3,2},{4,5},{5,4},{6,7},{7,6},{8,9},{9,8},{10,11... | collective-permute-start | bytes 393224 | tf_op jit(solution)/shard_map/gather_new/ppermute | solution.py:52
  64.7 9.8 %collective-permute-start.35 = (bf16[128,512]{1,0:T(8,128)(2,1)S(1)}, bf16[128,512]{1,0:T(8,128)(2,1)S(1)}, u32[]{:S(2)}, u32[]{:S(2)}) collective-permute-start(bf16[128,512]{1,0:T(8,128)(2,1)S(1)} %fusion.17.a0), channel_id=1, source_target_pairs={{0,12},{1,13},{2,14},{3,15},{4,0},{5,1},{6,2},{7,3},{8,4},{9,5},{1... | collective-permute-start | bytes 393224 | tf_op jit(solution)/shard_map/gather_new/ppermute | solution.py:238
  67.8 6.7 %collective-permute-start.27 = (bf16[128,512]{1,0:T(8,128)(2,1)S(1)}, bf16[128,512]{1,0:T(8,128)(2,1)S(1)}, u32[]{:S(2)}, u32[]{:S(2)}) collective-permute-start(bf16[128,512]{1,0:T(8,128)(2,1)S(1)} %collective-permute-done.25.a0), channel_id=1, source_target_pairs={{0,1},{1,0},{2,3},{3,2},{4,5},{5,4},{6,7},{7,6},{8,9},{9,8},{10,11... | collective-permute-start | bytes 393224 | tf_op jit(solution)/shard_map/gather_new/ppermute | solution.py:52
  67.8 6.7 %collective-permute-start.28 = (bf16[128,512]{1,0:T(8,128)(2,1)S(1)}, bf16[128,512]{1,0:T(8,128)(2,1)S(1)}, u32[]{:S(2)}, u32[]{:S(2)}) collective-permute-start(bf16[128,512]{1,0:T(8,128)(2,1)S(1)} %collective-permute-done.26.a1), channel_id=1, source_target_pairs={{0,1},{1,0},{2,3},{3,2},{4,5},{5,4},{6,7},{7,6},{8,9},{9,8},{10,11... | collective-permute-start | bytes 393224 | tf_op jit(solution)/shard_map/gather_new/ppermute | solution.py:52
  71.9 5.0 %collective-permute-start.24 = (bf16[128,512]{1,0:T(8,128)(2,1)S(1)}, bf16[128,512]{1,0:T(8,128)(2,1)S(1)}, u32[]{:S(2)}, u32[]{:S(2)}) collective-permute-start(bf16[128,512]{1,0:T(8,128)(2,1)S(1)} %fusion.17.a0), channel_id=1, source_target_pairs={{0,2},{1,3},{2,0},{3,1},{4,6},{5,7},{6,4},{7,5},{8,10},{9,11},{10,... | collective-permute-start | bytes 393224 | tf_op jit(solution)/shard_map/gather_new/ppermute | solution.py:238
  71.9 6.2 %collective-permute-start.23 = (bf16[128,512]{1,0:T(8,128)(2,1)S(1)}, bf16[128,512]{1,0:T(8,128)(2,1)S(1)}, u32[]{:S(2)}, u32[]{:S(2)}) collective-permute-start(bf16[128,512]{1,0:T(8,128)(2,1)S(1)} %fusion.17.a0), channel_id=1, source_target_pairs={{0,4},{1,5},{2,6},{3,7},{4,8},{5,9},{6,10},{7,11},{8,12},{9,13},{1... | collective-permute-start | bytes 393224 | tf_op jit(solution)/shard_map/gather_new/ppermute | solution.py:238
  76.8 1.7 %collective-permute-start.36 = (bf16[128,512]{1,0:T(8,128)(2,1)S(1)}, bf16[128,512]{1,0:T(8,128)(2,1)S(1)}, u32[]{:S(2)}, u32[]{:S(2)}) collective-permute-start(bf16[128,512]{1,0:T(8,128)(2,1)S(1)} %collective-permute-done.34.a0), channel_id=1, source_target_pairs={{0,1},{1,0},{2,3},{3,2},{4,5},{5,4},{6,7},{7,6},{8,9},{9,8},{10,11... | collective-permute-start | bytes 393224 | tf_op jit(solution)/shard_map/gather_new/ppermute | solution.py:52
  76.8 1.7 %collective-permute-start.37 = (bf16[128,512]{1,0:T(8,128)(2,1)S(1)}, bf16[128,512]{1,0:T(8,128)(2,1)S(1)}, u32[]{:S(2)}, u32[]{:S(2)}) collective-permute-start(bf16[128,512]{1,0:T(8,128)(2,1)S(1)} %collective-permute-done.35.a1), channel_id=1, source_target_pairs={{0,1},{1,0},{2,3},{3,2},{4,5},{5,4},{6,7},{7,6},{8,9},{9,8},{10,11... | collective-permute-start | bytes 393224 | tf_op jit(solution)/shard_map/gather_new/ppermute | solution.py:52
  78.1 2.0 %collective-permute-start.33 = (bf16[128,512]{1,0:T(8,128)(2,1)S(1)}, bf16[128,512]{1,0:T(8,128)(2,1)S(1)}, u32[]{:S(2)}, u32[]{:S(2)}) collective-permute-start(bf16[128,512]{1,0:T(8,128)(2,1)S(1)} %collective-permute-done.24.a1), channel_id=1, source_target_pairs={{0,1},{1,0},{2,3},{3,2},{4,5},{5,4},{6,7},{7,6},{8,9},{9,8},{10,11... | collective-permute-start | bytes 393224 | tf_op jit(solution)/shard_map/gather_new/ppermute | solution.py:52
  78.1 2.0 %collective-permute-start.32 = (bf16[128,512]{1,0:T(8,128)(2,1)S(1)}, bf16[128,512]{1,0:T(8,128)(2,1)S(1)}, u32[]{:S(2)}, u32[]{:S(2)}) collective-permute-start(bf16[128,512]{1,0:T(8,128)(2,1)S(1)} %collective-permute-done.23.a0), channel_id=1, source_target_pairs={{0,1},{1,0},{2,3},{3,2},{4,5},{5,4},{6,7},{7,6},{8,9},{9,8},{10,11... | collective-permute-start | bytes 393224 | tf_op jit(solution)/shard_map/gather_new/ppermute | solution.py:52
  81.9 10.6 %collective-permute-start.38 = (f16[136,512]{1,0:T(8,128)(2,1)S(1)}, f16[136,512]{1,0:T(8,128)(2,1)S(1)}, u32[]{:S(2)}, u32[]{:S(2)}) collective-permute-start(f16[136,512]{1,0:T(8,128)(2,1)S(1)} %get-tuple-element.48), channel_id=1, source_target_pairs={{0,80},{16,64},{32,112},{48,96},{64,16},{80,0},{96,48},{112,32},{1... | collective-permute-start | bytes 417800 | tf_op jit(solution)/shard_map/reduce_columns/ppermute | solution.py:264
  86.1 9.4 %collective-permute-start.39 = (f16[136,512]{1,0:T(8,128)(2,1)S(1)}, f16[136,512]{1,0:T(8,128)(2,1)S(1)}, u32[]{:S(2)}, u32[]{:S(2)}) collective-permute-start(f16[136,512]{1,0:T(8,128)(2,1)S(1)} %get-tuple-element.54), channel_id=1, source_target_pairs={{0,64},{16,80},{32,96},{48,112},{64,0},{80,16},{96,32},{112,48},{1... | collective-permute-start | bytes 417800 | tf_op jit(solution)/shard_map/reduce_columns/ppermute | solution.py:264
  86.7 12.6 %collective-permute-start.40 = (f16[136,512]{1,0:T(8,128)(2,1)S(1)}, f16[136,512]{1,0:T(8,128)(2,1)S(1)}, u32[]{:S(2)}, u32[]{:S(2)}) collective-permute-start(f16[136,512]{1,0:T(8,128)(2,1)S(1)} %get-tuple-element.53), channel_id=1, source_target_pairs={{0,48},{16,32},{32,80},{48,64},{64,112},{80,96},{96,16},{112,0},{1... | collective-permute-start | bytes 417800 | tf_op jit(solution)/shard_map/reduce_columns/ppermute | solution.py:264
  89.4 10.4 %collective-permute-start.41 = (f16[136,512]{1,0:T(8,128)(2,1)S(1)}, f16[136,512]{1,0:T(8,128)(2,1)S(1)}, u32[]{:S(2)}, u32[]{:S(2)}) collective-permute-start(f16[136,512]{1,0:T(8,128)(2,1)S(1)} %get-tuple-element.52), channel_id=1, source_target_pairs={{0,112},{16,96},{32,16},{48,0},{64,48},{80,32},{96,80},{112,64},{1... | collective-permute-start | bytes 417800 | tf_op jit(solution)/shard_map/reduce_columns/ppermute | solution.py:264
  92.3 7.5 %collective-permute-start.42 = (f16[136,512]{1,0:T(8,128)(2,1)S(1)}, f16[136,512]{1,0:T(8,128)(2,1)S(1)}, u32[]{:S(2)}, u32[]{:S(2)}) collective-permute-start(f16[136,512]{1,0:T(8,128)(2,1)S(1)} %get-tuple-element.51), channel_id=1, source_target_pairs={{0,32},{16,48},{32,64},{48,80},{64,96},{80,112},{96,0},{112,16},{1... | collective-permute-start | bytes 417800 | tf_op jit(solution)/shard_map/reduce_columns/ppermute | solution.py:264
  92.5 7.3 %collective-permute-start.43 = (f16[136,512]{1,0:T(8,128)(2,1)S(1)}, f16[136,512]{1,0:T(8,128)(2,1)S(1)}, u32[]{:S(2)}, u32[]{:S(2)}) collective-permute-start(f16[136,512]{1,0:T(8,128)(2,1)S(1)} %get-tuple-element.50), channel_id=1, source_target_pairs={{0,96},{16,112},{32,0},{48,16},{64,32},{80,48},{96,64},{112,80},{1... | collective-permute-start | bytes 417800 | tf_op jit(solution)/shard_map/reduce_columns/ppermute | solution.py:264
  95.5 7.2 %collective-permute-start.44 = (f16[136,512]{1,0:T(8,128)(2,1)S(1)}, f16[136,512]{1,0:T(8,128)(2,1)S(1)}, u32[]{:S(2)}, u32[]{:S(2)}) collective-permute-start(f16[136,512]{1,0:T(8,128)(2,1)S(1)} %get-tuple-element.49), channel_id=1, source_target_pairs={{0,16},{16,0},{32,48},{48,32},{64,80},{80,64},{96,112},{112,96},{1... | collective-permute-start | bytes 417800 | tf_op jit(solution)/shard_map/reduce_columns/ppermute | solution.py:264
  (1 other events, 0.7 us)

commit v5 on v4

--- a/solution.py
+++ b/solution.py
@@ -45,7 +45,7 @@
 SWAP_CORE = [(j, j ^ 1) for j in range(16)]
 
 
-AWAY = [(2, 1), (2, 0), (1, 1), (3, 1), (1, 0), (3, 0), (0, 1)]
+AWAY = [(0, 1), (1, 0), (3, 0), (1, 1), (3, 1), (2, 0), (2, 1)]
 
 
 def swap_core(value):
@@ -259,7 +259,7 @@
         sums = sums[0]
     with jax.named_scope("reduce_columns"):
         partial = sums[0] * COLUMN_SCALE
-        for d, e in AWAY:
+        for d, e in ((0, 1), (1, 0), (3, 0), (2, 1), (1, 1), (3, 1), (2, 0)):
             a = (sums[2 * d + e] * COLUMN_SCALE).astype(WIRE)
             partial = partial + lax.ppermute(a, "row", to_row(d, e)).astype(F32)
         share = partial[:BLOCK] * (1 / COLUMN_SCALE)

time: 105 us -> 103 us (0.981)
  waiting for transfers between devices: 28.9 us -> 27.7 us
    ppermute x7, waiting for transfers between devices: 7.73 us -> 5.77 us  [local(): own[d, e] = lax.ppermute(updated_rows, 'col', to_col(-d, e))]
    ppermute x7, starting transfers between devices: 9.16 us -> 10.5 us  [local(): own[d, e] = lax.ppermute(updated_rows, 'col', to_col(-d, e))]
    ppermute x7, starting transfers between devices: 15.5 us -> 14.2 us  [local(): partial = partial + lax.ppermute(a, 'row', to_row(d, e)).astype(F32)]
  transfers between devices with their start and end apart: 45 -> 45, of which waited for: 16 -> 13; matrix products, arithmetic and copies ran while one was open for 1% -> 1% of each run, Pallas kernels for 14% -> 14%
where the time goes in v5:
time: 103 us
  starting transfers between devices  55.2 us (54%)
  waiting for transfers between devices  27.7 us (27%)
  Pallas kernels  15.5 us (15%)
  other arithmetic  1.98 us (2%)
  local copies, waits for them, and re-layouts  1.24 us (1%)
    ppermute x7, starting transfers between devices, local(): partial = partial + lax.ppermute(a, 'row', to_row(d, e)).astype(F32)  14.2 us
    pallas_call x8, Pallas kernels, call(): pl.pallas_call(kernel, in_specs=[vmem] * len(operands) + [pl.BlockSpec(me...  11.4 us
    ppermute x7, starting transfers between devices, local(): own[d, e] = lax.ppermute(updated_rows, 'col', to_col(-d, e))  10.5 us
    ppermute x7, starting transfers between devices, local(): arrived.append(lax.ppermute(partial[k].astype(WIRE), 'col', to_col(d, e)))  9.77 us
    ppermute x3, starting transfers between devices, local(): own[d] = lax.ppermute(row_pair, 'col', along_z(-d))  7.62 us
    ppermute x7, waiting for transfers between devices, local(): arrived.append(lax.ppermute(partial[k].astype(WIRE), 'col', to_col(d, e)))  7.55 us
    ppermute x3, waiting for transfers between devices, local(): own[d] = lax.ppermute(row_pair, 'col', along_z(-d))  6.38 us
    ppermute x7, waiting for transfers between devices, local(): partial = partial + lax.ppermute(a, 'row', to_row(d, e)).astype(F32)  6.12 us
  transfers between devices with their start and end apart: 45, of which 13 were waited for; matrix products, arithmetic and copies ran while one was open for 1% of the time, Pallas kernels for 14%

profile of v5, /device:TPU:0, one launch (start us, length us, event | category | flops | bytes accessed | tf_op | source)
XLA Modules:
  0.0 102.6 jit_solution(13520552576561964832)
XLA Ops:
  0.6 1.7 %collective-permute-start = (bf16[128,512]{1,0:T(8,128)(2,1)}, bf16[128,512]{1,0:T(8,128)(2,1)S(1)}, u32[]{:S(2)}, u32[]{:S(2)}) collective-permute-start(bf16[128,512]{1,0:T(8,128)(2,1)} %param.6), channel_id=1, source_target_pairs={{0,2},{1,3},{2,0},{3,1},{4,6},{5,7},{6,4},{7,5},{8,10},{9,11},{10,... | collective-permute-start | bytes 393224 | tf_op jit(solution)/shard_map/gather_in/ppermute | solution.py:203
  2.4 2.9 %collective-permute-start.1 = (bf16[128,512]{1,0:T(8,128)(2,1)}, bf16[128,512]{1,0:T(8,128)(2,1)S(1)}, u32[]{:S(2)}, u32[]{:S(2)}) collective-permute-start(bf16[128,512]{1,0:T(8,128)(2,1)} %param.7), channel_id=1, source_target_pairs={{0,16},{16,0},{32,48},{48,32},{64,80},{80,64},{96,112},{112,96},{1... | collective-permute-start | bytes 393224 | tf_op jit(solution)/shard_map/gather_in/ppermute | solution.py:202
  5.5 0.7 copy-done.1
  6.1 4.2 %shard_map.59.counts = f32[16,128,1024]{2,1,0:T(8,128)S(1)} custom-call(s32[16]{0:T(128)S(1)} %stack.118.rows_ref, s32[8]{0:T(128)S(1)} %stack.127.place_ref, s32[4,8]{1,0:T(4,128)S(1)} %bitcast.121, s32[2048,1024]{1,0:T(8,128)} %counts.1), custom_call_target="tpu_custom_call" | custom-call | flops 2097152 | bytes 16777216 | tf_op jit(solution)/shard_map/pallas_call | solution.py:85
  10.4 1.1 %collective-permute-done.1 = bf16[128,512]{1,0:T(8,128)(2,1)S(1)} collective-permute-done((bf16[128,512]{1,0:T(8,128)(2,1)}, bf16[128,512]{1,0:T(8,128)(2,1)S(1)}, u32[]{:S(2)}, u32[]{:S(2)}) %collective-permute-start.1) | collective-permute-done | bytes 131104 | tf_op jit(solution)/shard_map/gather_in/ppermute | solution.py:202
  11.5 4.0 %collective-permute-start.8 = (bf16[2,128,512]{2,1,0:T(8,128)(2,1)S(1)}, bf16[2,128,512]{2,1,0:T(8,128)(2,1)S(1)}, u32[]{:S(2)}, u32[]{:S(2)}) collective-permute-start(bf16[2,128,512]{2,1,0:T(8,128)(2,1)S(1)} %pad_maximum_fusion), channel_id=1, source_target_pairs={{0,8},{1,9},{2,10},{3,11},{4,12},{5,13},{6,14},{7,15},{8,0},{9,1},... | collective-permute-start | bytes 786440 | tf_op jit(solution)/shard_map/gather_in/ppermute | solution.py:208
  15.5 0.7 collective-permute-start.10
  16.2 3.0 %collective-permute-start.3 = (bf16[2,128,512]{2,1,0:T(8,128)(2,1)S(1)}, bf16[2,128,512]{2,1,0:T(8,128)(2,1)S(1)}, u32[]{:S(2)}, u32[]{:S(2)}) collective-permute-start(bf16[2,128,512]{2,1,0:T(8,128)(2,1)S(1)} %pad_maximum_fusion.1), channel_id=1, source_target_pairs={{0,64},{16,80},{32,96},{48,112},{64,0},{80,16},{96,32},{112,48},{1... | collective-permute-start | bytes 786440 | tf_op jit(solution)/shard_map/gather_in/ppermute | solution.py:207
  19.3 1.2 %collective-permute-start.2 = (bf16[2,128,512]{2,1,0:T(8,128)(2,1)S(1)}, bf16[2,128,512]{2,1,0:T(8,128)(2,1)S(1)}, u32[]{:S(2)}, u32[]{:S(2)}) collective-permute-start(bf16[2,128,512]{2,1,0:T(8,128)(2,1)S(1)} %pad_maximum_fusion.1), channel_id=1, source_target_pairs={{0,96},{16,112},{32,0},{48,16},{64,32},{80,48},{96,64},{112,80},{1... | collective-permute-start | bytes 786440 | tf_op jit(solution)/shard_map/gather_in/ppermute | solution.py:207
  20.5 0.9 collective-permute-start.4
  21.4 2.9 %collective-permute-start.5 = (bf16[2,128,512]{2,1,0:T(8,128)(2,1)S(1)}, bf16[2,128,512]{2,1,0:T(8,128)(2,1)S(1)}, u32[]{:S(2)}, u32[]{:S(2)}) collective-permute-start(bf16[2,128,512]{2,1,0:T(8,128)(2,1)S(1)} %pad_maximum_fusion), channel_id=1, source_target_pairs={{0,4},{1,5},{2,6},{3,7},{4,8},{5,9},{6,10},{7,11},{8,12},{9,13},{1... | collective-permute-start | bytes 786440 | tf_op jit(solution)/shard_map/gather_in/ppermute | solution.py:208
  24.3 3.0 %collective-permute-done.10 = bf16[2,128,512]{2,1,0:T(8,128)(2,1)S(1)} collective-permute-done((bf16[2,128,512]{2,1,0:T(8,128)(2,1)S(1)}, bf16[2,128,512]{2,1,0:T(8,128)(2,1)S(1)}, u32[]{:S(2)}, u32[]{:S(2)}) %collective-permute-start.10) | collective-permute-done | bytes 262176 | tf_op jit(solution)/shard_map/gather_in/ppermute | solution.py:208
  27.3 3.4 %collective-permute-done.5 = bf16[2,128,512]{2,1,0:T(8,128)(2,1)S(1)} collective-permute-done((bf16[2,128,512]{2,1,0:T(8,128)(2,1)S(1)}, bf16[2,128,512]{2,1,0:T(8,128)(2,1)S(1)}, u32[]{:S(2)}, u32[]{:S(2)}) %collective-permute-start.5) | collective-permute-done | bytes 262176 | tf_op jit(solution)/shard_map/gather_in/ppermute | solution.py:208
  30.8 0.6 collective-permute-start.11
  31.6 0.7 collective-permute-done.9
  32.3 0.8 reduce_rows.4
  33.3 1.3 %reduce_rows.5 = (f32[2,136,512]{2,1,0:T(8,128)S(1)}, f32[2,136,512]{2,1,0:T(8,128)S(1)}) custom-call(f32[16,128,1024]{2,1,0:T(8,128)S(1)} %shard_map.59.counts, bf16[8,128,512]{2,1,0:T(8,128)(2,1)S(1)} %constant_dynamic-update-slice_fusion.panel, bf16[128,512]{1,0:T(8,128)(2,1)S(1)} %get-tuple-element.72.refs_0_, ...), custom_call_target="tpu_custom_call" | custom-call | flops 1048576 | bytes 65536 | tf_op jit(solution)/shard_map/reduce_rows/pallas_call | solution.py:168
  35.2 1.3 %reduce_rows.7 = (f32[2,136,512]{2,1,0:T(8,128)S(1)}, f32[2,136,512]{2,1,0:T(8,128)S(1)}) custom-call(f32[16,128,1024]{2,1,0:T(8,128)S(1)} %shard_map.59.counts, bf16[8,128,512]{2,1,0:T(8,128)(2,1)S(1)} %constant_dynamic-update-slice_fusion.panel, bf16[128,512]{1,0:T(8,128)(2,1)S(1)} %get-tuple-element.67.refs_0_, ...), custom_call_target="tpu_custom_call" | custom-call | flops 1048576 | bytes 65536 | tf_op jit(solution)/shard_map/reduce_rows/pallas_call | solution.py:168
  36.8 0.7 collective-permute-start.15
  37.5 1.9 %reduce_rows.6 = (f32[3,136,512]{2,1,0:T(8,128)S(1)}, f32[3,136,512]{2,1,0:T(8,128)S(1)}) custom-call(f32[16,128,1024]{2,1,0:T(8,128)S(1)} %shard_map.59.counts, bf16[8,128,512]{2,1,0:T(8,128)(2,1)S(1)} %constant_dynamic-update-slice_fusion.panel, bf16[128,512]{1,0:T(8,128)(2,1)S(1)} %get-tuple-element.64.refs_0_, ...), custom_call_target="tpu_custom_call" | custom-call | flops 1048576 | bytes 65536 | tf_op jit(solution)/shard_map/reduce_rows/pallas_call | solution.py:168
  39.8 2.6 %collective-permute-start.16 = (f16[136,512]{1,0:T(8,128)(2,1)S(1)}, f16[136,512]{1,0:T(8,128)(2,1)S(1)}, u32[]{:S(2)}, u32[]{:S(2)}) collective-permute-start(f16[136,512]{1,0:T(8,128)(2,1)S(1)} %get-tuple-element.57), channel_id=1, source_target_pairs={{0,8},{1,9},{2,10},{3,11},{4,12},{5,13},{6,14},{7,15},{8,0},{9,1},... | collective-permute-start | bytes 417800 | tf_op jit(solution)/shard_map/reduce_rows/ppermute | solution.py:227
  42.4 1.3 %collective-permute-start.17 = (f16[136,512]{1,0:T(8,128)(2,1)S(1)}, f16[136,512]{1,0:T(8,128)(2,1)S(1)}, u32[]{:S(2)}, u32[]{:S(2)}) collective-permute-start(f16[136,512]{1,0:T(8,128)(2,1)S(1)} %get-tuple-element.58), channel_id=1, source_target_pairs={{0,6},{1,7},{2,4},{3,5},{4,10},{5,11},{6,8},{7,9},{8,14},{9,15},{1... | collective-permute-start | bytes 417800 | tf_op jit(solution)/shard_map/reduce_rows/ppermute | solution.py:227
  43.8 1.1 %collective-permute-start.19 = (f16[136,512]{1,0:T(8,128)(2,1)S(1)}, f16[136,512]{1,0:T(8,128)(2,1)S(1)}, u32[]{:S(2)}, u32[]{:S(2)}) collective-permute-start(f16[136,512]{1,0:T(8,128)(2,1)S(1)} %get-tuple-element.59), channel_id=1, source_target_pairs={{0,4},{1,5},{2,6},{3,7},{4,8},{5,9},{6,10},{7,11},{8,12},{9,13},{1... | collective-permute-start | bytes 417800 | tf_op jit(solution)/shard_map/reduce_rows/ppermute | solution.py:227
  44.9 2.3 %collective-permute-start.20 = (f16[136,512]{1,0:T(8,128)(2,1)S(1)}, f16[136,512]{1,0:T(8,128)(2,1)S(1)}, u32[]{:S(2)}, u32[]{:S(2)}) collective-permute-start(f16[136,512]{1,0:T(8,128)(2,1)S(1)} %get-tuple-element.60), channel_id=1, source_target_pairs={{0,14},{1,15},{2,12},{3,13},{4,2},{5,3},{6,0},{7,1},{8,6},{9,7},{1... | collective-permute-start | bytes 417800 | tf_op jit(solution)/shard_map/reduce_rows/ppermute | solution.py:227
  47.5 1.7 %collective-permute-start.21 = (f16[136,512]{1,0:T(8,128)(2,1)S(1)}, f16[136,512]{1,0:T(8,128)(2,1)S(1)}, u32[]{:S(2)}, u32[]{:S(2)}) collective-permute-start(f16[136,512]{1,0:T(8,128)(2,1)S(1)} %get-tuple-element.55), channel_id=1, source_target_pairs={{0,12},{1,13},{2,14},{3,15},{4,0},{5,1},{6,2},{7,3},{8,4},{9,5},{1... | collective-permute-start | bytes 417800 | tf_op jit(solution)/shard_map/reduce_rows/ppermute | solution.py:227
  49.1 2.3 %collective-permute-done.16 = f16[136,512]{1,0:T(8,128)(2,1)S(1)} collective-permute-done((f16[136,512]{1,0:T(8,128)(2,1)S(1)}, f16[136,512]{1,0:T(8,128)(2,1)S(1)}, u32[]{:S(2)}, u32[]{:S(2)}) %collective-permute-start.16) | collective-permute-done | bytes 139296 | tf_op jit(solution)/shard_map/reduce_rows/ppermute | solution.py:227
  51.6 2.6 %collective-permute-done.19 = f16[136,512]{1,0:T(8,128)(2,1)S(1)} collective-permute-done((f16[136,512]{1,0:T(8,128)(2,1)S(1)}, f16[136,512]{1,0:T(8,128)(2,1)S(1)}, u32[]{:S(2)}, u32[]{:S(2)}) %collective-permute-start.19) | collective-permute-done | bytes 139296 | tf_op jit(solution)/shard_map/reduce_rows/ppermute | solution.py:227
  54.2 0.8 collective-permute-done.21
  55.0 1.9 %collective-permute-done.22 = f16[136,512]{1,0:T(8,128)(2,1)S(1)} collective-permute-done((f16[136,512]{1,0:T(8,128)(2,1)S(1)}, f16[136,512]{1,0:T(8,128)(2,1)S(1)}, u32[]{:S(2)}, u32[]{:S(2)}) %collective-permute-start.22) | collective-permute-done | bytes 139296 | tf_op jit(solution)/shard_map/reduce_rows/ppermute | solution.py:227
  57.5 1.7 %collective-permute-start.25 = (bf16[128,512]{1,0:T(8,128)(2,1)S(1)}, bf16[128,512]{1,0:T(8,128)(2,1)S(1)}, u32[]{:S(2)}, u32[]{:S(2)}) collective-permute-start(bf16[128,512]{1,0:T(8,128)(2,1)S(1)} %fusion.17.a0), channel_id=1, source_target_pairs={{0,12},{1,13},{2,14},{3,15},{4,0},{5,1},{6,2},{7,3},{8,4},{9,5},{1... | collective-permute-start | bytes 393224 | tf_op jit(solution)/shard_map/gather_new/ppermute | solution.py:238
  59.5 3.3 %collective-permute-start.34 = (bf16[128,512]{1,0:T(8,128)(2,1)S(1)}, bf16[128,512]{1,0:T(8,128)(2,1)S(1)}, u32[]{:S(2)}, u32[]{:S(2)}) collective-permute-start(bf16[128,512]{1,0:T(8,128)(2,1)S(1)} %fusion.17.a0), channel_id=1, source_target_pairs={{0,14},{1,15},{2,12},{3,13},{4,2},{5,3},{6,0},{7,1},{8,6},{9,7},{1... | collective-permute-start | bytes 393224 | tf_op jit(solution)/shard_map/gather_new/ppermute | solution.py:238
  63.0 3.3 %collective-permute-done.25.a0 = bf16[128,512]{1,0:T(8,128)(2,1)S(1)} collective-permute-done((bf16[128,512]{1,0:T(8,128)(2,1)S(1)}, bf16[128,512]{1,0:T(8,128)(2,1)S(1)}, u32[]{:S(2)}, u32[]{:S(2)}) %collective-permute-start.25) | collective-permute-done | bytes 131104 | tf_op jit(solution)/shard_map/gather_new/ppermute | solution.py:238
  66.8 3.0 %collective-permute-start.24 = (bf16[128,512]{1,0:T(8,128)(2,1)S(1)}, bf16[128,512]{1,0:T(8,128)(2,1)S(1)}, u32[]{:S(2)}, u32[]{:S(2)}) collective-permute-start(bf16[128,512]{1,0:T(8,128)(2,1)S(1)} %fusion.17.a0), channel_id=1, source_target_pairs={{0,10},{1,11},{2,8},{3,9},{4,14},{5,15},{6,12},{7,13},{8,2},{9,3},... | collective-permute-start | bytes 393224 | tf_op jit(solution)/shard_map/gather_new/ppermute | solution.py:238
  69.8 1.7 %collective-permute-start.23 = (bf16[128,512]{1,0:T(8,128)(2,1)S(1)}, bf16[128,512]{1,0:T(8,128)(2,1)S(1)}, u32[]{:S(2)}, u32[]{:S(2)}) collective-permute-start(bf16[128,512]{1,0:T(8,128)(2,1)S(1)} %fusion.17.a0), channel_id=1, source_target_pairs={{0,8},{1,9},{2,10},{3,11},{4,12},{5,13},{6,14},{7,15},{8,0},{9,1},... | collective-permute-start | bytes 393224 | tf_op jit(solution)/shard_map/gather_new/ppermute | solution.py:238
  71.5 1.4 %gather_new.4 = (f32[8,136,512]{2,1,0:T(8,128)S(1)}, f32[8,512]{1,0:T(8,128)S(1)}) custom-call(f32[16,128,1024]{2,1,0:T(8,128)S(1)} %shard_map.59.counts, bf16[128,512]{1,0:T(8,128)(2,1)S(1)} %fusion.17.a0, bf16[128,512]{1,0:T(8,128)(2,1)S(1)} %collective-permute-done.29.a1, bf16[128,512]{1,0:T(8,128)(2,1)S(1)} %collective-permute-done.30.b0, ...), custom_call_target="tpu_custom_call" | custom-call | flops 1048576 | bytes 65536 | tf_op jit(solution)/shard_map/gather_new/pallas_call | solution.py:168
  72.9 1.5 %gather_new.5 = (f32[8,136,512]{2,1,0:T(8,128)S(1)}, f32[8,512]{1,0:T(8,128)S(1)}) custom-call(f32[16,128,1024]{2,1,0:T(8,128)S(1)} %shard_map.59.counts, bf16[128,512]{1,0:T(8,128)(2,1)S(1)} %collective-permute-done.25.a0, bf16[128,512]{1,0:T(8,128)(2,1)S(1)} %collective-permute-done.26.a1, ...), custom_call_target="tpu_custom_call", output_to_operand_aliasing={{0}: (6, {}), {1}: (7, {})} | custom-call | flops 1048576 | bytes 65536 | tf_op jit(solution)/shard_map/gather_new/pallas_call | solution.py:168
  75.3 2.2 %collective-permute-done.23.a0 = bf16[128,512]{1,0:T(8,128)(2,1)S(1)} collective-permute-done((bf16[128,512]{1,0:T(8,128)(2,1)S(1)}, bf16[128,512]{1,0:T(8,128)(2,1)S(1)}, u32[]{:S(2)}, u32[]{:S(2)}) %collective-permute-start.23) | collective-permute-done | bytes 131104 | tf_op jit(solution)/shard_map/gather_new/ppermute | solution.py:238
  78.0 1.5 %gather_new.6 = (f32[8,136,512]{2,1,0:T(8,128)S(1)}, f32[8,512]{1,0:T(8,128)S(1)}) custom-call(f32[16,128,1024]{2,1,0:T(8,128)S(1)} %shard_map.59.counts, bf16[128,512]{1,0:T(8,128)(2,1)S(1)} %collective-permute-done.34.a0, bf16[128,512]{1,0:T(8,128)(2,1)S(1)} %collective-permute-done.35.a1, ...), custom_call_target="tpu_custom_call", output_to_operand_aliasing={{0}: (6, {}), {1}: (7, {})} | custom-call | flops 1048576 | bytes 65536 | tf_op jit(solution)/shard_map/gather_new/pallas_call | solution.py:168
  79.5 1.5 %gather_new.7 = (f32[8,136,512]{2,1,0:T(8,128)S(1)}, f32[8,512]{1,0:T(8,128)S(1)}) custom-call(f32[16,128,1024]{2,1,0:T(8,128)S(1)} %shard_map.59.counts, bf16[128,512]{1,0:T(8,128)(2,1)S(1)} %collective-permute-done.23.a0, bf16[128,512]{1,0:T(8,128)(2,1)S(1)} %collective-permute-done.24.a1, ...), custom_call_target="tpu_custom_call", output_to_operand_aliasing={{0}: (6, {}), {1}: (7, {})} | custom-call | flops 1048576 | bytes 65536 | tf_op jit(solution)/shard_map/gather_new/pallas_call | solution.py:168
  81.3 0.7 collective-permute-start.38
  82.0 1.4 %collective-permute-start.39 = (f16[136,512]{1,0:T(8,128)(2,1)S(1)}, f16[136,512]{1,0:T(8,128)(2,1)S(1)}, u32[]{:S(2)}, u32[]{:S(2)}) collective-permute-start(f16[136,512]{1,0:T(8,128)(2,1)S(1)} %get-tuple-element.54), channel_id=1, source_target_pairs={{0,32},{16,48},{32,64},{48,80},{64,96},{80,112},{96,0},{112,16},{1... | collective-permute-start | bytes 417800 | tf_op jit(solution)/shard_map/reduce_columns/ppermute | solution.py:264
  83.4 1.8 %collective-permute-start.40 = (f16[136,512]{1,0:T(8,128)(2,1)S(1)}, f16[136,512]{1,0:T(8,128)(2,1)S(1)}, u32[]{:S(2)}, u32[]{:S(2)}) collective-permute-start(f16[136,512]{1,0:T(8,128)(2,1)S(1)} %get-tuple-element.53), channel_id=1, source_target_pairs={{0,96},{16,112},{32,0},{48,16},{64,32},{80,48},{96,64},{112,80},{1... | collective-permute-start | bytes 417800 | tf_op jit(solution)/shard_map/reduce_columns/ppermute | solution.py:264
  85.2 4.2 %collective-permute-start.41 = (f16[136,512]{1,0:T(8,128)(2,1)S(1)}, f16[136,512]{1,0:T(8,128)(2,1)S(1)}, u32[]{:S(2)}, u32[]{:S(2)}) collective-permute-start(f16[136,512]{1,0:T(8,128)(2,1)S(1)} %get-tuple-element.52), channel_id=1, source_target_pairs={{0,80},{16,64},{32,112},{48,96},{64,16},{80,0},{96,48},{112,32},{1... | collective-permute-start | bytes 417800 | tf_op jit(solution)/shard_map/reduce_columns/ppermute | solution.py:264
  89.4 0.6 collective-permute-start.42
  90.0 5.0 %collective-permute-start.43 = (f16[136,512]{1,0:T(8,128)(2,1)S(1)}, f16[136,512]{1,0:T(8,128)(2,1)S(1)}, u32[]{:S(2)}, u32[]{:S(2)}) collective-permute-start(f16[136,512]{1,0:T(8,128)(2,1)S(1)} %get-tuple-element.50), channel_id=1, source_target_pairs={{0,112},{16,96},{32,16},{48,0},{64,48},{80,32},{96,80},{112,64},{1... | collective-permute-start | bytes 417800 | tf_op jit(solution)/shard_map/reduce_columns/ppermute | solution.py:264
  95.6 1.4 %collective-permute-done.41 = f16[136,512]{1,0:T(8,128)(2,1)S(1)} collective-permute-done((f16[136,512]{1,0:T(8,128)(2,1)S(1)}, f16[136,512]{1,0:T(8,128)(2,1)S(1)}, u32[]{:S(2)}, u32[]{:S(2)}) %collective-permute-start.41) | collective-permute-done | bytes 139296 | tf_op jit(solution)/shard_map/reduce_columns/ppermute | solution.py:264
  96.9 4.7 %collective-permute-done.42 = f16[136,512]{1,0:T(8,128)(2,1)S(1)} collective-permute-done((f16[136,512]{1,0:T(8,128)(2,1)S(1)}, f16[136,512]{1,0:T(8,128)(2,1)S(1)}, u32[]{:S(2)}, u32[]{:S(2)}) %collective-permute-start.42) | collective-permute-done | bytes 139296 | tf_op jit(solution)/shard_map/reduce_columns/ppermute | solution.py:264
  101.9 0.7 fusion.18
  (89 shorter events, 6.4 us)
Async XLA Ops:
  0.6 9.7 %collective-permute-start = (bf16[128,512]{1,0:T(8,128)(2,1)}, bf16[128,512]{1,0:T(8,128)(2,1)S(1)}, u32[]{:S(2)}, u32[]{:S(2)}) collective-permute-start(bf16[128,512]{1,0:T(8,128)(2,1)} %param.6), channel_id=1, source_target_pairs={{0,2},{1,3},{2,0},{3,1},{4,6},{5,7},{6,4},{7,5},{8,10},{9,11},{10,... | collective-permute-start | bytes 393224 | tf_op jit(solution)/shard_map/gather_in/ppermute | solution.py:203
  2.4 9.1 %collective-permute-start.1 = (bf16[128,512]{1,0:T(8,128)(2,1)}, bf16[128,512]{1,0:T(8,128)(2,1)S(1)}, u32[]{:S(2)}, u32[]{:S(2)}) collective-permute-start(bf16[128,512]{1,0:T(8,128)(2,1)} %param.7), channel_id=1, source_target_pairs={{0,16},{16,0},{32,48},{48,32},{64,80},{80,64},{96,112},{112,96},{1... | collective-permute-start | bytes 393224 | tf_op jit(solution)/shard_map/gather_in/ppermute | solution.py:202
  6.1 4.2 %copy-start.2 = (bf16[128,512]{1,0:T(8,128)(2,1)S(1)}, bf16[128,512]{1,0:T(8,128)(2,1)}, u32[]{:S(2)}) copy-start(bf16[128,512]{1,0:T(8,128)(2,1)} %param.6) | copy-start | bytes 393220
  6.1 5.4 %copy-start.3 = (bf16[128,512]{1,0:T(8,128)(2,1)S(1)}, bf16[128,512]{1,0:T(8,128)(2,1)}, u32[]{:S(2)}) copy-start(bf16[128,512]{1,0:T(8,128)(2,1)} %param.7) | copy-start | bytes 393220
  11.5 9.8 %collective-permute-start.8 = (bf16[2,128,512]{2,1,0:T(8,128)(2,1)S(1)}, bf16[2,128,512]{2,1,0:T(8,128)(2,1)S(1)}, u32[]{:S(2)}, u32[]{:S(2)}) collective-permute-start(bf16[2,128,512]{2,1,0:T(8,128)(2,1)S(1)} %pad_maximum_fusion), channel_id=1, source_target_pairs={{0,8},{1,9},{2,10},{3,11},{4,12},{5,13},{6,14},{7,15},{8,0},{9,1},... | collective-permute-start | bytes 786440 | tf_op jit(solution)/shard_map/gather_in/ppermute | solution.py:208
  15.5 11.8 %collective-permute-start.10 = (bf16[2,128,512]{2,1,0:T(8,128)(2,1)S(1)}, bf16[2,128,512]{2,1,0:T(8,128)(2,1)S(1)}, u32[]{:S(2)}, u32[]{:S(2)}) collective-permute-start(bf16[2,128,512]{2,1,0:T(8,128)(2,1)S(1)} %pad_maximum_fusion), channel_id=1, source_target_pairs={{0,12},{1,13},{2,14},{3,15},{4,0},{5,1},{6,2},{7,3},{8,4},{9,5},{1... | collective-permute-start | bytes 786440 | tf_op jit(solution)/shard_map/gather_in/ppermute | solution.py:208
  16.2 15.2 %collective-permute-start.3 = (bf16[2,128,512]{2,1,0:T(8,128)(2,1)S(1)}, bf16[2,128,512]{2,1,0:T(8,128)(2,1)S(1)}, u32[]{:S(2)}, u32[]{:S(2)}) collective-permute-start(bf16[2,128,512]{2,1,0:T(8,128)(2,1)S(1)} %pad_maximum_fusion.1), channel_id=1, source_target_pairs={{0,64},{16,80},{32,96},{48,112},{64,0},{80,16},{96,32},{112,48},{1... | collective-permute-start | bytes 786440 | tf_op jit(solution)/shard_map/gather_in/ppermute | solution.py:207
  19.3 11.5 %collective-permute-start.2 = (bf16[2,128,512]{2,1,0:T(8,128)(2,1)S(1)}, bf16[2,128,512]{2,1,0:T(8,128)(2,1)S(1)}, u32[]{:S(2)}, u32[]{:S(2)}) collective-permute-start(bf16[2,128,512]{2,1,0:T(8,128)(2,1)S(1)} %pad_maximum_fusion.1), channel_id=1, source_target_pairs={{0,96},{16,112},{32,0},{48,16},{64,32},{80,48},{96,64},{112,80},{1... | collective-permute-start | bytes 786440 | tf_op jit(solution)/shard_map/gather_in/ppermute | solution.py:207
  20.5 11.0 %collective-permute-start.4 = (bf16[2,128,512]{2,1,0:T(8,128)(2,1)S(1)}, bf16[2,128,512]{2,1,0:T(8,128)(2,1)S(1)}, u32[]{:S(2)}, u32[]{:S(2)}) collective-permute-start(bf16[2,128,512]{2,1,0:T(8,128)(2,1)S(1)} %pad_maximum_fusion.1), channel_id=1, source_target_pairs={{0,32},{16,48},{32,64},{48,80},{64,96},{80,112},{96,0},{112,16},{1... | collective-permute-start | bytes 786440 | tf_op jit(solution)/shard_map/gather_in/ppermute | solution.py:207
  21.4 9.4 %collective-permute-start.5 = (bf16[2,128,512]{2,1,0:T(8,128)(2,1)S(1)}, bf16[2,128,512]{2,1,0:T(8,128)(2,1)S(1)}, u32[]{:S(2)}, u32[]{:S(2)}) collective-permute-start(bf16[2,128,512]{2,1,0:T(8,128)(2,1)S(1)} %pad_maximum_fusion), channel_id=1, source_target_pairs={{0,4},{1,5},{2,6},{3,7},{4,8},{5,9},{6,10},{7,11},{8,12},{9,13},{1... | collective-permute-start | bytes 786440 | tf_op jit(solution)/shard_map/gather_in/ppermute | solution.py:208
  27.3 7.8 %collective-permute-start.7 = (bf16[2,128,512]{2,1,0:T(8,128)(2,1)S(1)}, bf16[2,128,512]{2,1,0:T(8,128)(2,1)S(1)}, u32[]{:S(2)}, u32[]{:S(2)}) collective-permute-start(bf16[2,128,512]{2,1,0:T(8,128)(2,1)S(1)} %pad_maximum_fusion), channel_id=1, source_target_pairs={{0,1},{1,0},{2,3},{3,2},{4,5},{5,4},{6,7},{7,6},{8,9},{9,8},{10,11... | collective-permute-start | bytes 786440 | tf_op jit(solution)/shard_map/gather_in/ppermute | solution.py:52
  30.7 1.5 %collective-permute-start.9 = (bf16[2,128,512]{2,1,0:T(8,128)(2,1)S(1)}, bf16[2,128,512]{2,1,0:T(8,128)(2,1)S(1)}, u32[]{:S(2)}, u32[]{:S(2)}) collective-permute-start(bf16[2,128,512]{2,1,0:T(8,128)(2,1)S(1)} %collective-permute-done.8), channel_id=1, source_target_pairs={{0,1},{1,0},{2,3},{3,2},{4,5},{5,4},{6,7},{7,6},{8,9},{9,8},{10,11... | collective-permute-start | bytes 786440 | tf_op jit(solution)/shard_map/gather_in/ppermute | solution.py:52
  30.8 2.5 %collective-permute-start.11 = (bf16[2,128,512]{2,1,0:T(8,128)(2,1)S(1)}, bf16[2,128,512]{2,1,0:T(8,128)(2,1)S(1)}, u32[]{:S(2)}, u32[]{:S(2)}) collective-permute-start(bf16[2,128,512]{2,1,0:T(8,128)(2,1)S(1)} %collective-permute-done.10), channel_id=1, source_target_pairs={{0,1},{1,0},{2,3},{3,2},{4,5},{5,4},{6,7},{7,6},{8,9},{9,8},{10,11... | collective-permute-start | bytes 786440 | tf_op jit(solution)/shard_map/gather_in/ppermute | solution.py:52
  31.4 3.8 %collective-permute-start.6 = (bf16[2,128,512]{2,1,0:T(8,128)(2,1)S(1)}, bf16[2,128,512]{2,1,0:T(8,128)(2,1)S(1)}, u32[]{:S(2)}, u32[]{:S(2)}) collective-permute-start(bf16[2,128,512]{2,1,0:T(8,128)(2,1)S(1)} %collective-permute-done.5), channel_id=1, source_target_pairs={{0,1},{1,0},{2,3},{3,2},{4,5},{5,4},{6,7},{7,6},{8,9},{9,8},{10,11... | collective-permute-start | bytes 786440 | tf_op jit(solution)/shard_map/gather_in/ppermute | solution.py:52
  33.1 2.1 %collective-permute-start.14 = (f32[1,136,512]{2,1,0:T(8,128)S(1)}, f32[1,136,512]{2,1,0:T(8,128)S(1)}, u32[]{:S(2)}, u32[]{:S(2)}) collective-permute-start(f32[1,136,512]{2,1,0:T(8,128)S(1)} %get-tuple-element.31), channel_id=1, source_target_pairs={{0,1},{1,0},{2,3},{3,2},{4,5},{5,4},{6,7},{7,6},{8,9},{9,8},{10,11... | collective-permute-start | bytes 835592 | tf_op jit(solution)/shard_map/reduce_rows/ppermute | solution.py:52
  34.7 2.8 %collective-permute-start.12 = (f32[2,136,512]{2,1,0:T(8,128)S(1)}, f32[2,136,512]{2,1,0:T(8,128)S(1)}, u32[]{:S(2)}, u32[]{:S(2)}) collective-permute-start(f32[2,136,512]{2,1,0:T(8,128)S(1)} %get-tuple-element.28), channel_id=1, source_target_pairs={{0,1},{1,0},{2,3},{3,2},{4,5},{5,4},{6,7},{7,6},{8,9},{9,8},{10,11... | collective-permute-start | bytes 1671176 | tf_op jit(solution)/shard_map/reduce_rows/ppermute | solution.py:52
  36.6 7.1 %collective-permute-start.18 = (f32[2,136,512]{2,1,0:T(8,128)S(1)}, f32[2,136,512]{2,1,0:T(8,128)S(1)}, u32[]{:S(2)}, u32[]{:S(2)}) collective-permute-start(f32[2,136,512]{2,1,0:T(8,128)S(1)} %get-tuple-element.34), channel_id=1, source_target_pairs={{0,1},{1,0},{2,3},{3,2},{4,5},{5,4},{6,7},{7,6},{8,9},{9,8},{10,11... | collective-permute-start | bytes 1671176 | tf_op jit(solution)/shard_map/reduce_rows/ppermute | solution.py:52
  36.8 10.6 %collective-permute-start.15 = (f16[136,512]{1,0:T(8,128)(2,1)S(1)}, f16[136,512]{1,0:T(8,128)(2,1)S(1)}, u32[]{:S(2)}, u32[]{:S(2)}) collective-permute-start(f16[136,512]{1,0:T(8,128)(2,1)S(1)} %fusion.19), channel_id=1, source_target_pairs={{0,10},{1,11},{2,8},{3,9},{4,14},{5,15},{6,12},{7,13},{8,2},{9,3},... | collective-permute-start | bytes 417800 | tf_op jit(solution)/shard_map/reduce_rows/ppermute | solution.py:227
  39.4 5.5 %collective-permute-start.13 = (f32[3,136,512]{2,1,0:T(8,128)S(1)}, f32[3,136,512]{2,1,0:T(8,128)S(1)}, u32[]{:S(2)}, u32[]{:S(2)}) collective-permute-start(f32[3,136,512]{2,1,0:T(8,128)S(1)} %get-tuple-element.30), channel_id=1, source_target_pairs={{0,1},{1,0},{2,3},{3,2},{4,5},{5,4},{6,7},{7,6},{8,9},{9,8},{10,11... | collective-permute-start | bytes 2506760 | tf_op jit(solution)/shard_map/reduce_rows/ppermute | solution.py:52
  39.8 11.6 %collective-permute-start.16 = (f16[136,512]{1,0:T(8,128)(2,1)S(1)}, f16[136,512]{1,0:T(8,128)(2,1)S(1)}, u32[]{:S(2)}, u32[]{:S(2)}) collective-permute-start(f16[136,512]{1,0:T(8,128)(2,1)S(1)} %get-tuple-element.57), channel_id=1, source_target_pairs={{0,8},{1,9},{2,10},{3,11},{4,12},{5,13},{6,14},{7,15},{8,0},{9,1},... | collective-permute-start | bytes 417800 | tf_op jit(solution)/shard_map/reduce_rows/ppermute | solution.py:227
  42.4 9.2 %collective-permute-start.17 = (f16[136,512]{1,0:T(8,128)(2,1)S(1)}, f16[136,512]{1,0:T(8,128)(2,1)S(1)}, u32[]{:S(2)}, u32[]{:S(2)}) collective-permute-start(f16[136,512]{1,0:T(8,128)(2,1)S(1)} %get-tuple-element.58), channel_id=1, source_target_pairs={{0,6},{1,7},{2,4},{3,5},{4,10},{5,11},{6,8},{7,9},{8,14},{9,15},{1... | collective-permute-start | bytes 417800 | tf_op jit(solution)/shard_map/reduce_rows/ppermute | solution.py:227
  43.8 10.4 %collective-permute-start.19 = (f16[136,512]{1,0:T(8,128)(2,1)S(1)}, f16[136,512]{1,0:T(8,128)(2,1)S(1)}, u32[]{:S(2)}, u32[]{:S(2)}) collective-permute-start(f16[136,512]{1,0:T(8,128)(2,1)S(1)} %get-tuple-element.59), channel_id=1, source_target_pairs={{0,4},{1,5},{2,6},{3,7},{4,8},{5,9},{6,10},{7,11},{8,12},{9,13},{1... | collective-permute-start | bytes 417800 | tf_op jit(solution)/shard_map/reduce_rows/ppermute | solution.py:227
  44.9 9.3 %collective-permute-start.20 = (f16[136,512]{1,0:T(8,128)(2,1)S(1)}, f16[136,512]{1,0:T(8,128)(2,1)S(1)}, u32[]{:S(2)}, u32[]{:S(2)}) collective-permute-start(f16[136,512]{1,0:T(8,128)(2,1)S(1)} %get-tuple-element.60), channel_id=1, source_target_pairs={{0,14},{1,15},{2,12},{3,13},{4,2},{5,3},{6,0},{7,1},{8,6},{9,7},{1... | collective-permute-start | bytes 417800 | tf_op jit(solution)/shard_map/reduce_rows/ppermute | solution.py:227
  47.5 7.5 %collective-permute-start.21 = (f16[136,512]{1,0:T(8,128)(2,1)S(1)}, f16[136,512]{1,0:T(8,128)(2,1)S(1)}, u32[]{:S(2)}, u32[]{:S(2)}) collective-permute-start(f16[136,512]{1,0:T(8,128)(2,1)S(1)} %get-tuple-element.55), channel_id=1, source_target_pairs={{0,12},{1,13},{2,14},{3,15},{4,0},{5,1},{6,2},{7,3},{8,4},{9,5},{1... | collective-permute-start | bytes 417800 | tf_op jit(solution)/shard_map/reduce_rows/ppermute | solution.py:227
  51.4 5.5 %collective-permute-start.22 = (f16[136,512]{1,0:T(8,128)(2,1)S(1)}, f16[136,512]{1,0:T(8,128)(2,1)S(1)}, u32[]{:S(2)}, u32[]{:S(2)}) collective-permute-start(f16[136,512]{1,0:T(8,128)(2,1)S(1)} %get-tuple-element.56), channel_id=1, source_target_pairs={{0,2},{1,3},{2,0},{3,1},{4,6},{5,7},{6,4},{7,5},{8,10},{9,11},{10,... | collective-permute-start | bytes 417800 | tf_op jit(solution)/shard_map/reduce_rows/ppermute | solution.py:227
  57.1 15.8 %copy-start = (bf16[128,512]{1,0:T(8,128)(2,1)}, bf16[128,512]{1,0:T(8,128)(2,1)S(1)}, u32[]{:S(2)}) copy-start(bf16[128,512]{1,0:T(8,128)(2,1)S(1)} %fusion.17.a0) | copy-start | bytes 393220
  57.2 5.7 %collective-permute-start.29 = (bf16[128,512]{1,0:T(8,128)(2,1)S(1)}, bf16[128,512]{1,0:T(8,128)(2,1)S(1)}, u32[]{:S(2)}, u32[]{:S(2)}) collective-permute-start(bf16[128,512]{1,0:T(8,128)(2,1)S(1)} %fusion.17.a0), channel_id=1, source_target_pairs={{0,2},{1,3},{2,0},{3,1},{4,6},{5,7},{6,4},{7,5},{8,10},{9,11},{10,... | collective-permute-start | bytes 393224 | tf_op jit(solution)/shard_map/gather_new/ppermute | solution.py:238
  57.5 5.4 %collective-permute-start.30 = (bf16[128,512]{1,0:T(8,128)(2,1)S(1)}, bf16[128,512]{1,0:T(8,128)(2,1)S(1)}, u32[]{:S(2)}, u32[]{:S(2)}) collective-permute-start(bf16[128,512]{1,0:T(8,128)(2,1)S(1)} %fusion.17.a0), channel_id=1, source_target_pairs={{0,1},{1,0},{2,3},{3,2},{4,5},{5,4},{6,7},{7,6},{8,9},{9,8},{10,11... | collective-permute-start | bytes 393224 | tf_op jit(solution)/shard_map/gather_new/ppermute | solution.py:52
  57.5 8.7 %collective-permute-start.25 = (bf16[128,512]{1,0:T(8,128)(2,1)S(1)}, bf16[128,512]{1,0:T(8,128)(2,1)S(1)}, u32[]{:S(2)}, u32[]{:S(2)}) collective-permute-start(bf16[128,512]{1,0:T(8,128)(2,1)S(1)} %fusion.17.a0), channel_id=1, source_target_pairs={{0,12},{1,13},{2,14},{3,15},{4,0},{5,1},{6,2},{7,3},{8,4},{9,5},{1... | collective-permute-start | bytes 393224 | tf_op jit(solution)/shard_map/gather_new/ppermute | solution.py:238
  59.2 7.0 %collective-permute-start.26 = (bf16[128,512]{1,0:T(8,128)(2,1)S(1)}, bf16[128,512]{1,0:T(8,128)(2,1)S(1)}, u32[]{:S(2)}, u32[]{:S(2)}) collective-permute-start(bf16[128,512]{1,0:T(8,128)(2,1)S(1)} %fusion.17.a0), channel_id=1, source_target_pairs={{0,4},{1,5},{2,6},{3,7},{4,8},{5,9},{6,10},{7,11},{8,12},{9,13},{1... | collective-permute-start | bytes 393224 | tf_op jit(solution)/shard_map/gather_new/ppermute | solution.py:238
  59.5 7.2 %collective-permute-start.34 = (bf16[128,512]{1,0:T(8,128)(2,1)S(1)}, bf16[128,512]{1,0:T(8,128)(2,1)S(1)}, u32[]{:S(2)}, u32[]{:S(2)}) collective-permute-start(bf16[128,512]{1,0:T(8,128)(2,1)S(1)} %fusion.17.a0), channel_id=1, source_target_pairs={{0,14},{1,15},{2,12},{3,13},{4,2},{5,3},{6,0},{7,1},{8,6},{9,7},{1... | collective-permute-start | bytes 393224 | tf_op jit(solution)/shard_map/gather_new/ppermute | solution.py:238
  62.9 6.9 %collective-permute-start.31 = (bf16[128,512]{1,0:T(8,128)(2,1)S(1)}, bf16[128,512]{1,0:T(8,128)(2,1)S(1)}, u32[]{:S(2)}, u32[]{:S(2)}) collective-permute-start(bf16[128,512]{1,0:T(8,128)(2,1)S(1)} %collective-permute-done.29.a1), channel_id=1, source_target_pairs={{0,1},{1,0},{2,3},{3,2},{4,5},{5,4},{6,7},{7,6},{8,9},{9,8},{10,11... | collective-permute-start | bytes 393224 | tf_op jit(solution)/shard_map/gather_new/ppermute | solution.py:52
  62.9 10.0 %collective-permute-start.35 = (bf16[128,512]{1,0:T(8,128)(2,1)S(1)}, bf16[128,512]{1,0:T(8,128)(2,1)S(1)}, u32[]{:S(2)}, u32[]{:S(2)}) collective-permute-start(bf16[128,512]{1,0:T(8,128)(2,1)S(1)} %fusion.17.a0), channel_id=1, source_target_pairs={{0,6},{1,7},{2,4},{3,5},{4,10},{5,11},{6,8},{7,9},{8,14},{9,15},{1... | collective-permute-start | bytes 393224 | tf_op jit(solution)/shard_map/gather_new/ppermute | solution.py:238
  66.2 6.7 %collective-permute-start.27 = (bf16[128,512]{1,0:T(8,128)(2,1)S(1)}, bf16[128,512]{1,0:T(8,128)(2,1)S(1)}, u32[]{:S(2)}, u32[]{:S(2)}) collective-permute-start(bf16[128,512]{1,0:T(8,128)(2,1)S(1)} %collective-permute-done.25.a0), channel_id=1, source_target_pairs={{0,1},{1,0},{2,3},{3,2},{4,5},{5,4},{6,7},{7,6},{8,9},{9,8},{10,11... | collective-permute-start | bytes 393224 | tf_op jit(solution)/shard_map/gather_new/ppermute | solution.py:52
  66.2 6.7 %collective-permute-start.28 = (bf16[128,512]{1,0:T(8,128)(2,1)S(1)}, bf16[128,512]{1,0:T(8,128)(2,1)S(1)}, u32[]{:S(2)}, u32[]{:S(2)}) collective-permute-start(bf16[128,512]{1,0:T(8,128)(2,1)S(1)} %collective-permute-done.26.a1), channel_id=1, source_target_pairs={{0,1},{1,0},{2,3},{3,2},{4,5},{5,4},{6,7},{7,6},{8,9},{9,8},{10,11... | collective-permute-start | bytes 393224 | tf_op jit(solution)/shard_map/gather_new/ppermute | solution.py:52
  66.8 8.0 %collective-permute-start.24 = (bf16[128,512]{1,0:T(8,128)(2,1)S(1)}, bf16[128,512]{1,0:T(8,128)(2,1)S(1)}, u32[]{:S(2)}, u32[]{:S(2)}) collective-permute-start(bf16[128,512]{1,0:T(8,128)(2,1)S(1)} %fusion.17.a0), channel_id=1, source_target_pairs={{0,10},{1,11},{2,8},{3,9},{4,14},{5,15},{6,12},{7,13},{8,2},{9,3},... | collective-permute-start | bytes 393224 | tf_op jit(solution)/shard_map/gather_new/ppermute | solution.py:238
  69.8 7.7 %collective-permute-start.23 = (bf16[128,512]{1,0:T(8,128)(2,1)S(1)}, bf16[128,512]{1,0:T(8,128)(2,1)S(1)}, u32[]{:S(2)}, u32[]{:S(2)}) collective-permute-start(bf16[128,512]{1,0:T(8,128)(2,1)S(1)} %fusion.17.a0), channel_id=1, source_target_pairs={{0,8},{1,9},{2,10},{3,11},{4,12},{5,13},{6,14},{7,15},{8,0},{9,1},... | collective-permute-start | bytes 393224 | tf_op jit(solution)/shard_map/gather_new/ppermute | solution.py:238
  74.7 3.2 %collective-permute-start.36 = (bf16[128,512]{1,0:T(8,128)(2,1)S(1)}, bf16[128,512]{1,0:T(8,128)(2,1)S(1)}, u32[]{:S(2)}, u32[]{:S(2)}) collective-permute-start(bf16[128,512]{1,0:T(8,128)(2,1)S(1)} %collective-permute-done.34.a0), channel_id=1, source_target_pairs={{0,1},{1,0},{2,3},{3,2},{4,5},{5,4},{6,7},{7,6},{8,9},{9,8},{10,11... | collective-permute-start | bytes 393224 | tf_op jit(solution)/shard_map/gather_new/ppermute | solution.py:52
  74.7 3.2 %collective-permute-start.37 = (bf16[128,512]{1,0:T(8,128)(2,1)S(1)}, bf16[128,512]{1,0:T(8,128)(2,1)S(1)}, u32[]{:S(2)}, u32[]{:S(2)}) collective-permute-start(bf16[128,512]{1,0:T(8,128)(2,1)S(1)} %collective-permute-done.35.a1), channel_id=1, source_target_pairs={{0,1},{1,0},{2,3},{3,2},{4,5},{5,4},{6,7},{7,6},{8,9},{9,8},{10,11... | collective-permute-start | bytes 393224 | tf_op jit(solution)/shard_map/gather_new/ppermute | solution.py:52
  77.5 2.0 %collective-permute-start.33 = (bf16[128,512]{1,0:T(8,128)(2,1)S(1)}, bf16[128,512]{1,0:T(8,128)(2,1)S(1)}, u32[]{:S(2)}, u32[]{:S(2)}) collective-permute-start(bf16[128,512]{1,0:T(8,128)(2,1)S(1)} %collective-permute-done.24.a1), channel_id=1, source_target_pairs={{0,1},{1,0},{2,3},{3,2},{4,5},{5,4},{6,7},{7,6},{8,9},{9,8},{10,11... | collective-permute-start | bytes 393224 | tf_op jit(solution)/shard_map/gather_new/ppermute | solution.py:52
  77.5 2.0 %collective-permute-start.32 = (bf16[128,512]{1,0:T(8,128)(2,1)S(1)}, bf16[128,512]{1,0:T(8,128)(2,1)S(1)}, u32[]{:S(2)}, u32[]{:S(2)}) collective-permute-start(bf16[128,512]{1,0:T(8,128)(2,1)S(1)} %collective-permute-done.23.a0), channel_id=1, source_target_pairs={{0,1},{1,0},{2,3},{3,2},{4,5},{5,4},{6,7},{7,6},{8,9},{9,8},{10,11... | collective-permute-start | bytes 393224 | tf_op jit(solution)/shard_map/gather_new/ppermute | solution.py:52
  81.3 8.7 %collective-permute-start.38 = (f16[136,512]{1,0:T(8,128)(2,1)S(1)}, f16[136,512]{1,0:T(8,128)(2,1)S(1)}, u32[]{:S(2)}, u32[]{:S(2)}) collective-permute-start(f16[136,512]{1,0:T(8,128)(2,1)S(1)} %get-tuple-element.48), channel_id=1, source_target_pairs={{0,16},{16,0},{32,48},{48,32},{64,80},{80,64},{96,112},{112,96},{1... | collective-permute-start | bytes 417800 | tf_op jit(solution)/shard_map/reduce_columns/ppermute | solution.py:264
  82.0 13.0 %collective-permute-start.39 = (f16[136,512]{1,0:T(8,128)(2,1)S(1)}, f16[136,512]{1,0:T(8,128)(2,1)S(1)}, u32[]{:S(2)}, u32[]{:S(2)}) collective-permute-start(f16[136,512]{1,0:T(8,128)(2,1)S(1)} %get-tuple-element.54), channel_id=1, source_target_pairs={{0,32},{16,48},{32,64},{48,80},{64,96},{80,112},{96,0},{112,16},{1... | collective-permute-start | bytes 417800 | tf_op jit(solution)/shard_map/reduce_columns/ppermute | solution.py:264
  83.4 12.1 %collective-permute-start.40 = (f16[136,512]{1,0:T(8,128)(2,1)S(1)}, f16[136,512]{1,0:T(8,128)(2,1)S(1)}, u32[]{:S(2)}, u32[]{:S(2)}) collective-permute-start(f16[136,512]{1,0:T(8,128)(2,1)S(1)} %get-tuple-element.53), channel_id=1, source_target_pairs={{0,96},{16,112},{32,0},{48,16},{64,32},{80,48},{96,64},{112,80},{1... | collective-permute-start | bytes 417800 | tf_op jit(solution)/shard_map/reduce_columns/ppermute | solution.py:264
  85.2 11.7 %collective-permute-start.41 = (f16[136,512]{1,0:T(8,128)(2,1)S(1)}, f16[136,512]{1,0:T(8,128)(2,1)S(1)}, u32[]{:S(2)}, u32[]{:S(2)}) collective-permute-start(f16[136,512]{1,0:T(8,128)(2,1)S(1)} %get-tuple-element.52), channel_id=1, source_target_pairs={{0,80},{16,64},{32,112},{48,96},{64,16},{80,0},{96,48},{112,32},{1... | collective-permute-start | bytes 417800 | tf_op jit(solution)/shard_map/reduce_columns/ppermute | solution.py:264
  89.4 12.3 %collective-permute-start.42 = (f16[136,512]{1,0:T(8,128)(2,1)S(1)}, f16[136,512]{1,0:T(8,128)(2,1)S(1)}, u32[]{:S(2)}, u32[]{:S(2)}) collective-permute-start(f16[136,512]{1,0:T(8,128)(2,1)S(1)} %get-tuple-element.51), channel_id=1, source_target_pairs={{0,48},{16,32},{32,80},{48,64},{64,112},{80,96},{96,16},{112,0},{1... | collective-permute-start | bytes 417800 | tf_op jit(solution)/shard_map/reduce_columns/ppermute | solution.py:264
  90.0 11.7 %collective-permute-start.43 = (f16[136,512]{1,0:T(8,128)(2,1)S(1)}, f16[136,512]{1,0:T(8,128)(2,1)S(1)}, u32[]{:S(2)}, u32[]{:S(2)}) collective-permute-start(f16[136,512]{1,0:T(8,128)(2,1)S(1)} %get-tuple-element.50), channel_id=1, source_target_pairs={{0,112},{16,96},{32,16},{48,0},{64,48},{80,32},{96,80},{112,64},{1... | collective-permute-start | bytes 417800 | tf_op jit(solution)/shard_map/reduce_columns/ppermute | solution.py:264
  95.0 6.6 %collective-permute-start.44 = (f16[136,512]{1,0:T(8,128)(2,1)S(1)}, f16[136,512]{1,0:T(8,128)(2,1)S(1)}, u32[]{:S(2)}, u32[]{:S(2)}) collective-permute-start(f16[136,512]{1,0:T(8,128)(2,1)S(1)} %get-tuple-element.49), channel_id=1, source_target_pairs={{0,64},{16,80},{32,96},{48,112},{64,0},{80,16},{96,32},{112,48},{1... | collective-permute-start | bytes 417800 | tf_op jit(solution)/shard_map/reduce_columns/ppermute | solution.py:264
  (1 other events, 0.7 us)

commit v6 on v5

--- a/solution.py
+++ b/solution.py
@@ -171,7 +171,7 @@
         out_specs=(vmem,) * len(out_shape),
         out_shape=out_shape,
         input_output_aliases=aliases,
-        cost_estimate=pl.CostEstimate(flops=2**20, bytes_accessed=2**16, transcendentals=0),
+        cost_estimate=pl.CostEstimate(flops=2**30, bytes_accessed=2**24, transcendentals=0),
         compiler_params=pltpu.CompilerParams(vmem_limit_bytes=24 * 2**20),
     )(*operands, *after)
 
@@ -203,7 +203,7 @@
         row_pair = jnp.stack([row_factors, lax.ppermute(row_factors, "col", to_col(0, 1))])
         row_pair, column_pair, counts = lax.optimization_barrier((row_pair, column_pair, counts))
         own, panel = {0: row_pair}, {0: column_pair}
-        for d in (2, 1, 3):
+        for d in (1, 3, 2):
             panel[d] = lax.ppermute(column_pair, "row", along_x(-d))
             own[d] = lax.ppermute(row_pair, "col", along_z(-d))
         panel = jnp.concatenate([panel[d] for d in range(4)])

time: 103 us -> 103 us (level)
  waiting for transfers between devices: 27.7 us -> 25.5 us
  starting transfers between devices: 55.2 us -> 57.4 us
    ppermute x7, waiting for transfers between devices: 7.55 us -> 4.18 us  [local(): arrived.append(lax.ppermute(partial[k].astype(WIRE), 'col', to_col(d, e)))]
    ppermute x7, starting transfers between devices: 9.77 us -> 11.7 us  [local(): arrived.append(lax.ppermute(partial[k].astype(WIRE), 'col', to_col(d, e)))]
    ppermute x3, waiting for transfers between devices: 0.01 us -> 1.5 us  [local(): panel[d] = lax.ppermute(column_pair, 'row', along_x(-d))]
  transfers between devices with their start and end apart: 45 -> 45, of which waited for: 13 -> 17; matrix products, arithmetic and copies ran while one was open for 1% -> 1% of each run, Pallas kernels for 14% -> 14%
where the time goes in v6:
time: 103 us
  starting transfers between devices  57.4 us (56%)
  waiting for transfers between devices  25.5 us (25%)
  Pallas kernels  15.5 us (15%)
  other arithmetic  2 us (2%)
  local copies, waits for them, and re-layouts  1.24 us (1%)
  between operations  1.05 us (1%)
    ppermute x7, starting transfers between devices, local(): partial = partial + lax.ppermute(a, 'row', to_row(d, e)).astype(F32)  14.2 us
    ppermute x7, starting transfers between devices, local(): arrived.append(lax.ppermute(partial[k].astype(WIRE), 'col', to_col(d, e)))  11.7 us
    pallas_call x8, Pallas kernels, call(): pl.pallas_call(kernel, in_specs=[vmem] * len(operands) + [pl.BlockSpec(me...  11.3 us
    ppermute x7, starting transfers between devices, local(): own[d, e] = lax.ppermute(updated_rows, 'col', to_col(-d, e))  11.1 us
    ppermute x3, starting transfers between devices, local(): own[d] = lax.ppermute(row_pair, 'col', along_z(-d))  7.8 us
    ppermute x7, waiting for transfers between devices, local(): partial = partial + lax.ppermute(a, 'row', to_row(d, e)).astype(F32)  6.46 us
    ppermute x7, waiting for transfers between devices, local(): own[d, e] = lax.ppermute(updated_rows, 'col', to_col(-d, e))  6.31 us
    ppermute x3, waiting for transfers between devices, local(): own[d] = lax.ppermute(row_pair, 'col', along_z(-d))  5.86 us
  transfers between devices with their start and end apart: 45, of which 17 were waited for; matrix products, arithmetic and copies ran while one was open for 1% of the time, Pallas kernels for 14%

profile of v6, /device:TPU:0, one launch (start us, length us, event | category | flops | bytes accessed | tf_op | source)
XLA Modules:
  0.0 102.7 jit_solution(2859962318636607658)
XLA Ops:
  0.6 1.7 %collective-permute-start = (bf16[128,512]{1,0:T(8,128)(2,1)}, bf16[128,512]{1,0:T(8,128)(2,1)S(1)}, u32[]{:S(2)}, u32[]{:S(2)}) collective-permute-start(bf16[128,512]{1,0:T(8,128)(2,1)} %param.6), channel_id=1, source_target_pairs={{0,2},{1,3},{2,0},{3,1},{4,6},{5,7},{6,4},{7,5},{8,10},{9,11},{10,... | collective-permute-start | bytes 393224 | tf_op jit(solution)/shard_map/gather_in/ppermute | solution.py:203
  2.4 2.9 %collective-permute-start.1 = (bf16[128,512]{1,0:T(8,128)(2,1)}, bf16[128,512]{1,0:T(8,128)(2,1)S(1)}, u32[]{:S(2)}, u32[]{:S(2)}) collective-permute-start(bf16[128,512]{1,0:T(8,128)(2,1)} %param.7), channel_id=1, source_target_pairs={{0,16},{16,0},{32,48},{48,32},{64,80},{80,64},{96,112},{112,96},{1... | collective-permute-start | bytes 393224 | tf_op jit(solution)/shard_map/gather_in/ppermute | solution.py:202
  5.5 0.7 copy-done.1
  6.1 4.2 %shard_map.59.counts = f32[16,128,1024]{2,1,0:T(8,128)S(1)} custom-call(s32[16]{0:T(128)S(1)} %stack.118.rows_ref, s32[8]{0:T(128)S(1)} %stack.127.place_ref, s32[4,8]{1,0:T(4,128)S(1)} %bitcast.121, s32[2048,1024]{1,0:T(8,128)} %counts.1), custom_call_target="tpu_custom_call" | custom-call | flops 2097152 | bytes 16777216 | tf_op jit(solution)/shard_map/pallas_call | solution.py:85
  10.4 1.1 %collective-permute-done.1 = bf16[128,512]{1,0:T(8,128)(2,1)S(1)} collective-permute-done((bf16[128,512]{1,0:T(8,128)(2,1)}, bf16[128,512]{1,0:T(8,128)(2,1)S(1)}, u32[]{:S(2)}, u32[]{:S(2)}) %collective-permute-start.1) | collective-permute-done | bytes 131104 | tf_op jit(solution)/shard_map/gather_in/ppermute | solution.py:202
  11.5 4.0 %collective-permute-start.8 = (bf16[2,128,512]{2,1,0:T(8,128)(2,1)S(1)}, bf16[2,128,512]{2,1,0:T(8,128)(2,1)S(1)}, u32[]{:S(2)}, u32[]{:S(2)}) collective-permute-start(bf16[2,128,512]{2,1,0:T(8,128)(2,1)S(1)} %pad_maximum_fusion), channel_id=1, source_target_pairs={{0,8},{1,9},{2,10},{3,11},{4,12},{5,13},{6,14},{7,15},{8,0},{9,1},... | collective-permute-start | bytes 786440 | tf_op jit(solution)/shard_map/gather_in/ppermute | solution.py:208
  15.5 2.8 %collective-permute-start.2 = (bf16[2,128,512]{2,1,0:T(8,128)(2,1)S(1)}, bf16[2,128,512]{2,1,0:T(8,128)(2,1)S(1)}, u32[]{:S(2)}, u32[]{:S(2)}) collective-permute-start(bf16[2,128,512]{2,1,0:T(8,128)(2,1)S(1)} %pad_maximum_fusion.1), channel_id=1, source_target_pairs={{0,96},{16,112},{32,0},{48,16},{64,32},{80,48},{96,64},{112,80},{1... | collective-permute-start | bytes 786440 | tf_op jit(solution)/shard_map/gather_in/ppermute | solution.py:207
  18.3 0.8 collective-permute-start.3
  19.1 0.9 collective-permute-start.4
  20.0 0.7 collective-permute-start.10
  20.9 3.1 %collective-permute-start.5 = (bf16[2,128,512]{2,1,0:T(8,128)(2,1)S(1)}, bf16[2,128,512]{2,1,0:T(8,128)(2,1)S(1)}, u32[]{:S(2)}, u32[]{:S(2)}) collective-permute-start(bf16[2,128,512]{2,1,0:T(8,128)(2,1)S(1)} %pad_maximum_fusion), channel_id=1, source_target_pairs={{0,4},{1,5},{2,6},{3,7},{4,8},{5,9},{6,10},{7,11},{8,12},{9,13},{1... | collective-permute-start | bytes 786440 | tf_op jit(solution)/shard_map/gather_in/ppermute | solution.py:208
  24.1 3.2 %collective-permute-done.10 = bf16[2,128,512]{2,1,0:T(8,128)(2,1)S(1)} collective-permute-done((bf16[2,128,512]{2,1,0:T(8,128)(2,1)S(1)}, bf16[2,128,512]{2,1,0:T(8,128)(2,1)S(1)}, u32[]{:S(2)}, u32[]{:S(2)}) %collective-permute-start.10) | collective-permute-done | bytes 262176 | tf_op jit(solution)/shard_map/gather_in/ppermute | solution.py:208
  27.3 2.5 %collective-permute-done.5 = bf16[2,128,512]{2,1,0:T(8,128)(2,1)S(1)} collective-permute-done((bf16[2,128,512]{2,1,0:T(8,128)(2,1)S(1)}, bf16[2,128,512]{2,1,0:T(8,128)(2,1)S(1)}, u32[]{:S(2)}, u32[]{:S(2)}) %collective-permute-start.5) | collective-permute-done | bytes 262176 | tf_op jit(solution)/shard_map/gather_in/ppermute | solution.py:208
  29.8 0.6 collective-permute-start.11
  30.6 1.5 %collective-permute-done.4 = bf16[2,128,512]{2,1,0:T(8,128)(2,1)S(1)} collective-permute-done((bf16[2,128,512]{2,1,0:T(8,128)(2,1)S(1)}, bf16[2,128,512]{2,1,0:T(8,128)(2,1)S(1)}, u32[]{:S(2)}, u32[]{:S(2)}) %collective-permute-start.4) | collective-permute-done | bytes 262176 | tf_op jit(solution)/shard_map/gather_in/ppermute | solution.py:207
  32.2 0.8 reduce_rows.4
  33.1 1.3 %reduce_rows.5 = (f32[2,136,512]{2,1,0:T(8,128)S(1)}, f32[2,136,512]{2,1,0:T(8,128)S(1)}) custom-call(f32[16,128,1024]{2,1,0:T(8,128)S(1)} %shard_map.59.counts, bf16[8,128,512]{2,1,0:T(8,128)(2,1)S(1)} %constant_dynamic-update-slice_fusion.panel, bf16[128,512]{1,0:T(8,128)(2,1)S(1)} %get-tuple-element.72.refs_0_, ...), custom_call_target="tpu_custom_call" | custom-call | flops 1073741824 | bytes 16777216 | tf_op jit(solution)/shard_map/reduce_rows/pallas_call | solution.py:168
  34.4 0.6 collective-permute-start.12
  35.2 1.4 %reduce_rows.7 = (f32[2,136,512]{2,1,0:T(8,128)S(1)}, f32[2,136,512]{2,1,0:T(8,128)S(1)}) custom-call(f32[16,128,1024]{2,1,0:T(8,128)S(1)} %shard_map.59.counts, bf16[8,128,512]{2,1,0:T(8,128)(2,1)S(1)} %constant_dynamic-update-slice_fusion.panel, bf16[128,512]{1,0:T(8,128)(2,1)S(1)} %get-tuple-element.67.refs_0_, ...), custom_call_target="tpu_custom_call" | custom-call | flops 1073741824 | bytes 16777216 | tf_op jit(solution)/shard_map/reduce_rows/pallas_call | solution.py:168
  36.7 1.9 %reduce_rows.6 = (f32[3,136,512]{2,1,0:T(8,128)S(1)}, f32[3,136,512]{2,1,0:T(8,128)S(1)}) custom-call(f32[16,128,1024]{2,1,0:T(8,128)S(1)} %shard_map.59.counts, bf16[8,128,512]{2,1,0:T(8,128)(2,1)S(1)} %constant_dynamic-update-slice_fusion.panel, bf16[128,512]{1,0:T(8,128)(2,1)S(1)} %get-tuple-element.64.refs_0_, ...), custom_call_target="tpu_custom_call" | custom-call | flops 1073741824 | bytes 16777216 | tf_op jit(solution)/shard_map/reduce_rows/pallas_call | solution.py:168
  38.6 0.6 collective-permute-start.13
  39.3 3.2 %collective-permute-start.16 = (f16[136,512]{1,0:T(8,128)(2,1)S(1)}, f16[136,512]{1,0:T(8,128)(2,1)S(1)}, u32[]{:S(2)}, u32[]{:S(2)}) collective-permute-start(f16[136,512]{1,0:T(8,128)(2,1)S(1)} %get-tuple-element.57), channel_id=1, source_target_pairs={{0,8},{1,9},{2,10},{3,11},{4,12},{5,13},{6,14},{7,15},{8,0},{9,1},... | collective-permute-start | bytes 417800 | tf_op jit(solution)/shard_map/reduce_rows/ppermute | solution.py:227
  42.5 2.3 %collective-permute-start.17 = (f16[136,512]{1,0:T(8,128)(2,1)S(1)}, f16[136,512]{1,0:T(8,128)(2,1)S(1)}, u32[]{:S(2)}, u32[]{:S(2)}) collective-permute-start(f16[136,512]{1,0:T(8,128)(2,1)S(1)} %get-tuple-element.58), channel_id=1, source_target_pairs={{0,6},{1,7},{2,4},{3,5},{4,10},{5,11},{6,8},{7,9},{8,14},{9,15},{1... | collective-permute-start | bytes 417800 | tf_op jit(solution)/shard_map/reduce_rows/ppermute | solution.py:227
  45.1 2.8 %collective-permute-start.20 = (f16[136,512]{1,0:T(8,128)(2,1)S(1)}, f16[136,512]{1,0:T(8,128)(2,1)S(1)}, u32[]{:S(2)}, u32[]{:S(2)}) collective-permute-start(f16[136,512]{1,0:T(8,128)(2,1)S(1)} %get-tuple-element.60), channel_id=1, source_target_pairs={{0,14},{1,15},{2,12},{3,13},{4,2},{5,3},{6,0},{7,1},{8,6},{9,7},{1... | collective-permute-start | bytes 417800 | tf_op jit(solution)/shard_map/reduce_rows/ppermute | solution.py:227
  48.2 1.1 %collective-permute-start.21 = (f16[136,512]{1,0:T(8,128)(2,1)S(1)}, f16[136,512]{1,0:T(8,128)(2,1)S(1)}, u32[]{:S(2)}, u32[]{:S(2)}) collective-permute-start(f16[136,512]{1,0:T(8,128)(2,1)S(1)} %get-tuple-element.55), channel_id=1, source_target_pairs={{0,12},{1,13},{2,14},{3,15},{4,0},{5,1},{6,2},{7,3},{8,4},{9,5},{1... | collective-permute-start | bytes 417800 | tf_op jit(solution)/shard_map/reduce_rows/ppermute | solution.py:227
  49.6 2.1 %collective-permute-start.22 = (f16[136,512]{1,0:T(8,128)(2,1)S(1)}, f16[136,512]{1,0:T(8,128)(2,1)S(1)}, u32[]{:S(2)}, u32[]{:S(2)}) collective-permute-start(f16[136,512]{1,0:T(8,128)(2,1)S(1)} %get-tuple-element.56), channel_id=1, source_target_pairs={{0,2},{1,3},{2,0},{3,1},{4,6},{5,7},{6,4},{7,5},{8,10},{9,11},{10,... | collective-permute-start | bytes 417800 | tf_op jit(solution)/shard_map/reduce_rows/ppermute | solution.py:227
  51.7 1.2 %collective-permute-done.19 = f16[136,512]{1,0:T(8,128)(2,1)S(1)} collective-permute-done((f16[136,512]{1,0:T(8,128)(2,1)S(1)}, f16[136,512]{1,0:T(8,128)(2,1)S(1)}, u32[]{:S(2)}, u32[]{:S(2)}) %collective-permute-start.19) | collective-permute-done | bytes 139296 | tf_op jit(solution)/shard_map/reduce_rows/ppermute | solution.py:227
  53.2 1.8 %collective-permute-done.21 = f16[136,512]{1,0:T(8,128)(2,1)S(1)} collective-permute-done((f16[136,512]{1,0:T(8,128)(2,1)S(1)}, f16[136,512]{1,0:T(8,128)(2,1)S(1)}, u32[]{:S(2)}, u32[]{:S(2)}) %collective-permute-start.21) | collective-permute-done | bytes 139296 | tf_op jit(solution)/shard_map/reduce_rows/ppermute | solution.py:227
  55.8 1.3 %collective-permute-start.29 = (bf16[128,512]{1,0:T(8,128)(2,1)S(1)}, bf16[128,512]{1,0:T(8,128)(2,1)S(1)}, u32[]{:S(2)}, u32[]{:S(2)}) collective-permute-start(bf16[128,512]{1,0:T(8,128)(2,1)S(1)} %fusion.17.a0), channel_id=1, source_target_pairs={{0,2},{1,3},{2,0},{3,1},{4,6},{5,7},{6,4},{7,5},{8,10},{9,11},{10,... | collective-permute-start | bytes 393224 | tf_op jit(solution)/shard_map/gather_new/ppermute | solution.py:238
  57.2 2.1 %collective-permute-start.25 = (bf16[128,512]{1,0:T(8,128)(2,1)S(1)}, bf16[128,512]{1,0:T(8,128)(2,1)S(1)}, u32[]{:S(2)}, u32[]{:S(2)}) collective-permute-start(bf16[128,512]{1,0:T(8,128)(2,1)S(1)} %fusion.17.a0), channel_id=1, source_target_pairs={{0,12},{1,13},{2,14},{3,15},{4,0},{5,1},{6,2},{7,3},{8,4},{9,5},{1... | collective-permute-start | bytes 393224 | tf_op jit(solution)/shard_map/gather_new/ppermute | solution.py:238
  59.2 3.8 %collective-permute-start.34 = (bf16[128,512]{1,0:T(8,128)(2,1)S(1)}, bf16[128,512]{1,0:T(8,128)(2,1)S(1)}, u32[]{:S(2)}, u32[]{:S(2)}) collective-permute-start(bf16[128,512]{1,0:T(8,128)(2,1)S(1)} %fusion.17.a0), channel_id=1, source_target_pairs={{0,14},{1,15},{2,12},{3,13},{4,2},{5,3},{6,0},{7,1},{8,6},{9,7},{1... | collective-permute-start | bytes 393224 | tf_op jit(solution)/shard_map/gather_new/ppermute | solution.py:238
  63.1 2.8 %collective-permute-done.25.a0 = bf16[128,512]{1,0:T(8,128)(2,1)S(1)} collective-permute-done((bf16[128,512]{1,0:T(8,128)(2,1)S(1)}, bf16[128,512]{1,0:T(8,128)(2,1)S(1)}, u32[]{:S(2)}, u32[]{:S(2)}) %collective-permute-start.25) | collective-permute-done | bytes 131104 | tf_op jit(solution)/shard_map/gather_new/ppermute | solution.py:238
  66.9 3.0 %collective-permute-start.24 = (bf16[128,512]{1,0:T(8,128)(2,1)S(1)}, bf16[128,512]{1,0:T(8,128)(2,1)S(1)}, u32[]{:S(2)}, u32[]{:S(2)}) collective-permute-start(bf16[128,512]{1,0:T(8,128)(2,1)S(1)} %fusion.17.a0), channel_id=1, source_target_pairs={{0,10},{1,11},{2,8},{3,9},{4,14},{5,15},{6,12},{7,13},{8,2},{9,3},... | collective-permute-start | bytes 393224 | tf_op jit(solution)/shard_map/gather_new/ppermute | solution.py:238
  69.9 0.8 collective-permute-start.23
  70.8 1.4 %gather_new.4 = (f32[8,136,512]{2,1,0:T(8,128)S(1)}, f32[8,512]{1,0:T(8,128)S(1)}) custom-call(f32[16,128,1024]{2,1,0:T(8,128)S(1)} %shard_map.59.counts, bf16[128,512]{1,0:T(8,128)(2,1)S(1)} %fusion.17.a0, bf16[128,512]{1,0:T(8,128)(2,1)S(1)} %collective-permute-done.29.a1, bf16[128,512]{1,0:T(8,128)(2,1)S(1)} %collective-permute-done.30.b0, ...), custom_call_target="tpu_custom_call" | custom-call | flops 1073741824 | bytes 16777216 | tf_op jit(solution)/shard_map/gather_new/pallas_call | solution.py:168
  72.8 1.5 %gather_new.5 = (f32[8,136,512]{2,1,0:T(8,128)S(1)}, f32[8,512]{1,0:T(8,128)S(1)}) custom-call(f32[16,128,1024]{2,1,0:T(8,128)S(1)} %shard_map.59.counts, bf16[128,512]{1,0:T(8,128)(2,1)S(1)} %collective-permute-done.25.a0, bf16[128,512]{1,0:T(8,128)(2,1)S(1)} %collective-permute-done.26.a1, ...), custom_call_target="tpu_custom_call", output_to_operand_aliasing={{0}: (6, {}), {1}: (7, {})} | custom-call | flops 1073741824 | bytes 16777216 | tf_op jit(solution)/shard_map/gather_new/pallas_call | solution.py:168
  74.4 2.8 %collective-permute-done.23.a0 = bf16[128,512]{1,0:T(8,128)(2,1)S(1)} collective-permute-done((bf16[128,512]{1,0:T(8,128)(2,1)S(1)}, bf16[128,512]{1,0:T(8,128)(2,1)S(1)}, u32[]{:S(2)}, u32[]{:S(2)}) %collective-permute-start.23) | collective-permute-done | bytes 131104 | tf_op jit(solution)/shard_map/gather_new/ppermute | solution.py:238
  77.7 1.5 %gather_new.6 = (f32[8,136,512]{2,1,0:T(8,128)S(1)}, f32[8,512]{1,0:T(8,128)S(1)}) custom-call(f32[16,128,1024]{2,1,0:T(8,128)S(1)} %shard_map.59.counts, bf16[128,512]{1,0:T(8,128)(2,1)S(1)} %collective-permute-done.34.a0, bf16[128,512]{1,0:T(8,128)(2,1)S(1)} %collective-permute-done.35.a1, ...), custom_call_target="tpu_custom_call", output_to_operand_aliasing={{0}: (6, {}), {1}: (7, {})} | custom-call | flops 1073741824 | bytes 16777216 | tf_op jit(solution)/shard_map/gather_new/pallas_call | solution.py:168
  79.2 1.5 %gather_new.7 = (f32[8,136,512]{2,1,0:T(8,128)S(1)}, f32[8,512]{1,0:T(8,128)S(1)}) custom-call(f32[16,128,1024]{2,1,0:T(8,128)S(1)} %shard_map.59.counts, bf16[128,512]{1,0:T(8,128)(2,1)S(1)} %collective-permute-done.23.a0, bf16[128,512]{1,0:T(8,128)(2,1)S(1)} %collective-permute-done.24.a1, ...), custom_call_target="tpu_custom_call", output_to_operand_aliasing={{0}: (6, {}), {1}: (7, {})} | custom-call | flops 1073741824 | bytes 16777216 | tf_op jit(solution)/shard_map/gather_new/pallas_call | solution.py:168
  81.0 1.3 %collective-permute-start.38 = (f16[136,512]{1,0:T(8,128)(2,1)S(1)}, f16[136,512]{1,0:T(8,128)(2,1)S(1)}, u32[]{:S(2)}, u32[]{:S(2)}) collective-permute-start(f16[136,512]{1,0:T(8,128)(2,1)S(1)} %get-tuple-element.48), channel_id=1, source_target_pairs={{0,16},{16,0},{32,48},{48,32},{64,80},{80,64},{96,112},{112,96},{1... | collective-permute-start | bytes 417800 | tf_op jit(solution)/shard_map/reduce_columns/ppermute | solution.py:264
  82.4 3.2 %collective-permute-start.40 = (f16[136,512]{1,0:T(8,128)(2,1)S(1)}, f16[136,512]{1,0:T(8,128)(2,1)S(1)}, u32[]{:S(2)}, u32[]{:S(2)}) collective-permute-start(f16[136,512]{1,0:T(8,128)(2,1)S(1)} %get-tuple-element.53), channel_id=1, source_target_pairs={{0,96},{16,112},{32,0},{48,16},{64,32},{80,48},{96,64},{112,80},{1... | collective-permute-start | bytes 417800 | tf_op jit(solution)/shard_map/reduce_columns/ppermute | solution.py:264
  85.6 3.4 %collective-permute-start.41 = (f16[136,512]{1,0:T(8,128)(2,1)S(1)}, f16[136,512]{1,0:T(8,128)(2,1)S(1)}, u32[]{:S(2)}, u32[]{:S(2)}) collective-permute-start(f16[136,512]{1,0:T(8,128)(2,1)S(1)} %get-tuple-element.52), channel_id=1, source_target_pairs={{0,80},{16,64},{32,112},{48,96},{64,16},{80,0},{96,48},{112,32},{1... | collective-permute-start | bytes 417800 | tf_op jit(solution)/shard_map/reduce_columns/ppermute | solution.py:264
  88.9 0.7 collective-permute-start.42
  89.7 4.9 %collective-permute-start.43 = (f16[136,512]{1,0:T(8,128)(2,1)S(1)}, f16[136,512]{1,0:T(8,128)(2,1)S(1)}, u32[]{:S(2)}, u32[]{:S(2)}) collective-permute-start(f16[136,512]{1,0:T(8,128)(2,1)S(1)} %get-tuple-element.50), channel_id=1, source_target_pairs={{0,112},{16,96},{32,16},{48,0},{64,48},{80,32},{96,80},{112,64},{1... | collective-permute-start | bytes 417800 | tf_op jit(solution)/shard_map/reduce_columns/ppermute | solution.py:264
  94.6 0.7 collective-permute-start.44
  95.3 1.8 %collective-permute-done.41 = f16[136,512]{1,0:T(8,128)(2,1)S(1)} collective-permute-done((f16[136,512]{1,0:T(8,128)(2,1)S(1)}, f16[136,512]{1,0:T(8,128)(2,1)S(1)}, u32[]{:S(2)}, u32[]{:S(2)}) %collective-permute-start.41) | collective-permute-done | bytes 139296 | tf_op jit(solution)/shard_map/reduce_columns/ppermute | solution.py:264
  97.1 4.7 %collective-permute-done.42 = f16[136,512]{1,0:T(8,128)(2,1)S(1)} collective-permute-done((f16[136,512]{1,0:T(8,128)(2,1)S(1)}, f16[136,512]{1,0:T(8,128)(2,1)S(1)}, u32[]{:S(2)}, u32[]{:S(2)}) %collective-permute-start.42) | collective-permute-done | bytes 139296 | tf_op jit(solution)/shard_map/reduce_columns/ppermute | solution.py:264
  102.0 0.7 fusion.18
  (89 shorter events, 6.1 us)
Async XLA Ops:
  0.6 9.7 %collective-permute-start = (bf16[128,512]{1,0:T(8,128)(2,1)}, bf16[128,512]{1,0:T(8,128)(2,1)S(1)}, u32[]{:S(2)}, u32[]{:S(2)}) collective-permute-start(bf16[128,512]{1,0:T(8,128)(2,1)} %param.6), channel_id=1, source_target_pairs={{0,2},{1,3},{2,0},{3,1},{4,6},{5,7},{6,4},{7,5},{8,10},{9,11},{10,... | collective-permute-start | bytes 393224 | tf_op jit(solution)/shard_map/gather_in/ppermute | solution.py:203
  2.4 9.1 %collective-permute-start.1 = (bf16[128,512]{1,0:T(8,128)(2,1)}, bf16[128,512]{1,0:T(8,128)(2,1)S(1)}, u32[]{:S(2)}, u32[]{:S(2)}) collective-permute-start(bf16[128,512]{1,0:T(8,128)(2,1)} %param.7), channel_id=1, source_target_pairs={{0,16},{16,0},{32,48},{48,32},{64,80},{80,64},{96,112},{112,96},{1... | collective-permute-start | bytes 393224 | tf_op jit(solution)/shard_map/gather_in/ppermute | solution.py:202
  6.1 4.2 %copy-start.2 = (bf16[128,512]{1,0:T(8,128)(2,1)S(1)}, bf16[128,512]{1,0:T(8,128)(2,1)}, u32[]{:S(2)}) copy-start(bf16[128,512]{1,0:T(8,128)(2,1)} %param.6) | copy-start | bytes 393220
  6.1 5.4 %copy-start.3 = (bf16[128,512]{1,0:T(8,128)(2,1)S(1)}, bf16[128,512]{1,0:T(8,128)(2,1)}, u32[]{:S(2)}) copy-start(bf16[128,512]{1,0:T(8,128)(2,1)} %param.7) | copy-start | bytes 393220
  11.5 9.4 %collective-permute-start.8 = (bf16[2,128,512]{2,1,0:T(8,128)(2,1)S(1)}, bf16[2,128,512]{2,1,0:T(8,128)(2,1)S(1)}, u32[]{:S(2)}, u32[]{:S(2)}) collective-permute-start(bf16[2,128,512]{2,1,0:T(8,128)(2,1)S(1)} %pad_maximum_fusion), channel_id=1, source_target_pairs={{0,8},{1,9},{2,10},{3,11},{4,12},{5,13},{6,14},{7,15},{8,0},{9,1},... | collective-permute-start | bytes 786440 | tf_op jit(solution)/shard_map/gather_in/ppermute | solution.py:208
  15.5 14.3 %collective-permute-start.2 = (bf16[2,128,512]{2,1,0:T(8,128)(2,1)S(1)}, bf16[2,128,512]{2,1,0:T(8,128)(2,1)S(1)}, u32[]{:S(2)}, u32[]{:S(2)}) collective-permute-start(bf16[2,128,512]{2,1,0:T(8,128)(2,1)S(1)} %pad_maximum_fusion.1), channel_id=1, source_target_pairs={{0,96},{16,112},{32,0},{48,16},{64,32},{80,48},{96,64},{112,80},{1... | collective-permute-start | bytes 786440 | tf_op jit(solution)/shard_map/gather_in/ppermute | solution.py:207
  18.3 12.1 %collective-permute-start.3 = (bf16[2,128,512]{2,1,0:T(8,128)(2,1)S(1)}, bf16[2,128,512]{2,1,0:T(8,128)(2,1)S(1)}, u32[]{:S(2)}, u32[]{:S(2)}) collective-permute-start(bf16[2,128,512]{2,1,0:T(8,128)(2,1)S(1)} %pad_maximum_fusion.1), channel_id=1, source_target_pairs={{0,64},{16,80},{32,96},{48,112},{64,0},{80,16},{96,32},{112,48},{1... | collective-permute-start | bytes 786440 | tf_op jit(solution)/shard_map/gather_in/ppermute | solution.py:207
  19.1 12.9 %collective-permute-start.4 = (bf16[2,128,512]{2,1,0:T(8,128)(2,1)S(1)}, bf16[2,128,512]{2,1,0:T(8,128)(2,1)S(1)}, u32[]{:S(2)}, u32[]{:S(2)}) collective-permute-start(bf16[2,128,512]{2,1,0:T(8,128)(2,1)S(1)} %pad_maximum_fusion.1), channel_id=1, source_target_pairs={{0,32},{16,48},{32,64},{48,80},{64,96},{80,112},{96,0},{112,16},{1... | collective-permute-start | bytes 786440 | tf_op jit(solution)/shard_map/gather_in/ppermute | solution.py:207
  20.0 7.2 %collective-permute-start.10 = (bf16[2,128,512]{2,1,0:T(8,128)(2,1)S(1)}, bf16[2,128,512]{2,1,0:T(8,128)(2,1)S(1)}, u32[]{:S(2)}, u32[]{:S(2)}) collective-permute-start(bf16[2,128,512]{2,1,0:T(8,128)(2,1)S(1)} %pad_maximum_fusion), channel_id=1, source_target_pairs={{0,12},{1,13},{2,14},{3,15},{4,0},{5,1},{6,2},{7,3},{8,4},{9,5},{1... | collective-permute-start | bytes 786440 | tf_op jit(solution)/shard_map/gather_in/ppermute | solution.py:208
  20.9 8.9 %collective-permute-start.5 = (bf16[2,128,512]{2,1,0:T(8,128)(2,1)S(1)}, bf16[2,128,512]{2,1,0:T(8,128)(2,1)S(1)}, u32[]{:S(2)}, u32[]{:S(2)}) collective-permute-start(bf16[2,128,512]{2,1,0:T(8,128)(2,1)S(1)} %pad_maximum_fusion), channel_id=1, source_target_pairs={{0,4},{1,5},{2,6},{3,7},{4,8},{5,9},{6,10},{7,11},{8,12},{9,13},{1... | collective-permute-start | bytes 786440 | tf_op jit(solution)/shard_map/gather_in/ppermute | solution.py:208
  27.3 4.8 %collective-permute-start.7 = (bf16[2,128,512]{2,1,0:T(8,128)(2,1)S(1)}, bf16[2,128,512]{2,1,0:T(8,128)(2,1)S(1)}, u32[]{:S(2)}, u32[]{:S(2)}) collective-permute-start(bf16[2,128,512]{2,1,0:T(8,128)(2,1)S(1)} %pad_maximum_fusion), channel_id=1, source_target_pairs={{0,1},{1,0},{2,3},{3,2},{4,5},{5,4},{6,7},{7,6},{8,9},{9,8},{10,11... | collective-permute-start | bytes 786440 | tf_op jit(solution)/shard_map/gather_in/ppermute | solution.py:52
  29.8 2.3 %collective-permute-start.9 = (bf16[2,128,512]{2,1,0:T(8,128)(2,1)S(1)}, bf16[2,128,512]{2,1,0:T(8,128)(2,1)S(1)}, u32[]{:S(2)}, u32[]{:S(2)}) collective-permute-start(bf16[2,128,512]{2,1,0:T(8,128)(2,1)S(1)} %collective-permute-done.8), channel_id=1, source_target_pairs={{0,1},{1,0},{2,3},{3,2},{4,5},{5,4},{6,7},{7,6},{8,9},{9,8},{10,11... | collective-permute-start | bytes 786440 | tf_op jit(solution)/shard_map/gather_in/ppermute | solution.py:52
  29.8 3.2 %collective-permute-start.11 = (bf16[2,128,512]{2,1,0:T(8,128)(2,1)S(1)}, bf16[2,128,512]{2,1,0:T(8,128)(2,1)S(1)}, u32[]{:S(2)}, u32[]{:S(2)}) collective-permute-start(bf16[2,128,512]{2,1,0:T(8,128)(2,1)S(1)} %collective-permute-done.10), channel_id=1, source_target_pairs={{0,1},{1,0},{2,3},{3,2},{4,5},{5,4},{6,7},{7,6},{8,9},{9,8},{10,11... | collective-permute-start | bytes 786440 | tf_op jit(solution)/shard_map/gather_in/ppermute | solution.py:52
  30.5 4.6 %collective-permute-start.6 = (bf16[2,128,512]{2,1,0:T(8,128)(2,1)S(1)}, bf16[2,128,512]{2,1,0:T(8,128)(2,1)S(1)}, u32[]{:S(2)}, u32[]{:S(2)}) collective-permute-start(bf16[2,128,512]{2,1,0:T(8,128)(2,1)S(1)} %collective-permute-done.5), channel_id=1, source_target_pairs={{0,1},{1,0},{2,3},{3,2},{4,5},{5,4},{6,7},{7,6},{8,9},{9,8},{10,11... | collective-permute-start | bytes 786440 | tf_op jit(solution)/shard_map/gather_in/ppermute | solution.py:52
  33.0 2.1 %collective-permute-start.14 = (f32[1,136,512]{2,1,0:T(8,128)S(1)}, f32[1,136,512]{2,1,0:T(8,128)S(1)}, u32[]{:S(2)}, u32[]{:S(2)}) collective-permute-start(f32[1,136,512]{2,1,0:T(8,128)S(1)} %get-tuple-element.31), channel_id=1, source_target_pairs={{0,1},{1,0},{2,3},{3,2},{4,5},{5,4},{6,7},{7,6},{8,9},{9,8},{10,11... | collective-permute-start | bytes 835592 | tf_op jit(solution)/shard_map/reduce_rows/ppermute | solution.py:52
  34.4 2.2 %collective-permute-start.12 = (f32[2,136,512]{2,1,0:T(8,128)S(1)}, f32[2,136,512]{2,1,0:T(8,128)S(1)}, u32[]{:S(2)}, u32[]{:S(2)}) collective-permute-start(f32[2,136,512]{2,1,0:T(8,128)S(1)} %get-tuple-element.28), channel_id=1, source_target_pairs={{0,1},{1,0},{2,3},{3,2},{4,5},{5,4},{6,7},{7,6},{8,9},{9,8},{10,11... | collective-permute-start | bytes 1671176 | tf_op jit(solution)/shard_map/reduce_rows/ppermute | solution.py:52
  35.1 13.1 %collective-permute-start.15 = (f16[136,512]{1,0:T(8,128)(2,1)S(1)}, f16[136,512]{1,0:T(8,128)(2,1)S(1)}, u32[]{:S(2)}, u32[]{:S(2)}) collective-permute-start(f16[136,512]{1,0:T(8,128)(2,1)S(1)} %fusion.19), channel_id=1, source_target_pairs={{0,10},{1,11},{2,8},{3,9},{4,14},{5,15},{6,12},{7,13},{8,2},{9,3},... | collective-permute-start | bytes 417800 | tf_op jit(solution)/shard_map/reduce_rows/ppermute | solution.py:227
  36.6 8.3 %collective-permute-start.18 = (f32[2,136,512]{2,1,0:T(8,128)S(1)}, f32[2,136,512]{2,1,0:T(8,128)S(1)}, u32[]{:S(2)}, u32[]{:S(2)}) collective-permute-start(f32[2,136,512]{2,1,0:T(8,128)S(1)} %get-tuple-element.34), channel_id=1, source_target_pairs={{0,1},{1,0},{2,3},{3,2},{4,5},{5,4},{6,7},{7,6},{8,9},{9,8},{10,11... | collective-permute-start | bytes 1671176 | tf_op jit(solution)/shard_map/reduce_rows/ppermute | solution.py:52
  38.6 6.5 %collective-permute-start.13 = (f32[3,136,512]{2,1,0:T(8,128)S(1)}, f32[3,136,512]{2,1,0:T(8,128)S(1)}, u32[]{:S(2)}, u32[]{:S(2)}) collective-permute-start(f32[3,136,512]{2,1,0:T(8,128)S(1)} %get-tuple-element.30), channel_id=1, source_target_pairs={{0,1},{1,0},{2,3},{3,2},{4,5},{5,4},{6,7},{7,6},{8,9},{9,8},{10,11... | collective-permute-start | bytes 2506760 | tf_op jit(solution)/shard_map/reduce_rows/ppermute | solution.py:52
  39.3 10.3 %collective-permute-start.16 = (f16[136,512]{1,0:T(8,128)(2,1)S(1)}, f16[136,512]{1,0:T(8,128)(2,1)S(1)}, u32[]{:S(2)}, u32[]{:S(2)}) collective-permute-start(f16[136,512]{1,0:T(8,128)(2,1)S(1)} %get-tuple-element.57), channel_id=1, source_target_pairs={{0,8},{1,9},{2,10},{3,11},{4,12},{5,13},{6,14},{7,15},{8,0},{9,1},... | collective-permute-start | bytes 417800 | tf_op jit(solution)/shard_map/reduce_rows/ppermute | solution.py:227
  42.5 9.2 %collective-permute-start.17 = (f16[136,512]{1,0:T(8,128)(2,1)S(1)}, f16[136,512]{1,0:T(8,128)(2,1)S(1)}, u32[]{:S(2)}, u32[]{:S(2)}) collective-permute-start(f16[136,512]{1,0:T(8,128)(2,1)S(1)} %get-tuple-element.58), channel_id=1, source_target_pairs={{0,6},{1,7},{2,4},{3,5},{4,10},{5,11},{6,8},{7,9},{8,14},{9,15},{1... | collective-permute-start | bytes 417800 | tf_op jit(solution)/shard_map/reduce_rows/ppermute | solution.py:227
  45.0 7.9 %collective-permute-start.19 = (f16[136,512]{1,0:T(8,128)(2,1)S(1)}, f16[136,512]{1,0:T(8,128)(2,1)S(1)}, u32[]{:S(2)}, u32[]{:S(2)}) collective-permute-start(f16[136,512]{1,0:T(8,128)(2,1)S(1)} %get-tuple-element.59), channel_id=1, source_target_pairs={{0,4},{1,5},{2,6},{3,7},{4,8},{5,9},{6,10},{7,11},{8,12},{9,13},{1... | collective-permute-start | bytes 417800 | tf_op jit(solution)/shard_map/reduce_rows/ppermute | solution.py:227
  45.1 8.1 %collective-permute-start.20 = (f16[136,512]{1,0:T(8,128)(2,1)S(1)}, f16[136,512]{1,0:T(8,128)(2,1)S(1)}, u32[]{:S(2)}, u32[]{:S(2)}) collective-permute-start(f16[136,512]{1,0:T(8,128)(2,1)S(1)} %get-tuple-element.60), channel_id=1, source_target_pairs={{0,14},{1,15},{2,12},{3,13},{4,2},{5,3},{6,0},{7,1},{8,6},{9,7},{1... | collective-permute-start | bytes 417800 | tf_op jit(solution)/shard_map/reduce_rows/ppermute | solution.py:227
  48.2 6.8 %collective-permute-start.21 = (f16[136,512]{1,0:T(8,128)(2,1)S(1)}, f16[136,512]{1,0:T(8,128)(2,1)S(1)}, u32[]{:S(2)}, u32[]{:S(2)}) collective-permute-start(f16[136,512]{1,0:T(8,128)(2,1)S(1)} %get-tuple-element.55), channel_id=1, source_target_pairs={{0,12},{1,13},{2,14},{3,15},{4,0},{5,1},{6,2},{7,3},{8,4},{9,5},{1... | collective-permute-start | bytes 417800 | tf_op jit(solution)/shard_map/reduce_rows/ppermute | solution.py:227
  49.6 5.9 %collective-permute-start.22 = (f16[136,512]{1,0:T(8,128)(2,1)S(1)}, f16[136,512]{1,0:T(8,128)(2,1)S(1)}, u32[]{:S(2)}, u32[]{:S(2)}) collective-permute-start(f16[136,512]{1,0:T(8,128)(2,1)S(1)} %get-tuple-element.56), channel_id=1, source_target_pairs={{0,2},{1,3},{2,0},{3,1},{4,6},{5,7},{6,4},{7,5},{8,10},{9,11},{10,... | collective-permute-start | bytes 417800 | tf_op jit(solution)/shard_map/reduce_rows/ppermute | solution.py:227
  55.8 16.4 %copy-start = (bf16[128,512]{1,0:T(8,128)(2,1)}, bf16[128,512]{1,0:T(8,128)(2,1)S(1)}, u32[]{:S(2)}) copy-start(bf16[128,512]{1,0:T(8,128)(2,1)S(1)} %fusion.17.a0) | copy-start | bytes 393220
  55.8 7.2 %collective-permute-start.29 = (bf16[128,512]{1,0:T(8,128)(2,1)S(1)}, bf16[128,512]{1,0:T(8,128)(2,1)S(1)}, u32[]{:S(2)}, u32[]{:S(2)}) collective-permute-start(bf16[128,512]{1,0:T(8,128)(2,1)S(1)} %fusion.17.a0), channel_id=1, source_target_pairs={{0,2},{1,3},{2,0},{3,1},{4,6},{5,7},{6,4},{7,5},{8,10},{9,11},{10,... | collective-permute-start | bytes 393224 | tf_op jit(solution)/shard_map/gather_new/ppermute | solution.py:238
  57.2 5.9 %collective-permute-start.30 = (bf16[128,512]{1,0:T(8,128)(2,1)S(1)}, bf16[128,512]{1,0:T(8,128)(2,1)S(1)}, u32[]{:S(2)}, u32[]{:S(2)}) collective-permute-start(bf16[128,512]{1,0:T(8,128)(2,1)S(1)} %fusion.17.a0), channel_id=1, source_target_pairs={{0,1},{1,0},{2,3},{3,2},{4,5},{5,4},{6,7},{7,6},{8,9},{9,8},{10,11... | collective-permute-start | bytes 393224 | tf_op jit(solution)/shard_map/gather_new/ppermute | solution.py:52
  57.2 8.7 %collective-permute-start.25 = (bf16[128,512]{1,0:T(8,128)(2,1)S(1)}, bf16[128,512]{1,0:T(8,128)(2,1)S(1)}, u32[]{:S(2)}, u32[]{:S(2)}) collective-permute-start(bf16[128,512]{1,0:T(8,128)(2,1)S(1)} %fusion.17.a0), channel_id=1, source_target_pairs={{0,12},{1,13},{2,14},{3,15},{4,0},{5,1},{6,2},{7,3},{8,4},{9,5},{1... | collective-permute-start | bytes 393224 | tf_op jit(solution)/shard_map/gather_new/ppermute | solution.py:238
  59.2 6.8 %collective-permute-start.26 = (bf16[128,512]{1,0:T(8,128)(2,1)S(1)}, bf16[128,512]{1,0:T(8,128)(2,1)S(1)}, u32[]{:S(2)}, u32[]{:S(2)}) collective-permute-start(bf16[128,512]{1,0:T(8,128)(2,1)S(1)} %fusion.17.a0), channel_id=1, source_target_pairs={{0,4},{1,5},{2,6},{3,7},{4,8},{5,9},{6,10},{7,11},{8,12},{9,13},{1... | collective-permute-start | bytes 393224 | tf_op jit(solution)/shard_map/gather_new/ppermute | solution.py:238
  59.2 7.7 %collective-permute-start.34 = (bf16[128,512]{1,0:T(8,128)(2,1)S(1)}, bf16[128,512]{1,0:T(8,128)(2,1)S(1)}, u32[]{:S(2)}, u32[]{:S(2)}) collective-permute-start(bf16[128,512]{1,0:T(8,128)(2,1)S(1)} %fusion.17.a0), channel_id=1, source_target_pairs={{0,14},{1,15},{2,12},{3,13},{4,2},{5,3},{6,0},{7,1},{8,6},{9,7},{1... | collective-permute-start | bytes 393224 | tf_op jit(solution)/shard_map/gather_new/ppermute | solution.py:238
  63.0 6.9 %collective-permute-start.31 = (bf16[128,512]{1,0:T(8,128)(2,1)S(1)}, bf16[128,512]{1,0:T(8,128)(2,1)S(1)}, u32[]{:S(2)}, u32[]{:S(2)}) collective-permute-start(bf16[128,512]{1,0:T(8,128)(2,1)S(1)} %collective-permute-done.29.a1), channel_id=1, source_target_pairs={{0,1},{1,0},{2,3},{3,2},{4,5},{5,4},{6,7},{7,6},{8,9},{9,8},{10,11... | collective-permute-start | bytes 393224 | tf_op jit(solution)/shard_map/gather_new/ppermute | solution.py:52
  63.0 9.2 %collective-permute-start.35 = (bf16[128,512]{1,0:T(8,128)(2,1)S(1)}, bf16[128,512]{1,0:T(8,128)(2,1)S(1)}, u32[]{:S(2)}, u32[]{:S(2)}) collective-permute-start(bf16[128,512]{1,0:T(8,128)(2,1)S(1)} %fusion.17.a0), channel_id=1, source_target_pairs={{0,6},{1,7},{2,4},{3,5},{4,10},{5,11},{6,8},{7,9},{8,14},{9,15},{1... | collective-permute-start | bytes 393224 | tf_op jit(solution)/shard_map/gather_new/ppermute | solution.py:238
  65.9 6.4 %collective-permute-start.27 = (bf16[128,512]{1,0:T(8,128)(2,1)S(1)}, bf16[128,512]{1,0:T(8,128)(2,1)S(1)}, u32[]{:S(2)}, u32[]{:S(2)}) collective-permute-start(bf16[128,512]{1,0:T(8,128)(2,1)S(1)} %collective-permute-done.25.a0), channel_id=1, source_target_pairs={{0,1},{1,0},{2,3},{3,2},{4,5},{5,4},{6,7},{7,6},{8,9},{9,8},{10,11... | collective-permute-start | bytes 393224 | tf_op jit(solution)/shard_map/gather_new/ppermute | solution.py:52
  66.1 6.8 %collective-permute-start.28 = (bf16[128,512]{1,0:T(8,128)(2,1)S(1)}, bf16[128,512]{1,0:T(8,128)(2,1)S(1)}, u32[]{:S(2)}, u32[]{:S(2)}) collective-permute-start(bf16[128,512]{1,0:T(8,128)(2,1)S(1)} %collective-permute-done.26.a1), channel_id=1, source_target_pairs={{0,1},{1,0},{2,3},{3,2},{4,5},{5,4},{6,7},{7,6},{8,9},{9,8},{10,11... | collective-permute-start | bytes 393224 | tf_op jit(solution)/shard_map/gather_new/ppermute | solution.py:52
  66.9 7.5 %collective-permute-start.24 = (bf16[128,512]{1,0:T(8,128)(2,1)S(1)}, bf16[128,512]{1,0:T(8,128)(2,1)S(1)}, u32[]{:S(2)}, u32[]{:S(2)}) collective-permute-start(bf16[128,512]{1,0:T(8,128)(2,1)S(1)} %fusion.17.a0), channel_id=1, source_target_pairs={{0,10},{1,11},{2,8},{3,9},{4,14},{5,15},{6,12},{7,13},{8,2},{9,3},... | collective-permute-start | bytes 393224 | tf_op jit(solution)/shard_map/gather_new/ppermute | solution.py:238
  69.9 7.2 %collective-permute-start.23 = (bf16[128,512]{1,0:T(8,128)(2,1)S(1)}, bf16[128,512]{1,0:T(8,128)(2,1)S(1)}, u32[]{:S(2)}, u32[]{:S(2)}) collective-permute-start(bf16[128,512]{1,0:T(8,128)(2,1)S(1)} %fusion.17.a0), channel_id=1, source_target_pairs={{0,8},{1,9},{2,10},{3,11},{4,12},{5,13},{6,14},{7,15},{8,0},{9,1},... | collective-permute-start | bytes 393224 | tf_op jit(solution)/shard_map/gather_new/ppermute | solution.py:238
  72.2 5.5 %collective-permute-start.36 = (bf16[128,512]{1,0:T(8,128)(2,1)S(1)}, bf16[128,512]{1,0:T(8,128)(2,1)S(1)}, u32[]{:S(2)}, u32[]{:S(2)}) collective-permute-start(bf16[128,512]{1,0:T(8,128)(2,1)S(1)} %collective-permute-done.34.a0), channel_id=1, source_target_pairs={{0,1},{1,0},{2,3},{3,2},{4,5},{5,4},{6,7},{7,6},{8,9},{9,8},{10,11... | collective-permute-start | bytes 393224 | tf_op jit(solution)/shard_map/gather_new/ppermute | solution.py:52
  72.3 5.4 %collective-permute-start.37 = (bf16[128,512]{1,0:T(8,128)(2,1)S(1)}, bf16[128,512]{1,0:T(8,128)(2,1)S(1)}, u32[]{:S(2)}, u32[]{:S(2)}) collective-permute-start(bf16[128,512]{1,0:T(8,128)(2,1)S(1)} %collective-permute-done.35.a1), channel_id=1, source_target_pairs={{0,1},{1,0},{2,3},{3,2},{4,5},{5,4},{6,7},{7,6},{8,9},{9,8},{10,11... | collective-permute-start | bytes 393224 | tf_op jit(solution)/shard_map/gather_new/ppermute | solution.py:52
  77.2 2.0 %collective-permute-start.33 = (bf16[128,512]{1,0:T(8,128)(2,1)S(1)}, bf16[128,512]{1,0:T(8,128)(2,1)S(1)}, u32[]{:S(2)}, u32[]{:S(2)}) collective-permute-start(bf16[128,512]{1,0:T(8,128)(2,1)S(1)} %collective-permute-done.24.a1), channel_id=1, source_target_pairs={{0,1},{1,0},{2,3},{3,2},{4,5},{5,4},{6,7},{7,6},{8,9},{9,8},{10,11... | collective-permute-start | bytes 393224 | tf_op jit(solution)/shard_map/gather_new/ppermute | solution.py:52
  77.2 2.0 %collective-permute-start.32 = (bf16[128,512]{1,0:T(8,128)(2,1)S(1)}, bf16[128,512]{1,0:T(8,128)(2,1)S(1)}, u32[]{:S(2)}, u32[]{:S(2)}) collective-permute-start(bf16[128,512]{1,0:T(8,128)(2,1)S(1)} %collective-permute-done.23.a0), channel_id=1, source_target_pairs={{0,1},{1,0},{2,3},{3,2},{4,5},{5,4},{6,7},{7,6},{8,9},{9,8},{10,11... | collective-permute-start | bytes 393224 | tf_op jit(solution)/shard_map/gather_new/ppermute | solution.py:52
  81.0 8.6 %collective-permute-start.38 = (f16[136,512]{1,0:T(8,128)(2,1)S(1)}, f16[136,512]{1,0:T(8,128)(2,1)S(1)}, u32[]{:S(2)}, u32[]{:S(2)}) collective-permute-start(f16[136,512]{1,0:T(8,128)(2,1)S(1)} %get-tuple-element.48), channel_id=1, source_target_pairs={{0,16},{16,0},{32,48},{48,32},{64,80},{80,64},{96,112},{112,96},{1... | collective-permute-start | bytes 417800 | tf_op jit(solution)/shard_map/reduce_columns/ppermute | solution.py:264
  82.3 12.3 %collective-permute-start.39 = (f16[136,512]{1,0:T(8,128)(2,1)S(1)}, f16[136,512]{1,0:T(8,128)(2,1)S(1)}, u32[]{:S(2)}, u32[]{:S(2)}) collective-permute-start(f16[136,512]{1,0:T(8,128)(2,1)S(1)} %get-tuple-element.54), channel_id=1, source_target_pairs={{0,32},{16,48},{32,64},{48,80},{64,96},{80,112},{96,0},{112,16},{1... | collective-permute-start | bytes 417800 | tf_op jit(solution)/shard_map/reduce_columns/ppermute | solution.py:264
  82.4 12.9 %collective-permute-start.40 = (f16[136,512]{1,0:T(8,128)(2,1)S(1)}, f16[136,512]{1,0:T(8,128)(2,1)S(1)}, u32[]{:S(2)}, u32[]{:S(2)}) collective-permute-start(f16[136,512]{1,0:T(8,128)(2,1)S(1)} %get-tuple-element.53), channel_id=1, source_target_pairs={{0,96},{16,112},{32,0},{48,16},{64,32},{80,48},{96,64},{112,80},{1... | collective-permute-start | bytes 417800 | tf_op jit(solution)/shard_map/reduce_columns/ppermute | solution.py:264
  85.6 11.5 %collective-permute-start.41 = (f16[136,512]{1,0:T(8,128)(2,1)S(1)}, f16[136,512]{1,0:T(8,128)(2,1)S(1)}, u32[]{:S(2)}, u32[]{:S(2)}) collective-permute-start(f16[136,512]{1,0:T(8,128)(2,1)S(1)} %get-tuple-element.52), channel_id=1, source_target_pairs={{0,80},{16,64},{32,112},{48,96},{64,16},{80,0},{96,48},{112,32},{1... | collective-permute-start | bytes 417800 | tf_op jit(solution)/shard_map/reduce_columns/ppermute | solution.py:264
  88.9 12.8 %collective-permute-start.42 = (f16[136,512]{1,0:T(8,128)(2,1)S(1)}, f16[136,512]{1,0:T(8,128)(2,1)S(1)}, u32[]{:S(2)}, u32[]{:S(2)}) collective-permute-start(f16[136,512]{1,0:T(8,128)(2,1)S(1)} %get-tuple-element.51), channel_id=1, source_target_pairs={{0,48},{16,32},{32,80},{48,64},{64,112},{80,96},{96,16},{112,0},{1... | collective-permute-start | bytes 417800 | tf_op jit(solution)/shard_map/reduce_columns/ppermute | solution.py:264
  89.7 12.1 %collective-permute-start.43 = (f16[136,512]{1,0:T(8,128)(2,1)S(1)}, f16[136,512]{1,0:T(8,128)(2,1)S(1)}, u32[]{:S(2)}, u32[]{:S(2)}) collective-permute-start(f16[136,512]{1,0:T(8,128)(2,1)S(1)} %get-tuple-element.50), channel_id=1, source_target_pairs={{0,112},{16,96},{32,16},{48,0},{64,48},{80,32},{96,80},{112,64},{1... | collective-permute-start | bytes 417800 | tf_op jit(solution)/shard_map/reduce_columns/ppermute | solution.py:264
  94.6 7.2 %collective-permute-start.44 = (f16[136,512]{1,0:T(8,128)(2,1)S(1)}, f16[136,512]{1,0:T(8,128)(2,1)S(1)}, u32[]{:S(2)}, u32[]{:S(2)}) collective-permute-start(f16[136,512]{1,0:T(8,128)(2,1)S(1)} %get-tuple-element.49), channel_id=1, source_target_pairs={{0,64},{16,80},{32,96},{48,112},{64,0},{80,16},{96,32},{112,48},{1... | collective-permute-start | bytes 417800 | tf_op jit(solution)/shard_map/reduce_columns/ppermute | solution.py:264
  (1 other events, 0.7 us)
